TPU v7x, 32 devices: a whole 2x2x4 slice. The times are simulated.
32 devices in a mesh: grp: 2 (over y), seq: 4 (over z), sub: 2 (over x), hd: 2 (over core).
Axes of the slice: x: 2, y: 2, z: 4, core: 2. Of those that a mesh axis runs over, the one named last changes fastest.
Arguments:
- queries: bfloat16 [8192, 768], P(('grp', 'seq', 'sub'), 'hd'), parts along dimension 0, may hold values from -200 to 200
- keys: bfloat16 [8192, 768], P(('grp', 'seq', 'sub'), 'hd'), parts along dimension 0, may hold values from -10 to 10
- values: bfloat16 [8192, 768], P(('grp', 'seq', 'sub'), 'hd'), parts along dimension 0, may hold values from -6 to 6
- grad_out: bfloat16 [8192, 768], P(('grp', 'seq', 'sub'), 'hd'), parts along dimension 0, may hold values from -6 to 6
- center_head_shift: int32 [16], replicated, may hold values from 0 to 7
- wide_head_shift: int32 [16], replicated, may hold values from 0 to 127
- valid_count: int32 [2], P('grp'), parts along dimension 0, may hold values from 2048 to 4096
Outputs:
- attended: bfloat16 [8192, 768], P(('grp', 'seq', 'sub'), 'hd'), parts along dimension 0
- grad_queries: bfloat16 [8192, 768], P(('grp', 'seq', 'sub'), 'hd'), parts along dimension 0
- key_gradient: bfloat16 [8192, 768], P(('grp', 'seq', 'sub'), 'hd'), parts along dimension 0
- value_gradient: bfloat16 [8192, 768], P(('grp', 'seq', 'sub'), 'hd'), parts along dimension 0
There are 2 independent parts, one for each index of `grp`. A program takes and returns all parts, laid end to end along the dimension named above; an argument that names none is the same for every part. Nothing has to cross between parts.
All inputs are finite; a program needn't handle non-finite values.
Results may differ from a plain program's by a relative error of at most 0.0095.
Values may be sent and summed in bfloat16 or wider, within the bound.
No kernel may reach another device: no remote copies, remote signals or barrier semaphores. Data moves between devices by JAX's collectives and lax.ppermute only.
A program may use at most 64 MiB of HBM per device.

v0:
```python
import jax
import jax.numpy as jnp
from jax import lax
from jax.sharding import PartitionSpec as P

HEAD_WIDTH = 48
CENTER_DILATION = 8
WIDE_DILATION = 128


def from_partner(value, axis, apart):
    mask = 2**apart
    pairs = [(source, source ^ mask) for source in range(lax.axis_size(axis))]
    return lax.ppermute(value, axis, pairs)


def head_pass(queries_h, key_rows, value_rows, live_mask, grad_rows):
    scaling = HEAD_WIDTH ** (-0.5)
    scores = scaling * jnp.dot(queries_h, key_rows.T, preferred_element_type=jnp.float32)
    scores = jnp.where(live_mask[None, :], scores, -1e30)
    row_max = jnp.max(scores, axis=1, keepdims=True)
    lifted = jnp.where(live_mask[None, :], jnp.exp(scores - row_max), 0.0)
    attn_prob = lifted / jnp.sum(lifted, axis=1, keepdims=True)
    weights = attn_prob.astype(jnp.bfloat16)
    context = jnp.dot(weights, value_rows, preferred_element_type=jnp.float32)
    delta_row = jnp.sum(grad_rows.astype(jnp.float32) * context, axis=1, keepdims=True)
    grad_prob = jnp.dot(grad_rows, value_rows.T, preferred_element_type=jnp.float32)
    dscore = (scaling * attn_prob * (grad_prob - delta_row)).astype(jnp.bfloat16)
    grad_query = jnp.dot(dscore, key_rows, preferred_element_type=jnp.float32).astype(jnp.bfloat16)
    grad_key = jnp.dot(dscore.T, queries_h, preferred_element_type=jnp.float32)
    grad_value = jnp.dot(weights.T, grad_rows, preferred_element_type=jnp.float32)
    return (context.astype(jnp.bfloat16), grad_query, grad_key, grad_value)


def local(queries, keys, values, grad_out, center_head_shift, wide_head_shift, valid_count):
    tok_rows, width = queries.shape
    head_local = width // HEAD_WIDTH
    head_base = lax.axis_index("hd") * head_local
    center_present = lax.dynamic_slice_in_dim(center_head_shift, head_base, head_local)
    wide_present = lax.dynamic_slice_in_dim(wide_head_shift, head_base, head_local)

    def select_nearby(source, step, offsets):
        shaped = source.reshape(tok_rows // step, step, head_local, HEAD_WIDTH)
        picker = jnp.arange(step)[:, None] == offsets[None, :]
        picked = jnp.sum(
            jnp.where(picker[None, :, :, None], shaped, jnp.zeros((), source.dtype)), axis=1
        )
        return picked.reshape(tok_rows // step, width)

    def distribute_nearby(rows, step, offsets):
        picker = jnp.arange(step)[:, None] == offsets[None, :]
        shaped = rows.reshape(rows.shape[0], head_local, HEAD_WIDTH)
        spread = jnp.where(
            picker[None, :, :, None], shaped[:, None, :, :], jnp.zeros((), rows.dtype)
        )
        return spread.reshape(tok_rows, width)

    def to_heads(rows):
        return rows.reshape(rows.shape[0], head_local, HEAD_WIDTH).transpose(1, 0, 2)

    def from_heads(stack):
        return stack.transpose(1, 0, 2).reshape(stack.shape[1], width)

    center_key_spots = select_nearby(keys, CENTER_DILATION, center_present)
    center_value_spots = select_nearby(values, CENTER_DILATION, center_present)
    wide_key_spots = select_nearby(keys, WIDE_DILATION, wide_present)
    wide_value_spots = select_nearby(values, WIDE_DILATION, wide_present)
    partner_k, partner_v = from_partner((center_key_spots, center_value_spots), "sub", 0)
    lower_half = lax.axis_index("sub") % 2 == 0
    mid_k = jnp.where(
        lower_half,
        jnp.concatenate([center_key_spots, partner_k], axis=0),
        jnp.concatenate([partner_k, center_key_spots], axis=0),
    )
    mid_v = jnp.where(
        lower_half,
        jnp.concatenate([center_value_spots, partner_v], axis=0),
        jnp.concatenate([partner_v, center_value_spots], axis=0),
    )
    far_k, far_v = (
        lax.all_gather(wide_key_spots, ("seq", "sub"), axis=0, tiled=True),
        lax.all_gather(wide_value_spots, ("seq", "sub"), axis=0, tiled=True),
    )
    device = lax.axis_index(("seq", "sub"))
    valid_len = valid_count[0]
    start = device * tok_rows
    center_first = device // 2 * (2 * tok_rows)
    center_token_count = mid_k.shape[0]
    own_count = center_token_count // 2
    wide_token_count = far_k.shape[0]
    local_live = jnp.broadcast_to(
        (start + jnp.arange(tok_rows))[None, :] < valid_len, (head_local, tok_rows)
    )
    center_places = (
        center_first
        + jnp.arange(center_token_count)[None, :] * CENTER_DILATION
        + center_present[:, None]
    )
    wide_places = jnp.arange(wide_token_count)[None, :] * WIDE_DILATION + wide_present[:, None]
    live_all = jnp.concatenate(
        [local_live, center_places < valid_len, wide_places < valid_len], axis=1
    )
    key_all = jnp.concatenate([to_heads(keys), to_heads(mid_k), to_heads(far_k)], axis=1)
    value_all = jnp.concatenate([to_heads(values), to_heads(mid_v), to_heads(far_v)], axis=1)

    def run_head(packed):
        return head_pass(packed[0], packed[1], packed[2], packed[3], packed[4])

    out_heads, dq_heads, dk_heads, dv_heads = lax.map(
        run_head, (to_heads(queries), key_all, value_all, live_all, to_heads(grad_out))
    )
    attended = from_heads(out_heads)
    grad_queries = from_heads(dq_heads)
    dk_rows = from_heads(dk_heads)
    dv_rows = from_heads(dv_heads)
    upper = tok_rows + center_token_count
    middle = tok_rows + own_count
    first_k, second_k = (dk_rows[tok_rows:middle], dk_rows[middle:upper])
    first_v, second_v = (dv_rows[tok_rows:middle], dv_rows[middle:upper])
    mine_k = jnp.where(lower_half, first_k, second_k)
    mine_v = jnp.where(lower_half, first_v, second_v)
    other_k = jnp.where(lower_half, second_k, first_k)
    other_v = jnp.where(lower_half, second_v, first_v)
    came_k, came_v = from_partner((other_k, other_v), "sub", 0)
    center_key_sum = mine_k + came_k
    center_value_sum = mine_v + came_v
    total_k, total_v = lax.psum((dk_rows[upper:], dv_rows[upper:]), ("seq", "sub"))
    share = wide_token_count // lax.axis_size(("seq", "sub"))
    wide_key_sum = lax.dynamic_slice_in_dim(total_k, device * share, share, 0)
    wide_value_sum = lax.dynamic_slice_in_dim(total_v, device * share, share, 0)
    key_gradient = (
        dk_rows[:tok_rows]
        + distribute_nearby(center_key_sum, CENTER_DILATION, center_present)
        + distribute_nearby(wide_key_sum, WIDE_DILATION, wide_present)
    )
    value_gradient = (
        dv_rows[:tok_rows]
        + distribute_nearby(center_value_sum, CENTER_DILATION, center_present)
        + distribute_nearby(wide_value_sum, WIDE_DILATION, wide_present)
    )
    return (
        attended,
        grad_queries,
        key_gradient.astype(jnp.bfloat16),
        value_gradient.astype(jnp.bfloat16),
    )


def solution(mesh):
    return jax.shard_map(
        local,
        mesh=mesh,
        in_specs=(
            P(("grp", "seq", "sub"), "hd"),
            P(("grp", "seq", "sub"), "hd"),
            P(("grp", "seq", "sub"), "hd"),
            P(("grp", "seq", "sub"), "hd"),
            P(),
            P(),
            P("grp"),
        ),
        out_specs=(
            P(("grp", "seq", "sub"), "hd"),
            P(("grp", "seq", "sub"), "hd"),
            P(("grp", "seq", "sub"), "hd"),
            P(("grp", "seq", "sub"), "hd"),
        ),
        check_vma=False,
    )
```

profile of v0, /device:TPU:0, one launch (start us, length us, event | category | flops | bytes accessed | tf_op | source)
XLA Modules:
  0.0 235.8 jit_solution(4876844032087377391)
XLA Ops:
  7.2 0.8 dynamic_slice.30
  8.0 2.0 reshape.179
  10.0 0.9 reshape.185
  10.9 0.8 select_reduce_fusion
  11.7 0.8 reshape.180
  12.5 2.9 %collective-permute-start = (bf16[64,384]{1,0:T(8,128)(2,1)}, bf16[64,384]{1,0:T(8,128)(2,1)}, u32[]{:S(2)}, u32[]{:S(2)}) collective-permute-start(bf16[64,384]{1,0:T(8,128)(2,1)} %reshape.180), channel_id=1, source_target_pairs={{0,2},{2,0},{1,3},{3,1},{4,6},{6,4},{5,7},{7,5},{8,10},{10,8},{9,1... | collective-permute-start | bytes 147464 | tf_op jit(solution)/shard_map/ppermute | solution.py:14
  17.8 1.0 select_reduce_fusion.2
  19.3 31.2 %all-gather = bf16[8,4,384]{2,1,0:T(4,128)(2,1)S(1)} all-gather(bf16[1,4,384]{2,1,0:T(4,128)(2,1)S(1)} %copy.114), channel_id=1, replica_groups=mesh['grp'=2,'seq'=4,'sub'=2,'hd'=2] {'seq','sub'}, dimensions={0}, use_global_device_ids=true | all-gather | bytes 27648 | tf_op jit(solution)/shard_map/all_gather | solution.py:81
  50.8 30.5 %all-gather.1 = bf16[8,4,384]{2,1,0:T(4,128)(2,1)S(1)} all-gather(bf16[1,4,384]{2,1,0:T(4,128)(2,1)S(1)} %copy.122), channel_id=1, replica_groups=mesh['grp'=2,'seq'=4,'sub'=2,'hd'=2] {'seq','sub'}, dimensions={0}, use_global_device_ids=true | all-gather | bytes 27648 | tf_op jit(solution)/shard_map/all_gather | solution.py:82
  82.4 1.2 copy.124
  83.6 0.9 copy.144
  84.5 0.8 fusion.38
  85.3 0.9 copy.145
  86.3 0.9 pad_maximum_fusion
  87.3 1.8 pad_maximum_fusion.1
  89.1 51.5 %while.16 = (s32[]{:T(128)}, bf16[8,512,48]{1,2,0:T(8,128)(2,1)}, bf16[8,512,48]{1,2,0:T(8,128)(2,1)}, f32[8,672,48]{1,2,0:T(8,128)S(1)}, f32[8,672,48]{1,2,0:T(...) while((s32[]{:T(128)}, bf16[8,512,48]{1,2,0:T(8,128)(2,1)}, ...), condition=%wide.region_8.9_spmd, body=%wide.region_4.8_spmd.sunk | while | flops 205527552 | bytes 10110709 | solution.py:109
  89.8 1.1 fusion.70
  90.9 1.9 bitcast_dynamic-update-slice_fusion.2
  92.9 1.4 fusion.67
  94.6 0.9 fusion.68
  96.2 1.1 fusion.70
  97.3 1.9 bitcast_dynamic-update-slice_fusion.2
  99.3 1.4 fusion.67
  101.0 0.9 fusion.68
  102.6 1.1 fusion.70
  103.8 1.9 bitcast_dynamic-update-slice_fusion.2
  105.7 1.4 fusion.67
  107.5 0.9 fusion.68
  109.0 1.1 fusion.70
  110.2 1.9 bitcast_dynamic-update-slice_fusion.2
  112.1 1.4 fusion.67
  113.9 0.9 fusion.68
  115.5 1.1 fusion.70
  116.6 1.9 bitcast_dynamic-update-slice_fusion.2
  118.6 1.4 fusion.67
  120.3 0.9 fusion.68
  121.9 1.1 fusion.70
  123.0 1.9 bitcast_dynamic-update-slice_fusion.2
  125.0 1.4 fusion.67
  126.8 0.9 fusion.68
  128.3 1.1 fusion.70
  129.5 1.9 bitcast_dynamic-update-slice_fusion.2
  131.4 1.4 fusion.67
  133.2 0.9 fusion.68
  134.8 1.1 fusion.70
  135.9 1.9 bitcast_dynamic-update-slice_fusion.2
  137.9 1.4 fusion.67
  139.7 0.9 fusion.68
  140.5 1.3 slice_select_fusion
  141.9 1.5 collective-permute-start.2
  144.2 1.0 slice.56
  145.2 1.0 slice.52
  147.9 0.9 copy.138
  148.9 0.9 copy.139
  150.1 2.0 broadcast_select_fusion
  152.2 2.1 select_n.141
  154.3 1.2 copy.135
  155.4 64.9 %all-reduce.3.cloned.1.call-done = (f32[32,384]{1,0:T(8,128)}, f32[32,384]{1,0:T(8,128)}) async-done(((f32[32,384]{1,0:T(8,128)}, f32[32,384]{1,0:T(8,128)}), (f32[32,384]{1,0:T(8,128)}, f32[32,384]{1,0:T(8,128)})) %all-reduce.3.cloned.1.call-update) | async-done | bytes 98320 | tf_op jit(solution)/shard_map/psum | solution.py:127
  221.4 1.0 broadcast_select_fusion.2
  222.5 1.3 fusion.36
  223.8 0.9 copy.141
  224.8 1.5 select_n.132
  226.3 1.5 copy.130
  228.0 0.9 copy.140
  (111 shorter events, 16.4 us)
Async XLA Ops:
  7.2 2.8 %copy-start.4 = (bf16[512,384]{1,0:T(8,128)(2,1)S(1)}, bf16[512,384]{1,0:T(8,128)(2,1)}, u32[]{:S(2)}) copy-start(bf16[512,384]{1,0:T(8,128)(2,1)} %param.11) | copy-start | bytes 1179652
  7.2 213.2 %all-reduce.3.cloned.1.call-start = ((), (), s32[]{:S(2)}) async-start(), calls=%async_computation | async-start | bytes 196608 | tf_op jit(solution)/shard_map/psum | solution.py:127
  10.9 5.3 %copy-start.3 = (bf16[512,384]{1,0:T(8,128)(2,1)S(1)}, bf16[512,384]{1,0:T(8,128)(2,1)}, u32[]{:S(2)}) copy-start(bf16[512,384]{1,0:T(8,128)(2,1)} %param.10) | copy-start | bytes 1179652
  11.7 4.9 %copy-start.8 = (s32[16]{0:T(128)S(1)}, s32[16]{0:T(128)}, u32[]{:S(2)}) copy-start(s32[16]{0:T(128)} %param.14) | copy-start | bytes 196
  12.5 71.1 %collective-permute-start = (bf16[64,384]{1,0:T(8,128)(2,1)}, bf16[64,384]{1,0:T(8,128)(2,1)}, u32[]{:S(2)}, u32[]{:S(2)}) collective-permute-start(bf16[64,384]{1,0:T(8,128)(2,1)} %reshape.180), channel_id=1, source_target_pairs={{0,2},{2,0},{1,3},{3,1},{4,6},{6,4},{5,7},{7,5},{8,10},{10,8},{9,1... | collective-permute-start | bytes 147464 | tf_op jit(solution)/shard_map/ppermute | solution.py:14
  16.2 69.1 %collective-permute-start.1 = (bf16[64,384]{1,0:T(8,128)(2,1)}, bf16[64,384]{1,0:T(8,128)(2,1)}, u32[]{:S(2)}, u32[]{:S(2)}) collective-permute-start(bf16[64,384]{1,0:T(8,128)(2,1)} %reshape.186), channel_id=1, source_target_pairs={{0,2},{2,0},{1,3},{3,1},{4,6},{6,4},{5,7},{7,5},{8,10},{10,8},{9,1... | collective-permute-start | bytes 147464 | tf_op jit(solution)/shard_map/ppermute | solution.py:14
  16.8 65.4 %copy-start.5 = (bf16[512,384]{1,0:T(8,128)(2,1)S(1)}, bf16[512,384]{1,0:T(8,128)(2,1)}, u32[]{:S(2)}) copy-start(bf16[512,384]{1,0:T(8,128)(2,1)} %param.9) | copy-start | bytes 1179652
  140.5 3.7 %copy-start.2 = (f32[8,672,48]{1,2,0:T(8,128)S(1)}, f32[8,672,48]{1,2,0:T(8,128)}, u32[]{:S(2)}) copy-start(f32[8,672,48]{1,2,0:T(8,128)} %get-tuple-element.62) | copy-start | bytes 3096580
  141.9 7.9 %collective-permute-start.2 = (f32[64,384]{1,0:T(8,128)S(1)}, f32[64,384]{1,0:T(8,128)S(1)}, u32[]{:S(2)}, u32[]{:S(2)}) collective-permute-start(f32[64,384]{1,0:T(8,128)S(1)} %copy.128), channel_id=1, source_target_pairs={{0,2},{2,0},{1,3},{3,1},{4,6},{6,4},{5,7},{7,5},{8,10},{10,8},{9,1... | collective-permute-start | bytes 294920 | tf_op jit(solution)/shard_map/ppermute | solution.py:14
  143.6 6.4 %collective-permute-start.3 = (f32[64,384]{1,0:T(8,128)S(1)}, f32[64,384]{1,0:T(8,128)S(1)}, u32[]{:S(2)}, u32[]{:S(2)}) collective-permute-start(f32[64,384]{1,0:T(8,128)S(1)} %copy.133), channel_id=1, source_target_pairs={{0,2},{2,0},{1,3},{3,1},{4,6},{6,4},{5,7},{7,5},{8,10},{10,8},{9,1... | collective-permute-start | bytes 294920 | tf_op jit(solution)/shard_map/ppermute | solution.py:14
  145.2 2.7 %copy-start.6 = (bf16[8,512,48]{1,2,0:T(8,128)(2,1)S(1)}, bf16[8,512,48]{1,2,0:T(8,128)(2,1)}, u32[]{:S(2)}) copy-start(bf16[8,512,48]{1,2,0:T(8,128)(2,1)} %get-tuple-element.59) | copy-start | bytes 1179652
  145.2 3.6 %copy-start.7 = (bf16[8,512,48]{1,2,0:T(8,128)(2,1)S(1)}, bf16[8,512,48]{1,2,0:T(8,128)(2,1)}, u32[]{:S(2)}) copy-start(bf16[8,512,48]{1,2,0:T(8,128)(2,1)} %get-tuple-element.60) | copy-start | bytes 1179652
  221.4 1.1 copy-start.1
  226.3 1.5 copy-start
Sparse Core Ops, SparseCore 0:
  149.9 70.3 all-reduce.2
where the time goes:
time: 237 us; the launch traced here: 236 us
  waiting for transfers between devices  64.9 us (27%)
  blocking collectives  61.7 us (26%)
  matrix products  48.7 us (21%)
  local copies, waits for them, and re-layouts  26 us (11%)
  between operations  15.1 us (6%)
  other arithmetic  14.1 us (6%)
  starting transfers between devices  5.11 us (2%)
    psum x1, waiting for transfers between devices, local(): lax.psum((dk_rows[upper:], dv_rows[upper:]), ('seq', 'sub'))  64.9 us
    all_gather x1, blocking collectives, local(): lax.all_gather(wide_key_spots, ('seq', 'sub'), axis=0, tiled=True)  31.2 us
    all_gather x1, blocking collectives, local(): lax.all_gather(wide_value_spots, ('seq', 'sub'), axis=0, tiled=True)  30.5 us
    dot_general x8, matrix products, head_pass(): context = jnp.dot(weights, value_rows, preferred_element_type=jnp.float32)  15.4 us
    dot_general x8, matrix products, head_pass(): jnp.dot(grad_rows, value_rows.T, preferred_element_type=jnp.float32)  11.4 us
    dot_general x8, matrix products, head_pass(): jnp.dot(weights.T, grad_rows, preferred_element_type=jnp.float32)  9.1 us
    dot_general x8, matrix products, head_pass(): jnp.dot(dscore, key_rows, preferred_element_type=jnp.float32)  6.89 us
    select_n x4, local copies, waits for them, and re-layouts, distribute_nearby(): jnp.where(picker[None, :, :, None], shaped[:, None, :, :], jnp.zeros((),...  6.21 us
  transfers between devices with their start and end apart: 5, of which 1 were waited for; matrix products, arithmetic and copies ran while one was open for 8% of the time, Pallas kernels for 0%

commit v1 on v0

v1 whole, which is shorter than its diff:
```python
import functools
import math

import jax
import jax.numpy as jnp
from jax import lax
from jax.experimental import pallas as pl
from jax.experimental.pallas import tpu as pltpu
from jax.sharding import PartitionSpec as P

HEAD_WIDTH = 48
CENTER_DILATION = 8
WIDE_DILATION = 128
LANES = 128
DEAD = -1e30
SCALE = HEAD_WIDTH**-0.5
EXP2_SCALE = SCALE * math.log2(math.e)
F32 = jnp.float32
BF16 = jnp.bfloat16

VMEM = pl.BlockSpec(memory_space=pltpu.VMEM)
SMEM = pl.BlockSpec(memory_space=pltpu.SMEM)


def nn(a, b):
    return jnp.dot(a, b, preferred_element_type=F32)


def nt(a, b):
    return lax.dot_general(a, b, (((1,), (1,)), ((), ())), preferred_element_type=F32)


def head_rows(h):
    return slice(h * HEAD_WIDTH, (h + 1) * HEAD_WIDTH)


def window(h):
    low = h * HEAD_WIDTH // LANES * LANES
    high = -(-(h + 1) * HEAD_WIDTH // LANES) * LANES
    return low, high


def embed(rows, h):
    low, high = window(h)
    before, after = h * HEAD_WIDTH - low, high - (h + 1) * HEAD_WIDTH
    parts = [rows]
    if before:
        parts.insert(0, jnp.zeros((before, rows.shape[1]), rows.dtype))
    if after:
        parts.append(jnp.zeros((after, rows.shape[1]), rows.dtype))
    return jnp.concatenate(parts, axis=0) if len(parts) > 1 else rows


def add_window(ref, rows, h, value, started):
    low, high = window(h)
    for at in range(low, high, LANES):
        part = value[:, at - low : at - low + LANES]
        if at in started:
            ref[rows, at : at + LANES] += part
        else:
            started.add(at)
            ref[rows, at : at + LANES] = part


def lane_shifts(shift_ref, base, heads, width):
    lane = lax.broadcasted_iota(jnp.int32, (1, width), 1)
    row = jnp.zeros((1, width), jnp.int32)
    for h in range(heads):
        inside = (lane >= h * HEAD_WIDTH) & (lane < (h + 1) * HEAD_WIDTH)
        row = jnp.where(inside, shift_ref[base + h], row)
    return row


def select_kernel(heads, base_ref, center_ref, wide_ref, k_ref, v_ref, near_ref, far_ref, wide_f32):
    rows, width = k_ref.shape
    base = base_ref[0]
    center = lane_shifts(center_ref, base, heads, width)
    wide = lane_shifts(wide_ref, base, heads, width)
    near_rows = rows // CENTER_DILATION
    far_rows = rows // WIDE_DILATION
    row = lax.broadcasted_iota(jnp.int32, (far_rows, WIDE_DILATION, LANES), 1)
    for at, ref in ((0, k_ref), (width, v_ref)):
        for low in range(0, width, LANES):
            lanes = slice(low, low + LANES)
            spread = ref[:, lanes].astype(F32)
            wide_f32[...] = spread
            picked = jnp.zeros((near_rows, LANES), F32)
            for step in range(CENTER_DILATION):
                rows_at = wide_f32[pl.ds(step, near_rows, stride=CENTER_DILATION), :]
                picked = jnp.where(center[:, lanes] == step, rows_at, picked)
            near_ref[:, at + low : at + low + LANES] = picked.astype(BF16)
            chosen = jnp.where(row == wide[:, lanes], spread.reshape(far_rows, WIDE_DILATION, LANES), 0.0)
            far_ref[:, at + low : at + low + LANES] = jnp.sum(chosen, axis=1).astype(BF16)


def forward_kernel(
    heads, live_ref, q_ref, k_ref, v_ref, g_ref,
    p_ref, qt_ref, gt_ref, kt_ref, ot_ref, max_ref, sum_ref, vt_ref,
):
    rows = q_ref.shape[0]
    qt_ref[...] = q_ref[...].T
    gt_ref[...] = g_ref[...].T
    kt_ref[...] = k_ref[...].T
    vt_ref[...] = v_ref[...].T
    live = lax.broadcasted_iota(jnp.int32, (rows, rows), 0) < live_ref[0]
    for h in range(heads):
        low, high = window(h)
        scores = nn(k_ref[:, low:high], embed(qt_ref[head_rows(h), :], h))
        scores = jnp.where(live, scores, DEAD)
        top = jnp.max(scores, axis=0, keepdims=True)
        lifted = jnp.exp2((scores - top) * EXP2_SCALE)
        max_ref[h : h + 1, :] = top
        sum_ref[h : h + 1, :] = jnp.sum(lifted, axis=0, keepdims=True)
        weights = lifted.astype(BF16)
        p_ref[h] = weights
        ot_ref[head_rows(h), :] = nn(vt_ref[head_rows(h), :], weights)


def remote_kernel(
    heads, base_ref, center_ref, wide_ref, valid_ref,
    place_ref, near_ref, came_ref, far_ref, qt_ref, gt_ref, o1_ref, max_ref, sum_ref,
    out_ref, factor_ref, delta_ref, dq_ref, own_ref, send_ref, wides_ref,
    kr_ref, vr_ref, krt_ref, vrt_ref, ot_ref, dk_ref, dv_ref,
):
    width, rows = qt_ref.shape
    near_rows = near_ref.shape[0]
    far_rows = far_ref.shape[0]
    count = 2 * near_rows + far_rows
    base = base_ref[0]
    for at, ref, turned in ((0, kr_ref, krt_ref), (width, vr_ref, vrt_ref)):
        ref[:near_rows, :] = near_ref[:, at : at + width]
        ref[near_rows : 2 * near_rows, :] = came_ref[:, at : at + width]
        ref[2 * near_rows :, :] = far_ref[:, at : at + width]
        turned[...] = ref[...].T
    place = jnp.broadcast_to(place_ref[:, 0:1], (count, rows))
    is_near = lax.broadcasted_iota(jnp.int32, (count, rows), 0) < 2 * near_rows
    began_k, began_v = set(), set()
    everything = slice(0, count)
    for h in range(heads):
        low, high = window(h)
        q_rows = embed(qt_ref[head_rows(h), :], h)
        g_head = gt_ref[head_rows(h), :]
        g_rows = embed(g_head, h)
        scores = nn(kr_ref[:, low:high], q_rows)
        limit = jnp.where(
            is_near, valid_ref[0] - center_ref[base + h], valid_ref[0] - wide_ref[base + h]
        )
        scores = jnp.where(place < limit, scores, DEAD)
        top_here = max_ref[h : h + 1, :]
        top = jnp.maximum(jnp.max(scores, axis=0, keepdims=True), top_here)
        lifted = jnp.exp2((scores - top) * EXP2_SCALE)
        keep = jnp.exp2((top_here - top) * EXP2_SCALE)
        total = sum_ref[h : h + 1, :] * keep + jnp.sum(lifted, axis=0, keepdims=True)
        inverse = 1.0 / total
        prob = lifted * inverse
        factor = keep * inverse
        weights = prob.astype(BF16)
        context = o1_ref[head_rows(h), :] * factor + nn(vrt_ref[head_rows(h), :], weights)
        ot_ref[head_rows(h), :] = context
        delta = jnp.sum(g_head.astype(F32) * context, axis=0, keepdims=True)
        factor_ref[h : h + 1, :] = factor
        delta_ref[h : h + 1, :] = delta
        grad_prob = nn(vr_ref[:, low:high], g_rows)
        dscore = (prob * (grad_prob - delta)).astype(BF16)
        dq_ref[head_rows(h), :] = nn(krt_ref[head_rows(h), :], dscore)
        add_window(dk_ref, everything, h, nt(dscore, q_rows), began_k)
        add_window(dv_ref, everything, h, nt(weights, g_rows), began_v)
    out_ref[...] = ot_ref[...].astype(BF16).T
    for at, ref, by in ((0, dk_ref, SCALE), (width, dv_ref, None)):
        value = ref[...] * by if by is not None else ref[...]
        own_ref[:, at : at + width] = value[:near_rows].astype(own_ref.dtype)
        send_ref[:, at : at + width] = value[near_rows : 2 * near_rows].astype(send_ref.dtype)
        wides_ref[:, at : at + width] = value[2 * near_rows :].astype(wides_ref.dtype)


def backward_kernel(
    heads, p_ref, qt_ref, gt_ref, kt_ref, k_ref, v_ref, factor_ref, delta_ref, dq2_ref,
    dq_ref, dk_ref, dv_ref, dqt_ref,
):
    rows = k_ref.shape[0]
    began_k, began_v = set(), set()
    everything = slice(0, rows)
    for h in range(heads):
        low, high = window(h)
        q_rows = embed(qt_ref[head_rows(h), :], h)
        g_rows = embed(gt_ref[head_rows(h), :], h)
        prob = p_ref[h].astype(F32) * factor_ref[h : h + 1, :]
        grad_prob = nn(v_ref[:, low:high], g_rows)
        dscore = (prob * (grad_prob - delta_ref[h : h + 1, :])).astype(BF16)
        dqt_ref[head_rows(h), :] = dq2_ref[head_rows(h), :] + nn(kt_ref[head_rows(h), :], dscore)
        add_window(dk_ref, everything, h, nt(dscore, q_rows), began_k)
        add_window(dv_ref, everything, h, nt(prob.astype(BF16), g_rows), began_v)
    dq_ref[...] = (dqt_ref[...] * SCALE).astype(BF16).T
    dk_ref[...] = dk_ref[...] * SCALE


def combine_kernel(
    heads, base_ref, center_ref, wide_ref, dk_ref, dv_ref, own_ref, came_ref, far_ref,
    outk_ref, outv_ref, sum_ref,
):
    rows, width = dk_ref.shape
    base = base_ref[0]
    center = lane_shifts(center_ref, base, heads, width)
    wide = lane_shifts(wide_ref, base, heads, width)
    near_rows = own_ref.shape[0]
    far_rows = far_ref.shape[0]
    row = lax.broadcasted_iota(jnp.int32, (WIDE_DILATION, LANES), 0)
    for at, ref, out in ((0, dk_ref, outk_ref), (width, dv_ref, outv_ref)):
        for low in range(0, width, LANES):
            lanes = slice(low, low + LANES)
            packed = slice(at + low, at + low + LANES)
            near = own_ref[:, packed].astype(F32) + came_ref[:, packed].astype(F32)
            for block in range(far_rows):
                part = slice(block * WIDE_DILATION, (block + 1) * WIDE_DILATION)
                far = far_ref[block : block + 1, packed].astype(F32)
                sum_ref[part, :] = ref[part, lanes] + jnp.where(row == wide[:, lanes], far, 0.0)
            for step in range(CENTER_DILATION):
                strided = pl.ds(step, near_rows, stride=CENTER_DILATION)
                sum_ref[strided, :] += jnp.where(center[:, lanes] == step, near, 0.0)
            out[:, lanes] = sum_ref[...].astype(BF16)


def call(body, outs, ins, scratch=(), flops=0, moved=0):
    return pl.pallas_call(
        body,
        out_shape=[jax.ShapeDtypeStruct(s, d) for s, d in outs],
        in_specs=[SMEM if scalar else VMEM for scalar in ins],
        out_specs=[VMEM] * len(outs),
        scratch_shapes=[pltpu.VMEM(s, d) for s, d in scratch],
        compiler_params=pltpu.CompilerParams(vmem_limit_bytes=48 * 2**20),
        cost_estimate=pl.CostEstimate(flops=flops, bytes_accessed=moved, transcendentals=0),
    )


def local(queries, keys, values, grad_out, center_shift, wide_shift, valid_count):
    rows, width = queries.shape
    heads = width // HEAD_WIDTH
    near_rows, far_own = rows // CENTER_DILATION, rows // WIDE_DILATION
    axes = ("seq", "sub")
    devices = lax.axis_size(axes)
    device = lax.axis_index(axes)
    base = (lax.axis_index("hd") * heads).astype(jnp.int32).reshape(1)
    far_rows = far_own * devices
    count = 2 * near_rows + far_rows

    def swap(value, apart):
        return lax.ppermute(value, axes, [(at, at ^ apart) for at in range(devices)])

    near, far = call(
        functools.partial(select_kernel, heads),
        [((near_rows, 2 * width), BF16), ((far_own, 2 * width), BF16)],
        [1, 1, 1, 0, 0],
        [((rows, LANES), F32)],
        moved=4 * rows * width,
    )(base, center_shift, wide_shift, keys, values)

    came = swap(near, 1)
    step = 1
    while step < devices:
        far = jnp.concatenate([far, swap(far, step)], axis=0)
        step *= 2

    live = jnp.clip(valid_count - device * rows, 0, rows).astype(jnp.int32)
    product = 2 * rows * width
    p, qt, gt, kt, o1, top, total = call(
        functools.partial(forward_kernel, heads),
        [
            ((heads, rows, rows), BF16),
            ((width, rows), BF16),
            ((width, rows), BF16),
            ((width, rows), BF16),
            ((width, rows), F32),
            ((heads, rows), F32),
            ((heads, rows), F32),
        ],
        [1, 0, 0, 0, 0],
        [((width, rows), BF16)],
        flops=2 * product * rows * 5,
        moved=heads * rows * rows * 2,
    )(live, queries, keys, values, grad_out)

    own_at = device * rows
    near_at = jnp.arange(near_rows) * CENTER_DILATION
    slots = (jnp.arange(devices) ^ device)[:, None] * rows
    far_at = (slots + jnp.arange(far_own)[None, :] * WIDE_DILATION).reshape(-1)
    place = jnp.concatenate([own_at + near_at, (device ^ 1) * rows + near_at, far_at])
    place = jnp.broadcast_to(place.astype(jnp.int32)[:, None], (count, LANES))
    out, factor, delta, dq2, own, send, far_terms = call(
        functools.partial(remote_kernel, heads),
        [
            ((rows, width), BF16),
            ((heads, rows), F32),
            ((heads, rows), F32),
            ((width, rows), F32),
            ((near_rows, 2 * width), F32),
            ((near_rows, 2 * width), F32),
            ((far_rows, 2 * width), F32),
        ],
        [1, 1, 1, 1] + [0] * 9,
        [
            ((count, width), BF16),
            ((count, width), BF16),
            ((width, count), BF16),
            ((width, count), BF16),
            ((width, rows), F32),
            ((count, width), F32),
            ((count, width), F32),
        ],
        flops=6 * product * count * 5,
        moved=8 * rows * width,
    )(base, center_shift, wide_shift, valid_count, place, near, came, far, qt, gt, o1, top, total)

    back = swap(send, 1)
    step = devices // 2
    while step:
        half = far_own * step
        far_terms = far_terms[:half] + swap(far_terms[half:], step)
        step //= 2

    dq, dk, dv = call(
        functools.partial(backward_kernel, heads),
        [((rows, width), BF16), ((rows, width), F32), ((rows, width), F32)],
        [0] * 9,
        [((width, rows), F32)],
        flops=4 * product * rows * 5,
        moved=heads * rows * rows * 2,
    )(p, qt, gt, kt, keys, values, factor, delta, dq2)

    key_gradient, value_gradient = call(
        functools.partial(combine_kernel, heads),
        [((rows, width), BF16), ((rows, width), BF16)],
        [1, 1, 1, 0, 0, 0, 0, 0],
        [((rows, LANES), F32)],
        moved=12 * rows * width,
    )(base, center_shift, wide_shift, dk, dv, own, back, far_terms)
    return out, dq, key_gradient, value_gradient


def solution(mesh):
    split = P(("grp", "seq", "sub"), "hd")
    return jax.shard_map(
        local,
        mesh=mesh,
        in_specs=(split, split, split, split, P(), P(), P("grp")),
        out_specs=(split, split, split, split),
        check_vma=False,
    )
```

time: 237 us -> 55.5 us (0.23)
  blocking collectives: 61.7 us -> 0 us
  waiting for transfers between devices: 64.9 us -> 5.68 us
  matrix products: 48.7 us -> 0 us
  Pallas kernels: 0 us -> 23.6 us
  local copies, waits for them, and re-layouts: 26 us -> 7.46 us
  other arithmetic: 14.1 us -> 0.22 us
  between operations: 15.1 us -> 1.38 us
  starting transfers between devices: 5.11 us -> 16.7 us
    psum x1 -> x0, waiting for transfers between devices: 64.9 us -> none  [local(): lax.psum((dk_rows[upper:], dv_rows[upper:]), ('seq', 'sub'))]
    all_gather x2 -> x0, blocking collectives: 61.7 us -> none  [the longest x1 31.2 us: local(): lax.all_gather(wide_key_spots, ('seq', 'sub'), axis=0, tiled=True)]
    dot_general x48 -> x0, matrix products: 48.7 us -> none  [the longest x8 15.4 us: head_pass(): context = jnp.dot(weights, value_rows, preferred_element_type=jnp.float32)]
    pallas_call x0 -> x5, Pallas kernels: none -> 23.6 us  [the longest x1 7.81 us: local(): call(functools.partial(backward_kernel, heads), [((rows, width), BF16), (...]
    ppermute x4 -> x8, starting transfers between devices: 5.08 us -> 16.7 us  [swap(): lax.ppermute(value, axes, [(at, at ^ apart) for at in range(devices)])]
    select_n x8 -> x0, local copies, waits for them, and re-layouts: 6.66 us -> none  [the longest x4 6.21 us: distribute_nearby(): jnp.where(picker[None, :, :, None], shaped[:, None, :, :], jnp.zeros((),...]
    ppermute x4 -> x8, waiting for transfers between devices: 0.01 us -> 5.68 us  [swap(): lax.ppermute(value, axes, [(at, at ^ apart) for at in range(devices)])]
    reshape x10 -> x0, local copies, waits for them, and re-layouts: 5.62 us -> none  [the longest x4 3.02 us: select_nearby(): shaped = source.reshape(tok_rows // step, step, head_local, HEAD_WIDTH)]
  transfers between devices with their start and end apart: 5 -> 8, of which waited for: 1 -> 4; matrix products, arithmetic and copies ran while one was open for 8% -> 1% of each run, Pallas kernels for 0% -> 26%
where the time goes in v1:
time: 55.5 us; the launch traced here: 55 us
  Pallas kernels  23.6 us (43%)
  starting transfers between devices  16.7 us (30%)
  local copies, waits for them, and re-layouts  7.46 us (13%)
  waiting for transfers between devices  5.68 us (10%)
  between operations  1.38 us (2%)
    ppermute x8, starting transfers between devices, swap(): lax.ppermute(value, axes, [(at, at ^ apart) for at in range(devices)])  16.7 us
    pallas_call x1, Pallas kernels, local(): call(functools.partial(backward_kernel, heads), [((rows, width), BF16), (...  7.81 us
    unnamed x24, local copies, waits for them, and re-layouts  7.29 us
    pallas_call x1, Pallas kernels, local(): call(functools.partial(forward_kernel, heads), [((heads, rows, rows), BF1...  6.37 us
    pallas_call x1, Pallas kernels, local(): call(functools.partial(remote_kernel, heads), [((rows, width), BF16), ((h...  6.24 us
    ppermute x8, waiting for transfers between devices, swap(): lax.ppermute(value, axes, [(at, at ^ apart) for at in range(devices)])  5.68 us
    pallas_call x1, Pallas kernels, local(): call(functools.partial(combine_kernel, heads), [((rows, width), BF16), ((...  2.12 us
  transfers between devices with their start and end apart: 8, of which 4 were waited for; matrix products, arithmetic and copies ran while one was open for 1% of the time, Pallas kernels for 26%

profile of v1, /device:TPU:0, one launch (start us, length us, event | category | flops | bytes accessed | tf_op | source)
XLA Modules:
  0.0 55.0 jit_solution(15047992212892413218)
XLA Ops:
  0.6 0.0 copy-start
  0.6 1.0 %copy-done = bf16[512,384]{1,0:T(8,128)(2,1)S(1)} copy-done((bf16[512,384]{1,0:T(8,128)(2,1)S(1)}, bf16[512,384]{1,0:T(8,128)(2,1)}, u32[]{:S(2)}) %copy-start) | copy-done | bytes 393240
  1.6 0.0 copy-start.3
  1.6 1.0 %copy-done.3 = bf16[512,384]{1,0:T(8,128)(2,1)S(1)} copy-done((bf16[512,384]{1,0:T(8,128)(2,1)S(1)}, bf16[512,384]{1,0:T(8,128)(2,1)}, u32[]{:S(2)}) %copy-start.3) | copy-done | bytes 393240
  2.6 0.0 copy-start.6
  2.6 0.7 %copy-done.6 = s32[16]{0:T(128)S(1)} copy-done((s32[16]{0:T(128)S(1)}, s32[16]{0:T(128)}, u32[]{:S(2)}) %copy-start.6) | copy-done | bytes 88
  3.3 0.0 copy-start.8
  3.3 0.7 %copy-done.8 = s32[16]{0:T(128)S(1)} copy-done((s32[16]{0:T(128)S(1)}, s32[16]{0:T(128)}, u32[]{:S(2)}) %copy-start.8) | copy-done | bytes 88
  3.9 0.0 copy-start.7
  3.9 0.0 copy-start.9
  3.9 1.0 %shard_map.102 = (bf16[64,768]{1,0:T(8,128)(2,1)S(1)}, bf16[4,768]{1,0:T(4,128)(2,1)S(1)}) custom-call(s32[1]{0:T(128)} %bitcast.base_ref, s32[16]{0:T(128)S(1)} %copy-done.6, s32[16]{0:T(128)S(1)} %copy-done.8, bf16[512,384]{1,0:T(8,128)(2,1)S(1)} %copy-done, bf16[512,384]{1,0:T(8,128)(2,1)S(1)} %copy-done.3), custom_call_target="tpu_custom_call" | custom-call | bytes 786432 | tf_op jit(solution)/shard_map/pallas_call | solution.py:249
  5.0 3.0 %collective-permute-start.1 = (bf16[4,768]{1,0:T(4,128)(2,1)S(1)}, bf16[4,768]{1,0:T(4,128)(2,1)S(1)}, u32[]{:S(2)}, u32[]{:S(2)}) collective-permute-start(bf16[4,768]{1,0:T(4,128)(2,1)S(1)} %get-tuple-element.26), channel_id=1, source_target_pairs={{0,2},{2,0},{4,6},{6,4},{8,10},{10,8},{12,14},{14,12},{1,3},{3,1},... | collective-permute-start | bytes 18440 | tf_op jit(solution)/shard_map/ppermute | solution.py:247
  8.0 0.1 collective-permute-start
  8.7 0.1 broadcast_add_fusion
  8.8 0.0 copy-start.1
  8.8 1.0 %copy-done.1 = bf16[512,384]{1,0:T(8,128)(2,1)S(1)} copy-done((bf16[512,384]{1,0:T(8,128)(2,1)S(1)}, bf16[512,384]{1,0:T(8,128)(2,1)}, u32[]{:S(2)}) %copy-start.1) | copy-done | bytes 393240
  9.8 0.0 copy-start.4
  9.8 1.0 %copy-done.4 = bf16[512,384]{1,0:T(8,128)(2,1)S(1)} copy-done((bf16[512,384]{1,0:T(8,128)(2,1)S(1)}, bf16[512,384]{1,0:T(8,128)(2,1)}, u32[]{:S(2)}) %copy-start.4) | copy-done | bytes 393240
  10.8 0.0 copy-start.10
  10.8 1.0 %copy-done.10 = bf16[512,384]{1,0:T(8,128)(2,1)S(1)} copy-done((bf16[512,384]{1,0:T(8,128)(2,1)S(1)}, bf16[512,384]{1,0:T(8,128)(2,1)}, u32[]{:S(2)}) %copy-start.10) | copy-done | bytes 393240
  11.8 0.0 copy-start.11
  11.8 1.0 %copy-done.11 = bf16[512,384]{1,0:T(8,128)(2,1)S(1)} copy-done((bf16[512,384]{1,0:T(8,128)(2,1)S(1)}, bf16[512,384]{1,0:T(8,128)(2,1)}, u32[]{:S(2)}) %copy-start.11) | copy-done | bytes 393240
  12.8 6.4 %shard_map.103 = (bf16[8,512,512]{2,1,0:T(8,128)(2,1)}, bf16[384,512]{1,0:T(8,128)(2,1)S(1)}, bf16[384,512]{1,0:T(8,128)(2,1)S(1)}, bf16[384,512]{1,0:T(8,128)(2...) custom-call(s32[1]{0:T(128)S(6)} %min.6.live_ref, bf16[512,384]{1,0:T(8,128)(2,1)S(1)} %copy-done.10, ...), custom_call_target="tpu_custom_call" | custom-call | flops 2013265920 | bytes 4194304 | tf_op jit(solution)/shard_map/pallas_call | solution.py:265
  19.2 0.0 copy-start.2
  19.2 0.0 copy-start.5
  19.2 0.0 collective-permute-done.1
  19.2 2.1 %collective-permute-start.2 = (bf16[8,768]{1,0:T(8,128)(2,1)S(1)}, bf16[8,768]{1,0:T(8,128)(2,1)S(1)}, u32[]{:S(2)}, u32[]{:S(2)}) collective-permute-start(bf16[8,768]{1,0:T(8,128)(2,1)S(1)} %pad_maximum_fusion.2), channel_id=1, source_target_pairs={{0,4},{2,6},{4,0},{6,2},{8,12},{10,14},{12,8},{14,10},{1,5},{3,7},... | collective-permute-start | bytes 36872 | tf_op jit(solution)/shard_map/ppermute | solution.py:247
  21.3 0.1 add.49
  21.4 1.6 %collective-permute-done.2 = bf16[8,768]{1,0:T(8,128)(2,1)S(1)} collective-permute-done((bf16[8,768]{1,0:T(8,128)(2,1)S(1)}, bf16[8,768]{1,0:T(8,128)(2,1)S(1)}, u32[]{:S(2)}, u32[]{:S(2)}) %collective-permute-start.2) | collective-permute-done | bytes 12320 | tf_op jit(solution)/shard_map/ppermute | solution.py:247
  23.0 3.1 %collective-permute-start.3 = (bf16[16,768]{1,0:T(8,128)(2,1)S(1)}, bf16[16,768]{1,0:T(8,128)(2,1)S(1)}, u32[]{:S(2)}, u32[]{:S(2)}) collective-permute-start(bf16[16,768]{1,0:T(8,128)(2,1)S(1)} %pad_maximum_fusion.1), channel_id=1, source_target_pairs={{0,8},{2,10},{4,12},{6,14},{8,0},{10,2},{12,4},{14,6},{1,9},{3,11}... | collective-permute-start | bytes 73736 | tf_op jit(solution)/shard_map/ppermute | solution.py:247
  26.1 0.1 pad_add_fusion
  26.2 1.7 %collective-permute-done.3 = bf16[16,768]{1,0:T(8,128)(2,1)S(1)} collective-permute-done((bf16[16,768]{1,0:T(8,128)(2,1)S(1)}, bf16[16,768]{1,0:T(8,128)(2,1)S(1)}, u32[]{:S(2)}, u32[]{:S(2)}) %collective-permute-start.3) | collective-permute-done | bytes 24608 | tf_op jit(solution)/shard_map/ppermute | solution.py:247
  27.9 0.0 collective-permute-done.came_ref
  27.9 0.1 broadcast_in_dim.2.place_ref
  28.0 0.0 copy-done.7
  28.0 0.0 copy-done.9
  28.0 6.2 %shard_map.104 = (bf16[512,384]{1,0:T(8,128)(2,1)}, f32[8,512]{1,0:T(8,128)S(1)}, f32[8,512]{1,0:T(8,128)S(1)}, f32[384,512]{1,0:T(8,128)S(1)}, f32[64,768]{1,0:...) custom-call(s32[1]{0:T(128)} %bitcast.base_ref, s32[16]{0:T(128)S(1)} %copy-done.7, s32[16]{0:T(128)S(1)} %copy-done.9, ...), custom_call_target="tpu_custom_call" | custom-call | flops 1887436800 | bytes 1572864 | tf_op jit(solution)/shard_map/pallas_call | solution.py:288
  34.3 2.9 %collective-permute-start.5 = (f32[16,768]{1,0:T(8,128)S(1)}, f32[16,768]{1,0:T(8,128)S(1)}, u32[]{:S(2)}, u32[]{:S(2)}) collective-permute-start(f32[16,768]{1,0:T(8,128)S(1)} %slice.19), channel_id=1, source_target_pairs={{0,8},{2,10},{4,12},{6,14},{8,0},{10,2},{12,4},{14,6},{1,9},{3,11}... | collective-permute-start | bytes 147464 | tf_op jit(solution)/shard_map/ppermute | solution.py:247
  37.2 2.1 %collective-permute-done.5 = f32[16,768]{1,0:T(8,128)S(1)} collective-permute-done((f32[16,768]{1,0:T(8,128)S(1)}, f32[16,768]{1,0:T(8,128)S(1)}, u32[]{:S(2)}, u32[]{:S(2)}) %collective-permute-start.5) | collective-permute-done | bytes 49184 | tf_op jit(solution)/shard_map/ppermute | solution.py:247
  39.3 2.2 %collective-permute-start.6 = (f32[8,768]{1,0:T(8,128)S(1)}, f32[8,768]{1,0:T(8,128)S(1)}, u32[]{:S(2)}, u32[]{:S(2)}) collective-permute-start(f32[8,768]{1,0:T(8,128)S(1)} %slice.25), channel_id=1, source_target_pairs={{0,4},{2,6},{4,0},{6,2},{8,12},{10,14},{12,8},{14,10},{1,5},{3,7},... | collective-permute-start | bytes 73736 | tf_op jit(solution)/shard_map/ppermute | solution.py:247
  41.5 1.5 %collective-permute-start.4 = (f32[64,768]{1,0:T(8,128)S(1)}, f32[64,768]{1,0:T(8,128)S(1)}, u32[]{:S(2)}, u32[]{:S(2)}) collective-permute-start(f32[64,768]{1,0:T(8,128)S(1)} %get-tuple-element.42), channel_id=1, source_target_pairs={{0,2},{2,0},{4,6},{6,4},{8,10},{10,8},{12,14},{14,12},{1,3},{3,1},... | collective-permute-start | bytes 589832 | tf_op jit(solution)/shard_map/ppermute | solution.py:247
  43.0 0.3 collective-permute-done.6
  43.3 1.8 %collective-permute-start.7 = (f32[4,768]{1,0:T(4,128)S(1)}, f32[4,768]{1,0:T(4,128)S(1)}, u32[]{:S(2)}, u32[]{:S(2)}) collective-permute-start(f32[4,768]{1,0:T(4,128)S(1)} %slice.27), channel_id=1, source_target_pairs={{0,2},{2,0},{4,6},{6,4},{8,10},{10,8},{12,14},{14,12},{1,3},{3,1},... | collective-permute-start | bytes 36872 | tf_op jit(solution)/shard_map/ppermute | solution.py:247
  45.1 0.0 copy-done.2
  45.1 0.0 copy-done.5
  45.1 7.8 %shard_map.105 = (bf16[512,384]{1,0:T(8,128)(2,1)}, f32[512,384]{1,0:T(8,128)S(1)}, f32[512,384]{1,0:T(8,128)S(1)}) custom-call(bf16[8,512,512]{2,1,0:T(8,128)(2,1)} %get-tuple-element.33.p_ref, bf16[384,512]{1,0:T(8,128)(2,1)S(1)} %get-tuple-element.27.qt_ref, bf16[384,512]{1,0:T(8,128)(2,1)S(1)} %get-tuple-element.28.gt_ref, ...), custom_call_target="tpu_custom_call" | custom-call | flops 4026531840 | bytes 4194304 | tf_op jit(solution)/shard_map/pallas_call | solution.py:320
  52.9 0.0 collective-permute-done.7
  52.9 0.0 collective-permute-done.4.came_ref
  52.9 2.1 %shard_map.106 = (bf16[512,384]{1,0:T(8,128)(2,1)}, bf16[512,384]{1,0:T(8,128)(2,1)}) custom-call(s32[1]{0:T(128)} %bitcast.base_ref, s32[16]{0:T(128)S(1)} %copy-done.7, s32[16]{0:T(128)S(1)} %copy-done.9, f32[512,384]{1,0:T(8,128)S(1)} %get-tuple-element.39.dk_ref, f32[512,384]{1,0:T(8,128)S(1)} %get-tuple-element.40.dv_ref, ...), custom_call_target="tpu_custom_call" | custom-call | bytes 2359296 | tf_op jit(solution)/shard_map/pallas_call | solution.py:329
  (12 shorter events, 0.1 us)
Async XLA Ops:
  0.6 1.0 %copy-start = (bf16[512,384]{1,0:T(8,128)(2,1)S(1)}, bf16[512,384]{1,0:T(8,128)(2,1)}, u32[]{:S(2)}) copy-start(bf16[512,384]{1,0:T(8,128)(2,1)} %k_ref.5) | copy-start | bytes 1179652
  1.6 1.0 %copy-start.3 = (bf16[512,384]{1,0:T(8,128)(2,1)S(1)}, bf16[512,384]{1,0:T(8,128)(2,1)}, u32[]{:S(2)}) copy-start(bf16[512,384]{1,0:T(8,128)(2,1)} %v_ref.5) | copy-start | bytes 1179652
  2.6 0.7 %copy-start.6 = (s32[16]{0:T(128)S(1)}, s32[16]{0:T(128)}, u32[]{:S(2)}) copy-start(s32[16]{0:T(128)} %center_ref.5) | copy-start | bytes 196
  3.3 0.7 %copy-start.8 = (s32[16]{0:T(128)S(1)}, s32[16]{0:T(128)}, u32[]{:S(2)}) copy-start(s32[16]{0:T(128)} %wide_ref.5) | copy-start | bytes 196
  3.9 24.1 %copy-start.7 = (s32[16]{0:T(128)S(1)}, s32[16]{0:T(128)}, u32[]{:S(2)}) copy-start(s32[16]{0:T(128)} %center_ref.5) | copy-start | bytes 196
  3.9 24.1 %copy-start.9 = (s32[16]{0:T(128)S(1)}, s32[16]{0:T(128)}, u32[]{:S(2)}) copy-start(s32[16]{0:T(128)} %wide_ref.5) | copy-start | bytes 196
  5.0 14.2 %collective-permute-start.1 = (bf16[4,768]{1,0:T(4,128)(2,1)S(1)}, bf16[4,768]{1,0:T(4,128)(2,1)S(1)}, u32[]{:S(2)}, u32[]{:S(2)}) collective-permute-start(bf16[4,768]{1,0:T(4,128)(2,1)S(1)} %get-tuple-element.26), channel_id=1, source_target_pairs={{0,2},{2,0},{4,6},{6,4},{8,10},{10,8},{12,14},{14,12},{1,3},{3,1},... | collective-permute-start | bytes 18440 | tf_op jit(solution)/shard_map/ppermute | solution.py:247
  8.0 19.9 %collective-permute-start = (bf16[64,768]{1,0:T(8,128)(2,1)S(1)}, bf16[64,768]{1,0:T(8,128)(2,1)S(1)}, u32[]{:S(2)}, u32[]{:S(2)}) collective-permute-start(bf16[64,768]{1,0:T(8,128)(2,1)S(1)} %get-tuple-element.25.near_ref), channel_id=1, source_target_pairs={{0,2},{2,0},{4,6},{6,4},{8,10},{10,8},{12,14},{14,12},{1,3},{3,1},... | collective-permute-start | bytes 294920 | tf_op jit(solution)/shard_map/ppermute | solution.py:247
  8.8 1.0 %copy-start.1 = (bf16[512,384]{1,0:T(8,128)(2,1)S(1)}, bf16[512,384]{1,0:T(8,128)(2,1)}, u32[]{:S(2)}) copy-start(bf16[512,384]{1,0:T(8,128)(2,1)} %k_ref.5) | copy-start | bytes 1179652
  9.8 1.0 %copy-start.4 = (bf16[512,384]{1,0:T(8,128)(2,1)S(1)}, bf16[512,384]{1,0:T(8,128)(2,1)}, u32[]{:S(2)}) copy-start(bf16[512,384]{1,0:T(8,128)(2,1)} %v_ref.5) | copy-start | bytes 1179652
  10.8 1.0 %copy-start.10 = (bf16[512,384]{1,0:T(8,128)(2,1)S(1)}, bf16[512,384]{1,0:T(8,128)(2,1)}, u32[]{:S(2)}) copy-start(bf16[512,384]{1,0:T(8,128)(2,1)} %q_ref.1) | copy-start | bytes 1179652
  11.8 1.0 %copy-start.11 = (bf16[512,384]{1,0:T(8,128)(2,1)S(1)}, bf16[512,384]{1,0:T(8,128)(2,1)}, u32[]{:S(2)}) copy-start(bf16[512,384]{1,0:T(8,128)(2,1)} %g_ref.1) | copy-start | bytes 1179652
  19.2 25.9 %copy-start.2 = (bf16[512,384]{1,0:T(8,128)(2,1)S(1)}, bf16[512,384]{1,0:T(8,128)(2,1)}, u32[]{:S(2)}) copy-start(bf16[512,384]{1,0:T(8,128)(2,1)} %k_ref.5) | copy-start | bytes 1179652
  19.2 25.9 %copy-start.5 = (bf16[512,384]{1,0:T(8,128)(2,1)S(1)}, bf16[512,384]{1,0:T(8,128)(2,1)}, u32[]{:S(2)}) copy-start(bf16[512,384]{1,0:T(8,128)(2,1)} %v_ref.5) | copy-start | bytes 1179652
  19.2 3.8 %collective-permute-start.2 = (bf16[8,768]{1,0:T(8,128)(2,1)S(1)}, bf16[8,768]{1,0:T(8,128)(2,1)S(1)}, u32[]{:S(2)}, u32[]{:S(2)}) collective-permute-start(bf16[8,768]{1,0:T(8,128)(2,1)S(1)} %pad_maximum_fusion.2), channel_id=1, source_target_pairs={{0,4},{2,6},{4,0},{6,2},{8,12},{10,14},{12,8},{14,10},{1,5},{3,7},... | collective-permute-start | bytes 36872 | tf_op jit(solution)/shard_map/ppermute | solution.py:247
  23.0 4.9 %collective-permute-start.3 = (bf16[16,768]{1,0:T(8,128)(2,1)S(1)}, bf16[16,768]{1,0:T(8,128)(2,1)S(1)}, u32[]{:S(2)}, u32[]{:S(2)}) collective-permute-start(bf16[16,768]{1,0:T(8,128)(2,1)S(1)} %pad_maximum_fusion.1), channel_id=1, source_target_pairs={{0,8},{2,10},{4,12},{6,14},{8,0},{10,2},{12,4},{14,6},{1,9},{3,11}... | collective-permute-start | bytes 73736 | tf_op jit(solution)/shard_map/ppermute | solution.py:247
  34.3 5.0 %collective-permute-start.5 = (f32[16,768]{1,0:T(8,128)S(1)}, f32[16,768]{1,0:T(8,128)S(1)}, u32[]{:S(2)}, u32[]{:S(2)}) collective-permute-start(f32[16,768]{1,0:T(8,128)S(1)} %slice.19), channel_id=1, source_target_pairs={{0,8},{2,10},{4,12},{6,14},{8,0},{10,2},{12,4},{14,6},{1,9},{3,11}... | collective-permute-start | bytes 147464 | tf_op jit(solution)/shard_map/ppermute | solution.py:247
  39.3 4.0 %collective-permute-start.6 = (f32[8,768]{1,0:T(8,128)S(1)}, f32[8,768]{1,0:T(8,128)S(1)}, u32[]{:S(2)}, u32[]{:S(2)}) collective-permute-start(f32[8,768]{1,0:T(8,128)S(1)} %slice.25), channel_id=1, source_target_pairs={{0,4},{2,6},{4,0},{6,2},{8,12},{10,14},{12,8},{14,10},{1,5},{3,7},... | collective-permute-start | bytes 73736 | tf_op jit(solution)/shard_map/ppermute | solution.py:247
  41.5 11.5 %collective-permute-start.4 = (f32[64,768]{1,0:T(8,128)S(1)}, f32[64,768]{1,0:T(8,128)S(1)}, u32[]{:S(2)}, u32[]{:S(2)}) collective-permute-start(f32[64,768]{1,0:T(8,128)S(1)} %get-tuple-element.42), channel_id=1, source_target_pairs={{0,2},{2,0},{4,6},{6,4},{8,10},{10,8},{12,14},{14,12},{1,3},{3,1},... | collective-permute-start | bytes 589832 | tf_op jit(solution)/shard_map/ppermute | solution.py:247
  43.3 9.6 %collective-permute-start.7 = (f32[4,768]{1,0:T(4,128)S(1)}, f32[4,768]{1,0:T(4,128)S(1)}, u32[]{:S(2)}, u32[]{:S(2)}) collective-permute-start(f32[4,768]{1,0:T(4,128)S(1)} %slice.27), channel_id=1, source_target_pairs={{0,2},{2,0},{4,6},{6,4},{8,10},{10,8},{12,14},{14,12},{1,3},{3,1},... | collective-permute-start | bytes 36872 | tf_op jit(solution)/shard_map/ppermute | solution.py:247

commit v2 on v1

v2 whole, which is shorter than its diff:
```python
import functools
import math

import jax
import jax.numpy as jnp
from jax import lax
from jax.experimental import pallas as pl
from jax.experimental.pallas import tpu as pltpu
from jax.sharding import PartitionSpec as P

HEAD_WIDTH = 48
CENTER_DILATION = 8
WIDE_DILATION = 128
LANES = 128
DEAD = -1e30
SCALE = HEAD_WIDTH**-0.5
EXP2_SCALE = SCALE * math.log2(math.e)
F32 = jnp.float32
BF16 = jnp.bfloat16

VMEM = pl.BlockSpec(memory_space=pltpu.VMEM)
SMEM = pl.BlockSpec(memory_space=pltpu.SMEM)


def nn(a, b):
    return jnp.dot(a, b, preferred_element_type=F32)


def nt(a, b):
    return lax.dot_general(a, b, (((1,), (1,)), ((), ())), preferred_element_type=F32)


def head_rows(h):
    return slice(h * HEAD_WIDTH, (h + 1) * HEAD_WIDTH)


def window(h):
    low = h * HEAD_WIDTH // LANES * LANES
    high = -(-(h + 1) * HEAD_WIDTH // LANES) * LANES
    return low, high


def embed(rows, h):
    low, high = window(h)
    before, after = h * HEAD_WIDTH - low, high - (h + 1) * HEAD_WIDTH
    parts = [rows]
    if before:
        parts.insert(0, jnp.zeros((before, rows.shape[1]), rows.dtype))
    if after:
        parts.append(jnp.zeros((after, rows.shape[1]), rows.dtype))
    return jnp.concatenate(parts, axis=0) if len(parts) > 1 else rows


def add_window(ref, h, value, started, at0):
    low, high = window(h)
    for at in range(low, high, LANES):
        part = value[:, at - low : at - low + LANES]
        here = slice(at - at0, at - at0 + LANES)
        if at in started:
            ref[:, here] += part
        else:
            started.add(at)
            ref[:, here] = part


def head_groups(heads):
    size = -(-heads // 3)
    groups = []
    for first in range(0, heads, size):
        last = min(first + size, heads)
        groups.append((first, last, window(first)[0], window(last - 1)[1]))
    return groups


def lane_shifts(shift_ref, base, heads, width):
    lane = lax.broadcasted_iota(jnp.int32, (1, width), 1)
    row = jnp.zeros((1, width), jnp.int32)
    for h in range(heads):
        inside = (lane >= h * HEAD_WIDTH) & (lane < (h + 1) * HEAD_WIDTH)
        row = jnp.where(inside, shift_ref[base + h], row)
    return row


def head_base(heads):
    return lax.axis_index("hd") * heads


def select_kernel(
    heads, valid_ref, center_any, wide_any, q_any, k_any, v_any, g_any,
    near_ref, far_ref, q_ref, k_ref, v_ref, g_ref, table_ref, lanes_ref,
    center_ref, wide_ref, spread_ref, sems,
):
    rows, width = k_ref.shape
    pairs = (
        (center_any, center_ref), (wide_any, wide_ref),
        (k_any, k_ref), (v_any, v_ref), (q_any, q_ref), (g_any, g_ref),
    )
    copies = [pltpu.make_async_copy(a, b, sems.at[i]) for i, (a, b) in enumerate(pairs)]
    for copy in copies:
        copy.start()
    for copy in copies[:2]:
        copy.wait()
    base = head_base(heads)
    center = lane_shifts(center_ref, base, heads, width)
    wide = lane_shifts(wide_ref, base, heads, width)
    lanes_ref[0:1, :] = center
    lanes_ref[1:2, :] = wide
    for h in range(heads):
        table_ref[h : h + 1, :] = jnp.full((1, rows), center_ref[base + h], jnp.int32)
        table_ref[heads + h : heads + h + 1, :] = jnp.full((1, rows), wide_ref[base + h], jnp.int32)
    table_ref[2 * heads : 2 * heads + 1, :] = jnp.full((1, rows), valid_ref[0], jnp.int32)
    near_rows = rows // CENTER_DILATION
    far_rows = rows // WIDE_DILATION
    row = lax.broadcasted_iota(jnp.int32, (far_rows, WIDE_DILATION, LANES), 1)
    for at, ref, copy in ((0, k_ref, copies[2]), (width, v_ref, copies[3])):
        copy.wait()
        for low in range(0, width, LANES):
            lanes = slice(low, low + LANES)
            packed = slice(at + low, at + low + LANES)
            spread = ref[:, lanes].astype(F32)
            spread_ref[at // width * (width // LANES) + low // LANES] = spread
            chosen = jnp.where(row == wide[:, lanes], spread.reshape(row.shape), 0.0)
            far_ref[:, packed] = jnp.sum(chosen, axis=1).astype(BF16)
    for at in (0, width):
        for low in range(0, width, LANES):
            lanes = slice(low, low + LANES)
            packed = slice(at + low, at + low + LANES)
            block = at // width * (width // LANES) + low // LANES
            picked = jnp.zeros((near_rows, LANES), F32)
            for step in range(CENTER_DILATION):
                rows_at = spread_ref[block, pl.ds(step, near_rows, stride=CENTER_DILATION), :]
                picked = jnp.where(center[:, lanes] == step, rows_at, picked)
            near_ref[:, packed] = picked.astype(BF16)
    copies[4].wait()
    copies[5].wait()


def forward_kernel(
    group, heads, q_ref, k_ref, v_ref, g_ref, table_ref, after_ref,
    p_ref, qt_ref, gt_ref, kt_ref, ot_ref, max_ref, sum_ref, vt_ref,
):
    first, last, low0, high0 = group
    rows = q_ref.shape[0]
    mine = slice(first * HEAD_WIDTH - low0, last * HEAD_WIDTH - low0)
    lanes0 = slice(low0, high0)
    qt_ref[...] = q_ref[:, lanes0].T[mine, :]
    vt_ref[...] = v_ref[:, lanes0].T[mine, :]
    device = lax.axis_index(("seq", "sub"))
    row = lax.broadcasted_iota(jnp.int32, (rows, LANES), 0)
    dead = jnp.where(device * rows + row < table_ref[2 * heads : 2 * heads + 1, :LANES], 0.0, DEAD)
    dead = jnp.concatenate([dead] * (rows // LANES), axis=1)

    def scores_of(h):
        low, high = window(h)
        return nn(k_ref[:, low:high], embed(qt_ref[head_rows(h - first), :], h))

    following = scores_of(first)
    for h in range(first, last):
        scores = following + dead
        if h + 1 < last:
            following = scores_of(h + 1)
        at = h - first
        is_near = (row & (CENTER_DILATION - 1)) == table_ref[h : h + 1, :LANES]
        is_far = (row & (WIDE_DILATION - 1)) == table_ref[heads + h : heads + h + 1, :LANES]
        times = 1.0 + is_near.astype(F32) + is_far.astype(F32)
        times = jnp.concatenate([times] * (rows // LANES), axis=1)
        top = jnp.max(scores, axis=0, keepdims=True)
        lifted = jnp.exp2((scores - top) * EXP2_SCALE) * times
        max_ref[at : at + 1, :] = top
        sum_ref[at : at + 1, :] = jnp.sum(lifted, axis=0, keepdims=True)
        weights = lifted.astype(BF16)
        p_ref[at] = weights
        ot_ref[head_rows(at), :] = nn(vt_ref[head_rows(at), :], weights)
    gt_ref[...] = g_ref[:, lanes0].T[mine, :]
    kt_ref[...] = k_ref[:, lanes0].T[mine, :]


def remote_kernel(heads, groups, far_own, table_ref, mine_ref, came_ref, *refs):
    parts = len(groups)
    qt_refs, gt_refs, o1_refs, max_refs, sum_refs = (refs[i * parts : (i + 1) * parts] for i in range(5))
    (
        ot_ref, factor_ref, delta_ref, ds_ref, kr_ref, keep_ref, send_ref,
        vr_ref, vrt_ref, dk_ref, dv_ref,
    ) = refs[5 * parts :]
    width, rows = ot_ref.shape
    half = came_ref.shape[0]
    near_rows = rows // CENTER_DILATION
    count = half + half - near_rows
    for at, ref in ((width, vr_ref), (0, kr_ref)):
        ref[:half, :] = came_ref[:, at : at + width]
        ref[half:, :] = mine_ref[near_rows:, at : at + width]
    vrt_ref[...] = vr_ref[...].T
    device = lax.axis_index(("seq", "sub"))
    row = lax.broadcasted_iota(jnp.int32, (count, LANES), 0)
    is_near = row < near_rows
    is_own = (row >= half) & (row < half + far_own)
    far_row = jnp.where(row < half, row - near_rows, row - half)
    slot = lax.shift_right_arithmetic(far_row, far_own.bit_length() - 1)
    code = 2 * slot + jnp.where(row < half, 1, 0)
    far_place = (device ^ code) * rows + (far_row & (far_own - 1)) * WIDE_DILATION
    place = jnp.where(is_near, (device ^ 1) * rows + row * CENTER_DILATION, far_place)
    room = jnp.where(is_own, -1, table_ref[2 * heads : 2 * heads + 1, :LANES] - place)
    began_k, began_v = set(), set()
    where = {}
    for part, (first, last, _, _) in enumerate(groups):
        for h in range(first, last):
            where[h] = part, h - first

    def products(h):
        low, high = window(h)
        part, at = where[h]
        q_rows = embed(qt_refs[part][head_rows(at), :], h)
        g_rows = embed(gt_refs[part][head_rows(at), :], h)
        return q_rows, g_rows, nn(kr_ref[:, low:high], q_rows), nn(vr_ref[:, low:high], g_rows)

    def forward(h, scores):
        part, at = where[h]
        shift = jnp.where(
            is_near, table_ref[h : h + 1, :LANES], table_ref[heads + h : heads + h + 1, :LANES]
        )
        dead = jnp.where(shift < room, 0.0, DEAD)
        scores = scores + jnp.concatenate([dead] * (rows // LANES), axis=1)
        top_here = max_refs[part][at : at + 1, :]
        top = jnp.maximum(jnp.max(scores, axis=0, keepdims=True), top_here)
        lifted = jnp.exp2((scores - top) * EXP2_SCALE)
        keep = jnp.exp2((top_here - top) * EXP2_SCALE)
        total = sum_refs[part][at : at + 1, :] * keep + jnp.sum(lifted, axis=0, keepdims=True)
        inverse = 1.0 / total
        prob = lifted * inverse
        factor = keep * inverse
        weights = prob.astype(BF16)
        return prob, weights, factor, nn(vrt_ref[head_rows(h), :], weights)

    def backward(h, q_rows, g_rows, grad_prob, prob, weights, factor, product):
        part, at = where[h]
        context = o1_refs[part][head_rows(at), :] * factor + product
        ot_ref[head_rows(h), :] = context.astype(BF16)
        g_head = gt_refs[part][head_rows(at), :].astype(F32)
        delta = jnp.sum(g_head * context, axis=0, keepdims=True)
        factor_ref[h : h + 1, :] = factor
        delta_ref[h : h + 1, :] = delta
        dscore = (prob * (grad_prob - delta)).astype(BF16)
        ds_ref[h] = dscore
        add_window(dk_ref, h, nt(dscore, q_rows), began_k, 0)
        add_window(dv_ref, h, nt(weights, g_rows), began_v, 0)

    made, done = {}, {}
    for step in range(heads + 2):
        if step < heads:
            made[step] = products(step)
        if 0 <= step - 1 < heads:
            done[step - 1] = forward(step - 1, made[step - 1][2])
        if 0 <= step - 2 < heads:
            q_rows, g_rows, _, grad_prob = made.pop(step - 2)
            backward(step - 2, q_rows, g_rows, grad_prob, *done.pop(step - 2))
    for at, ref, by in ((0, dk_ref, SCALE), (width, dv_ref, 1.0)):
        send_ref[:, at : at + width] = (ref[:half, :] * by).astype(send_ref.dtype)
        keep_ref[:, at : at + width] = ref[half:, :] * by


def backward_heads(
    group, p_ref, qt_ref, gt_ref, kt_ref, v_ref, kr_ref, ds2_ref, factor_ref, delta_ref,
    dqt_ref, dk_ref, dv_ref, krt_ref,
):
    first, last, low0, high0 = group
    mine = slice(first * HEAD_WIDTH - low0, last * HEAD_WIDTH - low0)
    krt_ref[...] = kr_ref[:, low0:high0].T[mine, :]
    began_k, began_v = set(), set()

    def products(h):
        low, high = window(h)
        g_rows = embed(gt_ref[head_rows(h - first), :], h)
        return g_rows, nn(v_ref[:, low:high], g_rows)

    following = products(first)
    for h in range(first, last):
        g_rows, grad_prob = following
        if h + 1 < last:
            following = products(h + 1)
        at = h - first
        q_rows = embed(qt_ref[head_rows(at), :], h)
        prob = p_ref[at].astype(F32) * factor_ref[h : h + 1, :]
        dscore = (prob * (grad_prob - delta_ref[h : h + 1, :])).astype(BF16)
        dqt = nn(krt_ref[head_rows(at), :], ds2_ref[h]) + nn(kt_ref[head_rows(at), :], dscore)
        dqt_ref[head_rows(at), :] = (dqt * SCALE).astype(BF16)
        add_window(dv_ref, h, nt(prob.astype(BF16), g_rows), began_v, low0)
        add_window(dk_ref, h, nt(dscore, q_rows), began_k, low0)


def first_backward_kernel(group, *refs):
    ot_ref, after_ref = refs[9:11]
    out_ref = refs[11]
    backward_heads(group, *refs[:9], *refs[12:])
    out_ref[...] = ot_ref[...].T


def middle_backward_kernel(group, *refs):
    backward_heads(group, *refs[:9], *refs[10:])


def last_backward_kernel(groups, *refs):
    others = len(groups) - 1
    lanes_ref, back_ref, after_ref = refs[9:12]
    terms = refs[12 : 12 + 3 * others]
    dq_ref, sum_ref, dqt_ref, dk_ref, dv_ref, krt_ref, turned_ref = refs[12 + 3 * others :]
    backward_heads(groups[-1], *refs[:9], dqt_ref, dk_ref, dv_ref, krt_ref)
    dqt_refs = (*terms[:others], dqt_ref)
    dk_refs = (*terms[others : 2 * others], dk_ref)
    dv_refs = (*terms[2 * others :], dv_ref)
    rows, width = dq_ref.shape
    near_rows = rows // CENTER_DILATION
    for (first, last, _, _), ref in zip(groups, dqt_refs):
        turned_ref[first * HEAD_WIDTH : last * HEAD_WIDTH, :] = ref[...]
    dq_ref[...] = turned_ref[...].T
    for at, parts, by in ((0, dk_refs, SCALE), (width, dv_refs, 1.0)):
        for low in range(0, width, LANES):
            block = (at + low) // LANES
            value = None
            for (_, _, low0, high0), ref in zip(groups, parts):
                if low0 <= low < high0:
                    term = ref[:, low - low0 : low - low0 + LANES]
                    value = term if value is None else value + term
            sum_ref[block] = value * by
            near = back_ref[:near_rows, at + low : at + low + LANES].astype(F32)
            center = lanes_ref[0:1, low : low + LANES]
            for step in range(CENTER_DILATION):
                strided = pl.ds(step, near_rows, stride=CENTER_DILATION)
                sum_ref[block, strided, :] += jnp.where(center == step, near, 0.0)


def combine_kernel(lanes_ref, sum_ref, far_ref, outk_ref, outv_ref):
    rows, width = outk_ref.shape
    far_rows = far_ref.shape[0]
    row = lax.broadcasted_iota(jnp.int32, (WIDE_DILATION, LANES), 0)
    for at, out in ((0, outk_ref), (width, outv_ref)):
        for low in range(0, width, LANES):
            block = (at + low) // LANES
            mask = row == lanes_ref[1:2, low : low + LANES]
            for index in range(far_rows):
                part = slice(index * WIDE_DILATION, (index + 1) * WIDE_DILATION)
                far = far_ref[index : index + 1, at + low : at + low + LANES]
                value = sum_ref[block, part, :] + jnp.where(mask, far, 0.0)
                out[part, low : low + LANES] = value.astype(BF16)


ANY = pl.BlockSpec(memory_space=pl.ANY)
HBM = pl.BlockSpec(memory_space=pltpu.HBM)


def call(body, outs, ins, scratch=(), flops=0, moved=0):
    return pl.pallas_call(
        body,
        out_shape=[jax.ShapeDtypeStruct(s, d) for s, d in outs],
        in_specs=ins,
        out_specs=[VMEM] * len(outs),
        scratch_shapes=list(scratch),
        compiler_params=pltpu.CompilerParams(vmem_limit_bytes=24 * 2**20),
        cost_estimate=pl.CostEstimate(flops=flops, bytes_accessed=moved, transcendentals=0),
    )


def local(queries, keys, values, grad_out, center_shift, wide_shift, valid_count):
    rows, width = queries.shape
    heads = width // HEAD_WIDTH
    groups = head_groups(heads)
    near_rows, far_own = rows // CENTER_DILATION, rows // WIDE_DILATION
    axes = ("seq", "sub")
    devices = lax.axis_size(axes)
    half = near_rows + far_own * devices // 2
    count = half + half - near_rows
    blocks = 2 * width // LANES
    order = [2**bit for bit in range(1, devices.bit_length() - 1)]

    def swap(value, apart):
        return lax.ppermute(value, axes, [(at, at ^ apart) for at in range(devices)])

    near, far, q, k, v, g, table, lanes = call(
        functools.partial(select_kernel, heads),
        [((near_rows, 2 * width), BF16), ((far_own, 2 * width), BF16)]
        + [((rows, width), BF16)] * 4
        + [((2 * heads + 8, rows), jnp.int32), ((8, width), jnp.int32)],
        [SMEM] + [HBM] * 6,
        [
            pltpu.SMEM(center_shift.shape, jnp.int32),
            pltpu.SMEM(wide_shift.shape, jnp.int32),
            pltpu.VMEM((blocks, rows, LANES), F32),
            pltpu.SemaphoreType.DMA((6,)),
        ],
        moved=16 * rows * width,
    )(
        valid_count,
        *(
            pltpu.with_memory_space_constraint(value, pltpu.HBM)
            for value in (center_shift, wide_shift, queries, keys, values, grad_out)
        )
    )

    def forward(index, after):
        first, last, _, _ = groups[index]
        size, tall = last - first, (last - first) * HEAD_WIDTH
        return call(
            functools.partial(forward_kernel, groups[index], heads),
            [
                ((size, rows, rows), BF16),
                ((tall, rows), BF16),
                ((tall, rows), BF16),
                ((tall, rows), BF16),
                ((tall, rows), F32),
                ((size, rows), F32),
                ((size, rows), F32),
            ],
            [VMEM] * 5 + [ANY],
            [pltpu.VMEM((tall, rows), BF16)],
            flops=2 * 2 * rows * rows * tall * 5,
            moved=size * rows * rows * 2,
        )(q, k, v, g, table, after)

    def in_step(run, sequence, after, transfers):
        results, left = {}, list(sequence)
        for start, finish in transfers:
            arrived = start()
            if left:
                index = left.pop(0)
                made = list(run(index, after, results))
                arrived, made[-1] = lax.optimization_barrier((arrived, made[-1]))
                results[index] = made
            finish(arrived)
            after = arrived
        for index in left:
            results[index] = run(index, after, results)
        return [results[index] for index in sorted(results)]

    box = {"far": far}

    def gather(step):
        def start():
            return swap(box["far"], step)

        def finish(arrived):
            box["far"] = jnp.concatenate([box["far"], arrived], axis=0)

        return start, finish

    def meet():
        box["mine"] = jnp.concatenate([near, box["far"]], axis=0)
        return swap(box["mine"], 1)

    def met(arrived):
        box["came"] = arrived

    parts = in_step(
        lambda index, after, _: forward(index, after),
        [len(groups) - 1, *range(len(groups) - 1)],
        far,
        [gather(step) for step in order] + [(meet, met)],
    )
    p, qt, gt, kt, o1, top, total = zip(*parts)

    ot, factor, delta, ds2, kr, keep, send = call(
        functools.partial(remote_kernel, heads, groups, far_own),
        [
            ((width, rows), BF16),
            ((heads, rows), F32),
            ((heads, rows), F32),
            ((heads, count, rows), BF16),
            ((count, width), BF16),
            ((count - half, 2 * width), F32),
            ((half, 2 * width), BF16),
        ],
        [VMEM] * (3 + 5 * len(groups)),
        [
            pltpu.VMEM((count, width), BF16),
            pltpu.VMEM((width, count), BF16),
            pltpu.VMEM((count, width), F32),
            pltpu.VMEM((count, width), F32),
        ],
        flops=5 * 2 * rows * width * count * 5,
        moved=8 * rows * width,
    )(table, box["mine"], box["came"], *qt, *gt, *o1, *top, *total)

    def meet_back():
        return swap(send, 1)

    def met_back(arrived):
        box["back"] = arrived
        box["terms"] = keep + arrived[near_rows:].astype(F32)

    def reduce(step):
        def start():
            return swap(box["terms"][box["terms"].shape[0] // 2 :], step)

        def finish(arrived):
            box["terms"] = box["terms"][: arrived.shape[0]] + arrived

        return start, finish

    def backward(index, after, results):
        first, last, low0, high0 = groups[index]
        size, tall = last - first, (last - first) * HEAD_WIDTH
        heads_in = (p[index], qt[index], gt[index], kt[index], v, kr, ds2, factor, delta)
        partial = [((tall, rows), BF16), ((rows, high0 - low0), F32), ((rows, high0 - low0), F32)]
        turned = pltpu.VMEM((tall, count), BF16)
        cost = dict(flops=4 * 2 * rows * rows * tall * 5, moved=size * rows * rows * 2)
        if index == 0:
            out, *terms = call(
                functools.partial(first_backward_kernel, groups[index]),
                [((rows, width), BF16), *partial],
                [VMEM] * 10 + [ANY],
                [turned],
                **cost,
            )(*heads_in, ot, after)
            box["out"] = out
            return terms
        if index < len(groups) - 1:
            return call(
                functools.partial(middle_backward_kernel, groups[index]),
                partial,
                [VMEM] * 9 + [ANY],
                [turned],
                **cost,
            )(*heads_in, after)
        others = [terms for _, terms in sorted(results.items())]
        return call(
            functools.partial(last_backward_kernel, groups),
            [((rows, width), BF16), ((blocks, rows, LANES), F32)],
            [VMEM] * 11 + [ANY] + [VMEM] * (3 * len(others)),
            [pltpu.VMEM(shape, dtype) for shape, dtype in partial]
            + [turned, pltpu.VMEM((width, rows), BF16)],
            **cost,
        )(*heads_in, lanes, box["back"], after, *[t[i] for i in range(3) for t in others])

    parts = in_step(
        backward, range(len(groups)), send, [(meet_back, met_back)] + [reduce(step) for step in reversed(order)]
    )
    dq, sums = parts[-1]
    key_gradient, value_gradient = call(
        combine_kernel,
        [((rows, width), BF16)] * 2,
        [VMEM] * 3,
        moved=12 * rows * width,
    )(lanes, sums, box["terms"])
    return box["out"], dq, key_gradient, value_gradient


def solution(mesh):
    split = P(("grp", "seq", "sub"), "hd")
    return jax.shard_map(
        local,
        mesh=mesh,
        in_specs=(split, split, split, split, P(), P(), P("grp")),
        out_specs=(split, split, split, split),
        check_vma=False,
    )
```

time: 55.5 us -> 35.9 us (0.65)
  local copies, waits for them, and re-layouts: 7.46 us -> 0.01 us
  Pallas kernels: 23.6 us -> 18.1 us
  starting transfers between devices: 16.7 us -> 13.5 us
  waiting for transfers between devices: 5.68 us -> 2.68 us
    unnamed x24 -> x0, local copies, waits for them, and re-layouts: 7.29 us -> none
    pallas_call x4 -> x8, Pallas kernels: 22.5 us -> 16.6 us  [the longest x3 5.58 us: forward(): call(functools.partial(forward_kernel, groups[index], heads), [((size, ro...]
    ppermute x8 -> x6, starting transfers between devices: 16.7 us -> 13.5 us  [swap(): lax.ppermute(value, axes, [(at, at ^ apart) for at in range(devices)])]
    ppermute x8 -> x6, waiting for transfers between devices: 5.68 us -> 2.68 us  [swap(): lax.ppermute(value, axes, [(at, at ^ apart) for at in range(devices)])]
  transfers between devices with their start and end apart: 8 -> 6, of which waited for: 4 -> 4; matrix products, arithmetic and copies ran while one was open for 1% -> 0% of each run, Pallas kernels for 26% -> 35%
where the time goes in v2:
time: 35.9 us; the launch traced here: 35.7 us
  Pallas kernels  18.1 us (50%)
  starting transfers between devices  13.5 us (38%)
  waiting for transfers between devices  2.68 us (7%)
  between operations  1.35 us (4%)
    ppermute x6, starting transfers between devices, swap(): lax.ppermute(value, axes, [(at, at ^ apart) for at in range(devices)])  13.5 us
    pallas_call x3, Pallas kernels, forward(): call(functools.partial(forward_kernel, groups[index], heads), [((size, ro...  5.58 us
    pallas_call x1, Pallas kernels, local(): call(functools.partial(remote_kernel, heads, groups, far_own), [((width,...  3.09 us
    ppermute x6, waiting for transfers between devices, swap(): lax.ppermute(value, axes, [(at, at ^ apart) for at in range(devices)])  2.68 us
    pallas_call x1, Pallas kernels, backward(): call(functools.partial(first_backward_kernel, groups[index]), [((rows, wi...  2.55 us
    pallas_call x1, Pallas kernels, backward(): call(functools.partial(last_backward_kernel, groups), [((rows, width), BF...  2.51 us
    pallas_call x1, Pallas kernels, backward(): call(functools.partial(middle_backward_kernel, groups[index]), partial, [...  1.88 us
    pallas_call x1, Pallas kernels, local(): call(functools.partial(select_kernel, heads), [((near_rows, 2 * width), B...  1.54 us
  transfers between devices with their start and end apart: 6, of which 4 were waited for; matrix products, arithmetic and copies ran while one was open for 0% of the time, Pallas kernels for 35%

profile of v2, /device:TPU:0, one launch (start us, length us, event | category | flops | bytes accessed | tf_op | source)
XLA Modules:
  0.0 35.7 jit_solution(7734887610977835859)
XLA Ops:
  1.3 1.5 %shard_map.102 = (bf16[64,768]{1,0:T(8,128)(2,1)S(1)}, bf16[4,768]{1,0:T(4,128)(2,1)S(1)}, bf16[512,384]{1,0:T(8,128)(2,1)S(1)}, bf16[512,384]{1,0:T(8,128)(2,1)...) custom-call(s32[1]{0:T(128)S(6)} %copy.11.valid_ref, ...), custom_call_target="tpu_custom_call" | custom-call | bytes 3145728 | tf_op jit(solution)/shard_map/pallas_call | solution.py:377
  2.8 3.1 %collective-permute-start = (bf16[4,768]{1,0:T(4,128)(2,1)S(1)}, bf16[4,768]{1,0:T(4,128)(2,1)S(1)}, u32[]{:S(2)}, u32[]{:S(2)}) collective-permute-start(bf16[4,768]{1,0:T(4,128)(2,1)S(1)} %get-tuple-element.68.after_ref), channel_id=1, source_target_pairs={{0,4},{2,6},{4,0},{6,2},{8,12},{10,14},{12,8},{14,10},{1,5},{3,7},... | collective-permute-start | bytes 18440 | tf_op jit(solution)/shard_map/ppermute | solution.py:375
  5.9 1.4 %shard_map.103 = (bf16[2,512,512]{2,1,0:T(8,128)(2,1)S(1)}, bf16[96,512]{1,0:T(8,128)(2,1)S(1)}, bf16[96,512]{1,0:T(8,128)(2,1)S(1)}, bf16[96,512]{1,0:T(8,128)(...) custom-call(bf16[512,384]{1,0:T(8,128)(2,1)S(1)} %get-tuple-element.63.q_ref, ...), custom_call_target="tpu_custom_call" | custom-call | flops 503316480 | bytes 1048576 | tf_op jit(solution)/shard_map/pallas_call | solution.py:401
  7.3 0.2 collective-permute-done.after_ref
  7.5 3.1 %collective-permute-start.1 = (bf16[8,768]{1,0:T(8,128)(2,1)S(1)}, bf16[8,768]{1,0:T(8,128)(2,1)S(1)}, u32[]{:S(2)}, u32[]{:S(2)}) collective-permute-start(bf16[8,768]{1,0:T(8,128)(2,1)S(1)} %pad_maximum_fusion.1), channel_id=1, source_target_pairs={{0,8},{2,10},{4,12},{6,14},{8,0},{10,2},{12,4},{14,6},{1,9},{3,11}... | collective-permute-start | bytes 36872 | tf_op jit(solution)/shard_map/ppermute | solution.py:375
  10.6 2.1 %shard_map.104 = (bf16[3,512,512]{2,1,0:T(8,128)(2,1)S(1)}, bf16[144,512]{1,0:T(8,128)(2,1)S(1)}, bf16[144,512]{1,0:T(8,128)(2,1)S(1)}, bf16[144,512]{1,0:T(8,12...) custom-call(bf16[512,384]{1,0:T(8,128)(2,1)S(1)} %get-tuple-element.63.q_ref, ...), custom_call_target="tpu_custom_call" | custom-call | flops 754974720 | bytes 1572864 | tf_op jit(solution)/shard_map/pallas_call | solution.py:401
  12.7 0.0 collective-permute-done.1.after_ref
  12.8 1.6 %collective-permute-start.2 = (bf16[80,768]{1,0:T(8,128)(2,1)S(1)}, bf16[80,768]{1,0:T(8,128)(2,1)S(1)}, u32[]{:S(2)}, u32[]{:S(2)}) collective-permute-start(bf16[80,768]{1,0:T(8,128)(2,1)S(1)} %pad_maximum_fusion.mine_ref), channel_id=1, source_target_pairs={{0,2},{2,0},{4,6},{6,4},{8,10},{10,8},{12,14},{14,12},{1,3},{3,1},... | collective-permute-start | bytes 368648 | tf_op jit(solution)/shard_map/ppermute | solution.py:375
  14.3 2.1 %shard_map.105 = (bf16[3,512,512]{2,1,0:T(8,128)(2,1)S(1)}, bf16[144,512]{1,0:T(8,128)(2,1)S(1)}, bf16[144,512]{1,0:T(8,128)(2,1)S(1)}, bf16[144,512]{1,0:T(8,12...) custom-call(bf16[512,384]{1,0:T(8,128)(2,1)S(1)} %get-tuple-element.63.q_ref, ...), custom_call_target="tpu_custom_call" | custom-call | flops 754974720 | bytes 1572864 | tf_op jit(solution)/shard_map/pallas_call | solution.py:401
  16.4 1.3 %collective-permute-done.2.came_ref = bf16[80,768]{1,0:T(8,128)(2,1)S(1)} collective-permute-done((bf16[80,768]{1,0:T(8,128)(2,1)S(1)}, bf16[80,768]{1,0:T(8,128)(2,1)S(1)}, u32[]{:S(2)}, u32[]{:S(2)}) %collective-permute-start.2) | collective-permute-done | bytes 122912 | tf_op jit(solution)/shard_map/ppermute | solution.py:375
  17.7 3.1 %shard_map.106 = (bf16[384,512]{1,0:T(8,128)(2,1)S(1)}, f32[8,512]{1,0:T(8,128)S(1)}, f32[8,512]{1,0:T(8,128)S(1)}, bf16[8,96,512]{2,1,0:T(8,128)(2,1)S(1)}, bf1...) custom-call(s32[24,512]{1,0:T(8,128)S(1)} %get-tuple-element.67.table_ref, ...), custom_call_target="tpu_custom_call" | custom-call | flops 943718400 | bytes 1572864 | tf_op jit(solution)/shard_map/pallas_call | solution.py:459
  20.8 1.6 %collective-permute-start.3 = (bf16[80,768]{1,0:T(8,128)(2,1)S(1)}, bf16[80,768]{1,0:T(8,128)(2,1)S(1)}, u32[]{:S(2)}, u32[]{:S(2)}) collective-permute-start(bf16[80,768]{1,0:T(8,128)(2,1)S(1)} %get-tuple-element.98.refs_10_), channel_id=1, source_target_pairs={{0,2},{2,0},{4,6},{6,4},{8,10},{10,8},{12,14},{14,12},{1,3},{3,1},... | collective-permute-start | bytes 368648 | tf_op jit(solution)/shard_map/ppermute | solution.py:375
  22.4 2.6 %shard_map.107 = (bf16[512,384]{1,0:T(8,128)(2,1)}, bf16[144,512]{1,0:T(8,128)(2,1)S(1)}, f32[512,256]{1,0:T(8,128)S(1)}, f32[512,256]{1,0:T(8,128)S(1)}) custom-call(bf16[3,512,512]{2,1,0:T(8,128)(2,1)S(1)} %get-tuple-element.71.refs_0_, bf16[144,512]{1,0:T(8,128)(2,1)S(1)} %get-tuple-element.72.refs_0_.refs_1_, ...), custom_call_target="tpu_custom_call" | custom-call | flops 1509949440 | bytes 1572864 | tf_op jit(solution)/shard_map/pallas_call | solution.py:505
  24.9 0.8 %collective-permute-done.3.refs_9_.refs_10_ = bf16[80,768]{1,0:T(8,128)(2,1)S(1)} collective-permute-done((bf16[80,768]{1,0:T(8,128)(2,1)S(1)}, bf16[80,768]{1,0:T(8,128)(2,1)S(1)}, u32[]{:S(2)}, u32[]{:S(2)}) %collective-permute-start.3) | collective-permute-done | bytes 122912 | tf_op jit(solution)/shard_map/ppermute | solution.py:375
  25.8 2.6 %collective-permute-start.4 = (f32[8,768]{1,0:T(8,128)S(1)}, f32[8,768]{1,0:T(8,128)S(1)}, u32[]{:S(2)}, u32[]{:S(2)}) collective-permute-start(f32[8,768]{1,0:T(8,128)S(1)} %slice.20), channel_id=1, source_target_pairs={{0,8},{2,10},{4,12},{6,14},{8,0},{10,2},{12,4},{14,6},{1,9},{3,11}... | collective-permute-start | bytes 73736 | tf_op jit(solution)/shard_map/ppermute | solution.py:375
  28.3 1.9 %shard_map.108 = (bf16[144,512]{1,0:T(8,128)(2,1)S(1)}, f32[512,256]{1,0:T(8,128)S(1)}, f32[512,256]{1,0:T(8,128)S(1)}) custom-call(bf16[3,512,512]{2,1,0:T(8,128)(2,1)S(1)} %get-tuple-element.106.refs_0_, bf16[144,512]{1,0:T(8,128)(2,1)S(1)} %get-tuple-element.80.refs_1_, bf16[144,512]{1,0:T(8,128)(2,1)S(1)} %get-tuple-element.82.refs_4_.refs_2_, ...), custom_call_target="tpu_custom_call" | custom-call | flops 1509949440 | bytes 1572864 | tf_op jit(solution)/shard_map/pallas_call | solution.py:515
  30.2 0.4 collective-permute-done.4.refs_11_
  30.6 1.6 %collective-permute-start.5 = (f32[4,768]{1,0:T(4,128)S(1)}, f32[4,768]{1,0:T(4,128)S(1)}, u32[]{:S(2)}, u32[]{:S(2)}) collective-permute-start(f32[4,768]{1,0:T(4,128)S(1)} %slice.22), channel_id=1, source_target_pairs={{0,4},{2,6},{4,0},{6,2},{8,12},{10,14},{12,8},{14,10},{1,5},{3,7},... | collective-permute-start | bytes 36872 | tf_op jit(solution)/shard_map/ppermute | solution.py:375
  32.2 2.5 %shard_map.109 = (bf16[512,384]{1,0:T(8,128)(2,1)}, f32[6,512,128]{2,1,0:T(8,128)S(1)}) custom-call(bf16[2,512,512]{2,1,0:T(8,128)(2,1)S(1)} %get-tuple-element.100.refs_0_, bf16[96,512]{1,0:T(8,128)(2,1)S(1)} %get-tuple-element.81.refs_2_.refs_1_, bf16[96,512]{1,0:T(8,128)(2,1)S(1)} %get-tuple-element.83.refs_5_.refs_2_, ...), custom_call_target="tpu_custom_call" | custom-call | flops 1006632960 | bytes 1048576 | tf_op jit(solution)/shard_map/pallas_call | solution.py:523
  34.7 0.0 collective-permute-done.5
  34.7 1.0 %shard_map.110 = (bf16[512,384]{1,0:T(8,128)(2,1)}, bf16[512,384]{1,0:T(8,128)(2,1)}) custom-call(s32[8,384]{1,0:T(8,128)S(1)} %get-tuple-element.102.refs_9_.lanes_ref, f32[6,512,128]{2,1,0:T(8,128)S(1)} %get-tuple-element.118.sum_ref, f32[4,768]{1,0:T(4,128)S(1)} %slice_add_fusion.1.far_ref), custom_call_target="tpu_custom_call" | custom-call | bytes 2359296 | tf_op jit(solution)/shard_map/pallas_call | solution.py:536
  (7 shorter events, 0.1 us)
Async XLA Ops:
  2.8 4.7 %collective-permute-start = (bf16[4,768]{1,0:T(4,128)(2,1)S(1)}, bf16[4,768]{1,0:T(4,128)(2,1)S(1)}, u32[]{:S(2)}, u32[]{:S(2)}) collective-permute-start(bf16[4,768]{1,0:T(4,128)(2,1)S(1)} %get-tuple-element.68.after_ref), channel_id=1, source_target_pairs={{0,4},{2,6},{4,0},{6,2},{8,12},{10,14},{12,8},{14,10},{1,5},{3,7},... | collective-permute-start | bytes 18440 | tf_op jit(solution)/shard_map/ppermute | solution.py:375
  7.5 5.2 %collective-permute-start.1 = (bf16[8,768]{1,0:T(8,128)(2,1)S(1)}, bf16[8,768]{1,0:T(8,128)(2,1)S(1)}, u32[]{:S(2)}, u32[]{:S(2)}) collective-permute-start(bf16[8,768]{1,0:T(8,128)(2,1)S(1)} %pad_maximum_fusion.1), channel_id=1, source_target_pairs={{0,8},{2,10},{4,12},{6,14},{8,0},{10,2},{12,4},{14,6},{1,9},{3,11}... | collective-permute-start | bytes 36872 | tf_op jit(solution)/shard_map/ppermute | solution.py:375
  12.8 4.9 %collective-permute-start.2 = (bf16[80,768]{1,0:T(8,128)(2,1)S(1)}, bf16[80,768]{1,0:T(8,128)(2,1)S(1)}, u32[]{:S(2)}, u32[]{:S(2)}) collective-permute-start(bf16[80,768]{1,0:T(8,128)(2,1)S(1)} %pad_maximum_fusion.mine_ref), channel_id=1, source_target_pairs={{0,2},{2,0},{4,6},{6,4},{8,10},{10,8},{12,14},{14,12},{1,3},{3,1},... | collective-permute-start | bytes 368648 | tf_op jit(solution)/shard_map/ppermute | solution.py:375
  20.8 4.9 %collective-permute-start.3 = (bf16[80,768]{1,0:T(8,128)(2,1)S(1)}, bf16[80,768]{1,0:T(8,128)(2,1)S(1)}, u32[]{:S(2)}, u32[]{:S(2)}) collective-permute-start(bf16[80,768]{1,0:T(8,128)(2,1)S(1)} %get-tuple-element.98.refs_10_), channel_id=1, source_target_pairs={{0,2},{2,0},{4,6},{6,4},{8,10},{10,8},{12,14},{14,12},{1,3},{3,1},... | collective-permute-start | bytes 368648 | tf_op jit(solution)/shard_map/ppermute | solution.py:375
  25.8 4.8 %collective-permute-start.4 = (f32[8,768]{1,0:T(8,128)S(1)}, f32[8,768]{1,0:T(8,128)S(1)}, u32[]{:S(2)}, u32[]{:S(2)}) collective-permute-start(f32[8,768]{1,0:T(8,128)S(1)} %slice.20), channel_id=1, source_target_pairs={{0,8},{2,10},{4,12},{6,14},{8,0},{10,2},{12,4},{14,6},{1,9},{3,11}... | collective-permute-start | bytes 73736 | tf_op jit(solution)/shard_map/ppermute | solution.py:375
  30.6 4.2 %collective-permute-start.5 = (f32[4,768]{1,0:T(4,128)S(1)}, f32[4,768]{1,0:T(4,128)S(1)}, u32[]{:S(2)}, u32[]{:S(2)}) collective-permute-start(f32[4,768]{1,0:T(4,128)S(1)} %slice.22), channel_id=1, source_target_pairs={{0,4},{2,6},{4,0},{6,2},{8,12},{10,14},{12,8},{14,10},{1,5},{3,7},... | collective-permute-start | bytes 36872 | tf_op jit(solution)/shard_map/ppermute | solution.py:375

commit v3 on v2

v3 whole, which is shorter than its diff:
```python
import functools
import math

import jax
import jax.numpy as jnp
from jax import lax
from jax.experimental import pallas as pl
from jax.experimental.pallas import tpu as pltpu
from jax.sharding import PartitionSpec as P

HEAD_WIDTH = 48
CENTER_DILATION = 8
WIDE_DILATION = 128
LANES = 128
STACK = 256
ONES = 16
DEAD = -1e30
SCALE = HEAD_WIDTH**-0.5
EXP2_SCALE = SCALE * math.log2(math.e)
F32 = jnp.float32
BF16 = jnp.bfloat16

VMEM = pl.BlockSpec(memory_space=pltpu.VMEM)
SMEM = pl.BlockSpec(memory_space=pltpu.SMEM)


def nn(a, b):
    return jnp.dot(a, b, preferred_element_type=F32)


def nt(a, b):
    return lax.dot_general(a, b, (((1,), (1,)), ((), ())), preferred_element_type=F32)


def head_rows(h):
    return slice(h * HEAD_WIDTH, (h + 1) * HEAD_WIDTH)


def window(h):
    low = h * HEAD_WIDTH // LANES * LANES
    high = -(-(h + 1) * HEAD_WIDTH // LANES) * LANES
    return low, high


def embed(rows, h):
    low, high = window(h)
    before, after = h * HEAD_WIDTH - low, high - (h + 1) * HEAD_WIDTH
    parts = [rows]
    if before:
        parts.insert(0, jnp.zeros((before, rows.shape[1]), rows.dtype))
    if after:
        parts.append(jnp.zeros((after, rows.shape[1]), rows.dtype))
    return jnp.concatenate(parts, axis=0) if len(parts) > 1 else rows


def head_groups(heads):
    size = -(-heads // 3)
    groups = []
    for first in range(0, heads, size):
        last = min(first + size, heads)
        groups.append((first, last, window(first)[0], window(last - 1)[1]))
    return groups


def lane_shifts(shift_ref, base, heads, width):
    lane = lax.broadcasted_iota(jnp.int32, (1, width), 1)
    row = jnp.zeros((1, width), jnp.int32)
    for h in range(heads):
        inside = (lane >= h * HEAD_WIDTH) & (lane < (h + 1) * HEAD_WIDTH)
        row = jnp.where(inside, shift_ref[base + h], row)
    return row


def head_base(heads):
    return lax.axis_index("hd") * heads


def select_kernel(
    heads, center_any, wide_any, q_any, k_any, v_any, g_any,
    near_ref, far_ref, q_ref, k_ref, v_ref, g_ref, table_ref, lanes_ref,
    center_ref, wide_ref, spread_ref, sems,
):
    rows, width = k_ref.shape
    pairs = (
        (center_any, center_ref), (wide_any, wide_ref),
        (k_any, k_ref), (v_any, v_ref), (q_any, q_ref), (g_any, g_ref),
    )
    copies = [pltpu.make_async_copy(a, b, sems.at[i]) for i, (a, b) in enumerate(pairs)]
    for copy in copies:
        copy.start()
    for copy in copies[:2]:
        copy.wait()
    base = head_base(heads)
    center = lane_shifts(center_ref, base, heads, width)
    wide = lane_shifts(wide_ref, base, heads, width)
    lanes_ref[0:1, :] = center
    lanes_ref[1:2, :] = wide
    for h in range(heads):
        table_ref[h : h + 1, :] = jnp.full((1, rows), center_ref[base + h], jnp.int32)
        table_ref[heads + h : heads + h + 1, :] = jnp.full((1, rows), wide_ref[base + h], jnp.int32)
    near_rows = rows // CENTER_DILATION
    far_rows = rows // WIDE_DILATION
    row = lax.broadcasted_iota(jnp.int32, (far_rows, WIDE_DILATION, LANES), 1)
    for at, ref, copy in ((0, k_ref, copies[2]), (width, v_ref, copies[3])):
        copy.wait()
        for low in range(0, width, LANES):
            lanes = slice(low, low + LANES)
            packed = slice(at + low, at + low + LANES)
            spread = ref[:, lanes].astype(F32)
            spread_ref[at // width * (width // LANES) + low // LANES] = spread
            chosen = jnp.where(row == wide[:, lanes], spread.reshape(row.shape), 0.0)
            far_ref[:, packed] = jnp.sum(chosen, axis=1).astype(BF16)
    for at in (0, width):
        for low in range(0, width, LANES):
            lanes = slice(low, low + LANES)
            packed = slice(at + low, at + low + LANES)
            block = at // width * (width // LANES) + low // LANES
            picked = jnp.zeros((near_rows, LANES), F32)
            for step in range(CENTER_DILATION):
                rows_at = spread_ref[block, pl.ds(step, near_rows, stride=CENTER_DILATION), :]
                picked = jnp.where(center[:, lanes] == step, rows_at, picked)
            near_ref[:, packed] = picked.astype(BF16)
    copies[4].wait()
    copies[5].wait()


def forward_heads(
    group, heads, valid_ref, table_ref, k_ref, qt_ref, vt_ref, p_ref, ot_ref, max_ref, sum_ref
):
    first, last, _, _ = group
    rows = k_ref.shape[0]
    device = lax.axis_index(("seq", "sub"))
    row = lax.broadcasted_iota(jnp.int32, (rows, LANES), 0)
    dead = jnp.where(device * rows + row < valid_ref[0], 0.0, DEAD)
    ones = jnp.ones((ONES, rows), BF16)

    def scores_of(h):
        low, high = window(h)
        is_near = (row & (CENTER_DILATION - 1)) == table_ref[h : h + 1, :LANES]
        is_far = (row & (WIDE_DILATION - 1)) == table_ref[heads + h : heads + h + 1, :LANES]
        once = jnp.where(is_near | is_far, 1.0 / EXP2_SCALE, 0.0)
        bias = dead + jnp.where(is_near & is_far, math.log2(3) / EXP2_SCALE, once)
        scores = nn(k_ref[:, low:high], embed(qt_ref[head_rows(h), :], h)) + widen(bias, rows)
        return scores, jnp.max(scores, axis=0, keepdims=True)

    following = scores_of(first)
    for h in range(first, last):
        scores, top = following
        if h + 1 < last:
            following = scores_of(h + 1)
        at = h - first
        weights = jnp.exp2((scores - top) * EXP2_SCALE).astype(BF16)
        p_ref[at] = weights
        summed = nn(jnp.concatenate([vt_ref[head_rows(h), :], ones], axis=0), weights)
        max_ref[at : at + 1, :] = top
        sum_ref[at : at + 1, :] = summed[HEAD_WIDTH : HEAD_WIDTH + 1]
        ot_ref[head_rows(at), :] = summed[:HEAD_WIDTH]


def first_forward_kernel(
    group, heads, valid_ref, table_ref, k_ref, q_ref, v_ref, g_ref, after_ref,
    qt_ref, gt_ref, kt_ref, vt_ref, *outs,
):
    qt_ref[...] = q_ref[...].T
    vt_ref[...] = v_ref[...].T
    forward_heads(group, heads, valid_ref, table_ref, k_ref, qt_ref, vt_ref, *outs)
    gt_ref[...] = g_ref[...].T
    kt_ref[...] = k_ref[...].T


def forward_kernel(group, heads, valid_ref, table_ref, k_ref, qt_ref, vt_ref, after_ref, *outs):
    forward_heads(group, heads, valid_ref, table_ref, k_ref, qt_ref, vt_ref, *outs)


def stacks(heads, count):
    size = max(1, min(heads, STACK // count))
    found = []
    for first in range(0, heads, size):
        last = min(first + size, heads)
        found.append((first, last, window(first)[0], window(last - 1)[1]))
    return found


def head_lanes(h, low, high):
    lane = low + lax.broadcasted_iota(jnp.int32, (1, high - low), 1)
    return (lane >= h * HEAD_WIDTH) & (lane < (h + 1) * HEAD_WIDTH)


def stacked(rows, stack):
    first, last, low, high = stack
    return jnp.concatenate(
        [rows[:, low:high] * head_lanes(h, low, high).astype(F32).astype(BF16) for h in range(first, last)],
        axis=0,
    )


def unstack(ref, at0, stack, count, value, by, started):
    first, last, low, high = stack
    total = None
    for at, h in enumerate(range(first, last)):
        part = jnp.where(head_lanes(h, low, high), value[at * count : (at + 1) * count], 0.0)
        total = part if total is None else total + part
    total = total * by
    for at in range(low, high, LANES):
        part = total[:, at - low : at - low + LANES]
        if (at0, at) in started:
            ref[:, at0 + at : at0 + at + LANES] += part
        else:
            started.add((at0, at))
            ref[:, at0 + at : at0 + at + LANES] = part


def widen(value, rows):
    return jnp.concatenate([value] * (rows // LANES), axis=1)


def near_forward_kernel(heads, groups, valid_ref, table_ref, near_ref, qt_ref, *refs):
    parts = len(groups)
    o1_refs, max_refs, sum_refs = (refs[i * parts : (i + 1) * parts] for i in range(3))
    after_ref, p_ref, o_ref, old_ref, top_ref, sum_ref = refs[3 * parts :]
    width, rows = qt_ref.shape
    count = near_ref.shape[0]
    device = lax.axis_index(("seq", "sub"))
    row = lax.broadcasted_iota(jnp.int32, (count, LANES), 0)
    room = valid_ref[0] - ((device ^ 1) * rows + row * CENTER_DILATION)
    where = {}
    for part, (first, last, _, _) in enumerate(groups):
        for h in range(first, last):
            where[h] = part, h - first
    for stack in stacks(heads, count):
        first, last, low, high = stack
        scores = nn(stacked(near_ref[:, :width], stack), qt_ref[low:high, :])
        lifts, keeps = [], []
        for at, h in enumerate(range(first, last)):
            part, index = where[h]
            dead = jnp.where(table_ref[h : h + 1, :LANES] < room, 0.0, DEAD)
            here = scores[at * count : (at + 1) * count] + widen(dead, rows)
            old = max_refs[part][index : index + 1, :]
            top = jnp.maximum(jnp.max(here, axis=0, keepdims=True), old)
            lifted = jnp.exp2((here - top) * EXP2_SCALE)
            keep = jnp.exp2((old - top) * EXP2_SCALE)
            old_ref[h : h + 1, :] = old
            top_ref[h : h + 1, :] = top
            sum_ref[h : h + 1, :] = sum_refs[part][index : index + 1, :] * keep + jnp.sum(
                lifted, axis=0, keepdims=True
            )
            keeps.append(keep)
            lifts.append(lifted.astype(BF16))
        weights = jnp.concatenate(lifts, axis=0)
        p_ref[first * count : last * count, :] = weights
        added = nn(stacked(near_ref[:, width:], stack).T, weights)
        for keep, h in zip(keeps, range(first, last)):
            part, index = where[h]
            inside = added[h * HEAD_WIDTH - low : (h + 1) * HEAD_WIDTH - low]
            o_ref[head_rows(h), :] = o1_refs[part][head_rows(index), :] * keep + inside


def wide_kernel(
    heads, far_own, valid_ref, table_ref, far_ref, qt_ref, gt_ref, o_ref, old_ref, near_top_ref, near_sum_ref,
    ot_ref, local_ref, near_ref, delta_ref, ds_ref, keep_ref, send_ref, sum_ref,
):
    width, rows = qt_ref.shape
    count = far_ref.shape[0]
    half = count // 2
    device = lax.axis_index(("seq", "sub"))
    row = lax.broadcasted_iota(jnp.int32, (count, LANES), 0)
    slot = lax.shift_right_arithmetic(row, far_own.bit_length() - 1)
    place = (device ^ slot) * rows + (row & (far_own - 1)) * WIDE_DILATION
    room = jnp.where(slot == 0, -1, valid_ref[0] - place)
    started = set()
    for stack in stacks(heads, count):
        first, last, low, high = stack
        value_rows = stacked(far_ref[:, width:], stack)
        scores = nn(stacked(far_ref[:, :width], stack), qt_ref[low:high, :])
        grad_prob = nn(value_rows, gt_ref[low:high, :])
        probs, factors = [], []
        for at, h in enumerate(range(first, last)):
            one = slice(h, h + 1)
            dead = jnp.where(table_ref[heads + h : heads + h + 1, :LANES] < room, 0.0, DEAD)
            here = scores[at * count : (at + 1) * count] + widen(dead, rows)
            near_top = near_top_ref[one, :]
            top = jnp.maximum(jnp.max(here, axis=0, keepdims=True), near_top)
            lifted = jnp.exp2((here - top) * EXP2_SCALE)
            keep = jnp.exp2((near_top - top) * EXP2_SCALE)
            inverse = 1.0 / (near_sum_ref[one, :] * keep + jnp.sum(lifted, axis=0, keepdims=True))
            probs.append(lifted * inverse)
            factors.append(keep * inverse)
            near_ref[one, :] = keep * inverse
            local_ref[one, :] = jnp.exp2((old_ref[one, :] - top) * EXP2_SCALE) * inverse
        weights = jnp.concatenate([prob.astype(BF16) for prob in probs], axis=0)
        added = nn(value_rows.T, weights)
        dscores = []
        for at, h in enumerate(range(first, last)):
            inside = added[h * HEAD_WIDTH - low : (h + 1) * HEAD_WIDTH - low]
            context = o_ref[head_rows(h), :] * factors[at] + inside
            ot_ref[head_rows(h), :] = context.astype(BF16)
            delta = jnp.sum(gt_ref[head_rows(h), :].astype(F32) * context, axis=0, keepdims=True)
            delta_ref[h : h + 1, :] = delta
            here = grad_prob[at * count : (at + 1) * count]
            dscores.append((probs[at] * (here - delta)).astype(BF16))
        dscore = jnp.concatenate(dscores, axis=0)
        ds_ref[first * count : last * count, :] = dscore
        unstack(sum_ref, 0, stack, count, nt(dscore, qt_ref[low:high, :]), SCALE, started)
        unstack(sum_ref, width, stack, count, nt(weights, gt_ref[low:high, :]), 1.0, started)
    keep_ref[...] = sum_ref[:half, :]
    send_ref[...] = sum_ref[half:, :].astype(send_ref.dtype)


def near_backward_kernel(
    heads, near_ref, far_ref, qt_ref, gt_ref, p_ref, ds_ref, factor_ref, delta_ref, ot_ref, after_ref,
    out_ref, dq_ref, send_ref, sum_ref,
):
    width, rows = qt_ref.shape
    count = near_ref.shape[0]
    started, begun = set(), set()

    def add_dq(stack, product):
        first, last, low, _ = stack
        for h in range(first, last):
            inside = product[h * HEAD_WIDTH - low : (h + 1) * HEAD_WIDTH - low]
            if h in begun:
                dq_ref[head_rows(h), :] += inside
            else:
                begun.add(h)
                dq_ref[head_rows(h), :] = inside

    for stack in stacks(heads, count):
        first, last, low, high = stack
        grad_prob = nn(stacked(near_ref[:, width:], stack), gt_ref[low:high, :])
        weights, dscores = [], []
        for at, h in enumerate(range(first, last)):
            prob = p_ref[h * count : (h + 1) * count, :].astype(F32) * factor_ref[h : h + 1, :]
            here = grad_prob[at * count : (at + 1) * count]
            weights.append(prob.astype(BF16))
            dscores.append((prob * (here - delta_ref[h : h + 1, :])).astype(BF16))
        dscore = jnp.concatenate(dscores, axis=0)
        add_dq(stack, nn(stacked(near_ref[:, :width], stack).T, dscore))
        unstack(sum_ref, 0, stack, count, nt(dscore, qt_ref[low:high, :]), SCALE, started)
        weight = jnp.concatenate(weights, axis=0)
        unstack(sum_ref, width, stack, count, nt(weight, gt_ref[low:high, :]), 1.0, started)
    send_ref[...] = sum_ref[...].astype(send_ref.dtype)
    count = far_ref.shape[0]
    for stack in stacks(heads, count):
        first, last, _, _ = stack
        dscore = ds_ref[first * count : last * count, :]
        add_dq(stack, nn(stacked(far_ref[:, :width], stack).T, dscore))
    out_ref[...] = ot_ref[...].T


def backward_heads(
    group, p_ref, qt_ref, gt_ref, kt_ref, v_ref, dq2_ref, factor_ref, delta_ref, dqt_ref, dk_ref, dv_ref
):
    first, last, _, _ = group
    rows = v_ref.shape[0]
    parts = [slice(at, at + rows // 2) for at in (0, rows // 2)]
    work = [(h, part) for h in range(first, last) for part in parts]

    def product(h, part):
        low, high = window(h)
        return nn(v_ref[part, low:high], embed(gt_ref[head_rows(h), :], h))

    following = product(*work[0])
    for index, (h, part) in enumerate(work):
        grad_prob = following
        if index + 1 < len(work):
            following = product(*work[index + 1])
        at, head = h - first, head_rows(h)
        here = head_rows(at)
        prob = p_ref[at, part, :].astype(F32) * factor_ref[h : h + 1, :]
        dv_ref[here, part] = nt(gt_ref[head, :], prob.astype(BF16))
        dscore = (prob * (grad_prob - delta_ref[h : h + 1, :])).astype(BF16)
        dk_ref[here, part] = nt(qt_ref[head, :], dscore)
        term = nn(kt_ref[head, part], dscore)
        dqt = term + (dq2_ref[head, :] if part is parts[0] else dqt)
        if part is parts[1]:
            dqt_ref[here, :] = (dqt * SCALE).astype(BF16)


def backward_kernel(group, *refs):
    backward_heads(group, *refs[:8], *refs[9:])


def last_backward_kernel(groups, index, *refs):
    others = len(groups) - 1
    lanes_ref, back_ref, after_ref = refs[8:11]
    terms = refs[11 : 11 + 3 * others]
    dq_ref, sum_ref, dqt_ref, dk_ref, dv_ref, turned_ref, wide_ref = refs[11 + 3 * others :]
    backward_heads(groups[index], *refs[:8], dqt_ref, dk_ref, dv_ref)

    def all_groups(at, mine):
        found = list(terms[at * others : (at + 1) * others])
        found.insert(index, mine)
        return found

    rows, width = dq_ref.shape
    near_rows = rows // CENTER_DILATION
    for (first, last, _, _), ref in zip(groups, all_groups(0, dqt_ref)):
        turned_ref[first * HEAD_WIDTH : last * HEAD_WIDTH, :] = ref[...]
    dq_ref[...] = turned_ref[...].T
    for at, parts, by in ((0, all_groups(1, dk_ref), SCALE), (width, all_groups(2, dv_ref), 1.0)):
        for (first, last, _, _), ref in zip(groups, parts):
            wide_ref[first * HEAD_WIDTH : last * HEAD_WIDTH, :] = ref[...] * by
        for low in range(0, width, LANES):
            block = (at + low) // LANES
            sum_ref[block] = wide_ref[low : low + LANES, :].T
            near = back_ref[:, at + low : at + low + LANES].astype(F32)
            center = lanes_ref[0:1, low : low + LANES]
            for step in range(CENTER_DILATION):
                strided = pl.ds(step, near_rows, stride=CENTER_DILATION)
                sum_ref[block, strided, :] += jnp.where(center == step, near, 0.0)


def combine_kernel(lanes_ref, sum_ref, far_ref, outk_ref, outv_ref):
    rows, width = outk_ref.shape
    far_rows = far_ref.shape[0]
    row = lax.broadcasted_iota(jnp.int32, (WIDE_DILATION, LANES), 0)
    for at, out in ((0, outk_ref), (width, outv_ref)):
        for low in range(0, width, LANES):
            block = (at + low) // LANES
            mask = row == lanes_ref[1:2, low : low + LANES]
            for index in range(far_rows):
                part = slice(index * WIDE_DILATION, (index + 1) * WIDE_DILATION)
                far = far_ref[index : index + 1, at + low : at + low + LANES]
                value = sum_ref[block, part, :] + jnp.where(mask, far, 0.0)
                out[part, low : low + LANES] = value.astype(BF16)


ANY = pl.BlockSpec(memory_space=pl.ANY)
HBM = pl.BlockSpec(memory_space=pltpu.HBM)


def call(body, outs, ins, scratch=(), *, flops=0, moved=0):
    return pl.pallas_call(
        body,
        out_shape=[jax.ShapeDtypeStruct(s, d) for s, d in outs],
        in_specs=ins,
        out_specs=[VMEM] * len(outs),
        scratch_shapes=list(scratch),
        compiler_params=pltpu.CompilerParams(vmem_limit_bytes=24 * 2**20),
        cost_estimate=pl.CostEstimate(flops=flops, bytes_accessed=moved, transcendentals=0),
    )


def local(queries, keys, values, grad_out, center_shift, wide_shift, valid_count):
    rows, width = queries.shape
    heads = width // HEAD_WIDTH
    groups = head_groups(heads)
    near_rows, far_own = rows // CENTER_DILATION, rows // WIDE_DILATION
    axes = ("seq", "sub")
    devices = lax.axis_size(axes)
    far_rows = far_own * devices
    blocks = 2 * width // LANES
    steps = [2**bit for bit in range(devices.bit_length() - 1)]

    def swap(value, apart):
        return lax.ppermute(value, axes, [(at, at ^ apart) for at in range(devices)])

    near, far, q, k, v, g, table, lanes = call(
        functools.partial(select_kernel, heads),
        [((near_rows, 2 * width), BF16), ((far_own, 2 * width), BF16)]
        + [((rows, width), BF16)] * 4
        + [((2 * heads, rows), jnp.int32), ((8, width), jnp.int32)],
        [HBM] * 6,
        [
            pltpu.SMEM(center_shift.shape, jnp.int32),
            pltpu.SMEM(wide_shift.shape, jnp.int32),
            pltpu.VMEM((blocks, rows, LANES), F32),
            pltpu.SemaphoreType.DMA((6,)),
        ],
        moved=16 * rows * width,
    )(
        *(
            pltpu.with_memory_space_constraint(value, pltpu.HBM)
            for value in (center_shift, wide_shift, queries, keys, values, grad_out)
        )
    )

    valid, far = lax.optimization_barrier((valid_count, far))

    def cost(heads_done, keys_done, products):
        done = heads_done * keys_done * rows
        return dict(flops=2 * HEAD_WIDTH * done * products * 5, moved=2 * done)

    turned = {}
    fronts = {}

    def front(index, after):
        first, last, _, _ = groups[index]
        size, tall = last - first, (last - first) * HEAD_WIDTH
        outs = [((size, rows, rows), BF16), ((tall, rows), F32), ((size, rows), F32), ((size, rows), F32)]
        if not turned:
            *flipped, p, o, top, total = call(
                functools.partial(first_forward_kernel, groups[index], heads),
                [((width, rows), BF16)] * 4 + outs,
                [SMEM] + [VMEM] * 5 + [ANY],
                **cost(size, rows, 2),
            )(valid, table, k, q, v, g, after)
            turned.update(zip(("qt", "gt", "kt", "vt"), flipped))
        else:
            p, o, top, total = call(
                functools.partial(forward_kernel, groups[index], heads),
                outs,
                [SMEM] + [VMEM] * 4 + [ANY],
                **cost(size, rows, 2),
            )(valid, table, k, turned["qt"], turned["vt"], after)
        fronts[index] = [p, o, top, total]

    def tie(arrived, holder, key):
        arrived, held = lax.optimization_barrier((arrived, holder[key][-1]))
        holder[key] = [*holder[key][:-1], held]
        return arrived

    last = len(groups) - 1
    order = [last, *range(last)]
    after = far
    for at, step in enumerate(steps):
        arrived = swap(far, step)
        if at == 0:
            near_came = swap(near, 1)
        if at < len(order):
            front(order[at], after)
        if at == len(order) - 1:
            p, o, top, total = zip(*(fronts[index] for index in range(len(groups))))
            fronts["near"] = call(
                functools.partial(near_forward_kernel, heads, groups),
                [((heads * near_rows, rows), BF16), ((width, rows), F32)] + [((heads, rows), F32)] * 3,
                [SMEM] + [VMEM] * (3 + 3 * len(groups)) + [ANY],
                **cost(heads, near_rows, 2),
            )(valid, table, near_came, turned["qt"], *o, *top, *total, after)
            arrived = tie(arrived, fronts, "near")
        elif at < len(order):
            arrived = tie(arrived, fronts, order[at])
        after = arrived
        far = jnp.concatenate([far, arrived], axis=0)
    near_p, o, old, near_top, near_sum = fronts["near"]
    qt, gt, kt = (turned[name] for name in ("qt", "gt", "kt"))

    ot, local_factor, near_factor, delta, ds, terms, send = call(
        functools.partial(wide_kernel, heads, far_own),
        [((width, rows), BF16)]
        + [((heads, rows), F32)] * 3
        + [((heads * far_rows, rows), BF16)]
        + [((far_rows // 2, 2 * width), F32)] * 2,
        [SMEM] + [VMEM] * 8,
        [pltpu.VMEM((far_rows, 2 * width), F32)],
        **cost(heads, far_rows, 5),
    )(valid, table, far, qt, gt, o, old, near_top, near_sum)

    backs = {}

    def back(index, after):
        first, end, _, _ = groups[index]
        size, tall = end - first, (end - first) * HEAD_WIDTH
        partial = [((tall, rows), BF16), ((tall, rows), F32), ((tall, rows), F32)]
        given = (p[index], qt, gt, kt, v, backs["near"][1], local_factor, delta)
        if len(backs) < len(groups):
            backs[index] = call(
                functools.partial(backward_kernel, groups[index]),
                partial,
                [VMEM] * 8 + [ANY],
                **cost(size, rows, 4),
            )(*given, after)
            return
        others = [backs[other] for other in range(len(groups)) if other != index]
        backs[index] = call(
            functools.partial(last_backward_kernel, groups, index),
            [((rows, width), BF16), ((blocks, rows, LANES), F32)],
            [VMEM] * 10 + [ANY] + [VMEM] * (3 * len(others)),
            [pltpu.VMEM(shape, dtype) for shape, dtype in partial]
            + [pltpu.VMEM((width, rows), BF16), pltpu.VMEM((width, rows), F32)],
            **cost(size, rows, 4),
        )(*given, lanes, near_back, after, *[terms[i] for i in range(3) for terms in others])

    after = send
    for at, step in enumerate(reversed(steps)):
        if at:
            half = terms.shape[0] // 2
            send, terms = terms[half:], terms[:half]
        arrived = swap(send, step)
        if at == 0:
            backs["near"] = call(
                functools.partial(near_backward_kernel, heads),
                [((rows, width), BF16), ((width, rows), F32), ((near_rows, 2 * width), BF16)],
                [VMEM] * 9 + [ANY],
                [pltpu.VMEM((near_rows, 2 * width), F32)],
                **cost(heads, near_rows, 4),
            )(near_came, far, qt, gt, near_p, ds, near_factor, delta, ot, after)
        if at == 1:
            near_back = swap(backs["near"][2], 1)
        if at < len(order):
            back(order[at], after)
            arrived = tie(arrived, backs, order[at])
        after = arrived
        terms = terms + arrived.astype(F32)

    dq, sums = backs[order[-1]]
    key_gradient, value_gradient = call(
        combine_kernel,
        [((rows, width), BF16)] * 2,
        [VMEM] * 3,
        moved=12 * rows * width,
    )(lanes, sums, terms)
    return backs["near"][0], dq, key_gradient, value_gradient


def solution(mesh):
    split = P(("grp", "seq", "sub"), "hd")
    return jax.shard_map(
        local,
        mesh=mesh,
        in_specs=(split, split, split, split, P(), P(), P("grp")),
        out_specs=(split, split, split, split),
        check_vma=False,
    )
```

time: 35.9 us -> 33.2 us (0.925)
  Pallas kernels: 18.1 us -> 15.4 us
  starting transfers between devices: 13.5 us -> 14.6 us
  waiting for transfers between devices: 2.68 us -> 1.61 us
    pallas_call x7 -> x9, Pallas kernels: 15.6 us -> 12.9 us  [the longest x2 2.77 us: front(): call(functools.partial(forward_kernel, groups[index], heads), outs, [SMEM...]
    ppermute x6 -> x8, starting transfers between devices: 13.5 us -> 14.6 us  [swap(): lax.ppermute(value, axes, [(at, at ^ apart) for at in range(devices)])]
    ppermute x6 -> x8, waiting for transfers between devices: 2.68 us -> 1.61 us  [swap(): lax.ppermute(value, axes, [(at, at ^ apart) for at in range(devices)])]
  transfers between devices with their start and end apart: 6 -> 8, of which waited for: 4 -> 3; matrix products, arithmetic and copies ran while one was open for 0% -> 0% of each run, Pallas kernels for 35% -> 35%
where the time goes in v3:
time: 33.2 us; the launch traced here: 33.1 us
  Pallas kernels  15.4 us (46%)
  starting transfers between devices  14.6 us (44%)
  waiting for transfers between devices  1.61 us (5%)
  between operations  1.41 us (4%)
    ppermute x8, starting transfers between devices, swap(): lax.ppermute(value, axes, [(at, at ^ apart) for at in range(devices)])  14.6 us
    pallas_call x2, Pallas kernels, front(): call(functools.partial(forward_kernel, groups[index], heads), outs, [SMEM...  2.77 us
    pallas_call x1, Pallas kernels, back(): call(functools.partial(last_backward_kernel, groups, index), [((rows, wid...  2.55 us
    pallas_call x2, Pallas kernels, back(): call(functools.partial(backward_kernel, groups[index]), partial, [VMEM] *...  2.46 us
    pallas_call x1, Pallas kernels, local(): call(functools.partial(near_backward_kernel, heads), [((rows, width), BF1...  1.84 us
    ppermute x8, waiting for transfers between devices, swap(): lax.ppermute(value, axes, [(at, at ^ apart) for at in range(devices)])  1.61 us
    pallas_call x1, Pallas kernels, local(): call(functools.partial(select_kernel, heads), [((near_rows, 2 * width), B...  1.53 us
    pallas_call x1, Pallas kernels, local(): call(functools.partial(wide_kernel, heads, far_own), [((width, rows), BF1...  1.22 us
  transfers between devices with their start and end apart: 8, of which 3 were waited for; matrix products, arithmetic and copies ran while one was open for 0% of the time, Pallas kernels for 35%

profile of v3, /device:TPU:0, one launch (start us, length us, event | category | flops | bytes accessed | tf_op | source)
XLA Modules:
  0.0 33.1 jit_solution(17325795271971479574)
XLA Ops:
  0.6 1.5 %shard_map.102 = (bf16[64,768]{1,0:T(8,128)(2,1)S(1)}, bf16[4,768]{1,0:T(4,128)(2,1)S(1)}, bf16[512,384]{1,0:T(8,128)(2,1)S(1)}, bf16[512,384]{1,0:T(8,128)(2,1)...) custom-call(s32[16]{0:T(128)} %center_any.1, ...), custom_call_target="tpu_custom_call" | custom-call | bytes 3145728 | tf_op jit(solution)/shard_map/pallas_call | solution.py:458
  2.2 3.0 %collective-permute-start.1 = (bf16[4,768]{1,0:T(4,128)(2,1)S(1)}, bf16[4,768]{1,0:T(4,128)(2,1)S(1)}, u32[]{:S(2)}, u32[]{:S(2)}) collective-permute-start(bf16[4,768]{1,0:T(4,128)(2,1)S(1)} %get-tuple-element.69.after_ref), channel_id=1, source_target_pairs={{0,2},{2,0},{4,6},{6,4},{8,10},{10,8},{12,14},{14,12},{1,3},{3,1},... | collective-permute-start | bytes 18440 | tf_op jit(solution)/shard_map/ppermute | solution.py:456
  5.2 0.1 collective-permute-start
  5.9 1.1 %shard_map.103 = (bf16[384,512]{1,0:T(8,128)(2,1)S(1)}, bf16[384,512]{1,0:T(8,128)(2,1)S(1)}, bf16[384,512]{1,0:T(8,128)(2,1)S(1)}, bf16[384,512]{1,0:T(8,128)(2...) custom-call(s32[1]{0:T(128)S(6)} %copy.11.valid_ref, ...), custom_call_target="tpu_custom_call" | custom-call | flops 503316480 | bytes 1048576 | tf_op jit(solution)/shard_map/pallas_call | solution.py:492
  7.0 0.0 collective-permute-done.1.after_ref
  7.1 2.1 %collective-permute-start.2 = (bf16[8,768]{1,0:T(8,128)(2,1)S(1)}, bf16[8,768]{1,0:T(8,128)(2,1)S(1)}, u32[]{:S(2)}, u32[]{:S(2)}) collective-permute-start(bf16[8,768]{1,0:T(8,128)(2,1)S(1)} %pad_maximum_fusion.2), channel_id=1, source_target_pairs={{0,4},{2,6},{4,0},{6,2},{8,12},{10,14},{12,8},{14,10},{1,5},{3,7},... | collective-permute-start | bytes 36872 | tf_op jit(solution)/shard_map/ppermute | solution.py:456
  9.2 1.4 %shard_map.104 = (bf16[3,512,512]{2,1,0:T(8,128)(2,1)S(1)}, f32[144,512]{1,0:T(8,128)S(1)}, f32[3,512]{1,0:T(4,128)S(1)}, f32[3,512]{1,0:T(4,128)S(1)}) custom-call(s32[1]{0:T(128)S(6)} %copy.11.valid_ref, s32[16,512]{1,0:T(8,128)S(1)} %get-tuple-element.71.table_ref, bf16[512,384]{1,0:T(8,128)(2,1)S(1)} %get-tuple-element.72.k_ref, ...), custom_call_target="tpu_custom_call" | custom-call | flops 754974720 | bytes 1572864 | tf_op jit(solution)/shard_map/pallas_call | solution.py:500
  10.6 0.3 collective-permute-done.2.after_ref.refs_9_
  10.9 3.1 %collective-permute-start.3 = (bf16[16,768]{1,0:T(8,128)(2,1)S(1)}, bf16[16,768]{1,0:T(8,128)(2,1)S(1)}, u32[]{:S(2)}, u32[]{:S(2)}) collective-permute-start(bf16[16,768]{1,0:T(8,128)(2,1)S(1)} %pad_maximum_fusion.1), channel_id=1, source_target_pairs={{0,8},{2,10},{4,12},{6,14},{8,0},{10,2},{12,4},{14,6},{1,9},{3,11}... | collective-permute-start | bytes 73736 | tf_op jit(solution)/shard_map/ppermute | solution.py:456
  14.0 1.4 %shard_map.105 = (bf16[3,512,512]{2,1,0:T(8,128)(2,1)S(1)}, f32[144,512]{1,0:T(8,128)S(1)}, f32[3,512]{1,0:T(4,128)S(1)}, f32[3,512]{1,0:T(4,128)S(1)}) custom-call(s32[1]{0:T(128)S(6)} %copy.11.valid_ref, s32[16,512]{1,0:T(8,128)S(1)} %get-tuple-element.71.table_ref, bf16[512,384]{1,0:T(8,128)(2,1)S(1)} %get-tuple-element.72.k_ref, ...), custom_call_target="tpu_custom_call" | custom-call | flops 754974720 | bytes 1572864 | tf_op jit(solution)/shard_map/pallas_call | solution.py:500
  15.4 0.0 collective-permute-done.near_ref
  15.4 0.9 %shard_map.106 = (bf16[512,512]{1,0:T(8,128)(2,1)S(1)}, f32[384,512]{1,0:T(8,128)S(1)}, f32[8,512]{1,0:T(8,128)S(1)}, f32[8,512]{1,0:T(8,128)S(1)}, f32[8,512]{1,0:T(8,128)S(1)}) custom-call(s32[1]{0:T(128)S(6)} %copy.11.valid_ref, s32[16,512]{1,0:T(8,128)S(1)} %get-tuple-element.71.table_ref, bf16[64,768]{1,0:T(8,128)(2,1)S(1)} %collective-permute-done.near_ref, ...), custom_call_target="tpu_custom_call" | custom-call | flops 251658240 | bytes 524288 | tf_op jit(solution)/shard_map/pallas_call | solution.py:524
  16.3 0.0 collective-permute-done.3
  16.4 1.2 %shard_map.107 = (bf16[384,512]{1,0:T(8,128)(2,1)S(1)}, f32[8,512]{1,0:T(8,128)S(1)}, f32[8,512]{1,0:T(8,128)S(1)}, f32[8,512]{1,0:T(8,128)S(1)}, bf16[256,512]{...) custom-call(s32[1]{0:T(128)S(6)} %copy.11.valid_ref, s32[16,512]{1,0:T(8,128)S(1)} %get-tuple-element.71.table_ref, ...), custom_call_target="tpu_custom_call" | custom-call | flops 314572800 | bytes 262144 | tf_op jit(solution)/shard_map/pallas_call | solution.py:538
  17.6 2.4 %collective-permute-start.5 = (f32[16,768]{1,0:T(8,128)S(1)}, f32[16,768]{1,0:T(8,128)S(1)}, u32[]{:S(2)}, u32[]{:S(2)}) collective-permute-start(f32[16,768]{1,0:T(8,128)S(1)} %get-tuple-element.103.after_ref.refs_8_), channel_id=1, source_target_pairs={{0,8},{2,10},{4,12},{6,14},{8,0},{10,2},{12,4},{14,6},{1,9},{3,11}... | collective-permute-start | bytes 147464 | tf_op jit(solution)/shard_map/ppermute | solution.py:456
  20.0 1.8 %shard_map.108 = (bf16[512,384]{1,0:T(8,128)(2,1)}, f32[384,512]{1,0:T(8,128)S(1)}, bf16[64,768]{1,0:T(8,128)(2,1)S(1)}) custom-call(bf16[64,768]{1,0:T(8,128)(2,1)S(1)} %collective-permute-done.near_ref, bf16[32,768]{1,0:T(8,128)(2,1)S(1)} %pad_maximum_fusion.far_ref, bf16[384,512]{1,0:T(8,128)(2,1)S(1)} %get-tuple-element.78.qt_ref.refs_1_, ...), custom_call_target="tpu_custom_call" | custom-call | flops 503316480 | bytes 524288 | tf_op jit(solution)/shard_map/pallas_call | solution.py:581
  21.9 1.5 %collective-permute-start.4 = (bf16[64,768]{1,0:T(8,128)(2,1)S(1)}, bf16[64,768]{1,0:T(8,128)(2,1)S(1)}, u32[]{:S(2)}, u32[]{:S(2)}) collective-permute-start(bf16[64,768]{1,0:T(8,128)(2,1)S(1)} %get-tuple-element.110), channel_id=1, source_target_pairs={{0,2},{2,0},{4,6},{6,4},{8,10},{10,8},{12,14},{14,12},{1,3},{3,1},... | collective-permute-start | bytes 294920 | tf_op jit(solution)/shard_map/ppermute | solution.py:456
  23.4 1.0 %shard_map.109 = (bf16[96,512]{1,0:T(8,128)(2,1)S(1)}, f32[96,512]{1,0:T(8,128)S(1)}, f32[96,512]{1,0:T(8,128)S(1)}) custom-call(bf16[2,512,512]{2,1,0:T(8,128)(2,1)S(1)} %get-tuple-element.112.refs_0_, bf16[384,512]{1,0:T(8,128)(2,1)S(1)} %get-tuple-element.78.qt_ref.refs_1_, bf16[384,512]{1,0:T(8,128)(2,1)S(1)} %get-tuple-element.93.gt_ref.refs_2_, ...), custom_call_target="tpu_custom_call" | custom-call | flops 1006632960 | bytes 1048576 | tf_op jit(solution)/shard_map/pallas_call | solution.py:557
  24.4 0.0 collective-permute-done.5.refs_8_
  24.4 1.8 %collective-permute-start.6 = (f32[8,768]{1,0:T(8,128)S(1)}, f32[8,768]{1,0:T(8,128)S(1)}, u32[]{:S(2)}, u32[]{:S(2)}) collective-permute-start(f32[8,768]{1,0:T(8,128)S(1)} %slice.16), channel_id=1, source_target_pairs={{0,4},{2,6},{4,0},{6,2},{8,12},{10,14},{12,8},{14,10},{1,5},{3,7},... | collective-permute-start | bytes 73736 | tf_op jit(solution)/shard_map/ppermute | solution.py:456
  26.2 1.4 %shard_map.110 = (bf16[144,512]{1,0:T(8,128)(2,1)S(1)}, f32[144,512]{1,0:T(8,128)S(1)}, f32[144,512]{1,0:T(8,128)S(1)}) custom-call(bf16[3,512,512]{2,1,0:T(8,128)(2,1)S(1)} %get-tuple-element.115.refs_0_, bf16[384,512]{1,0:T(8,128)(2,1)S(1)} %get-tuple-element.78.qt_ref.refs_1_, bf16[384,512]{1,0:T(8,128)(2,1)S(1)} %get-tuple-element.93.gt_ref.refs_2_, ...), custom_call_target="tpu_custom_call" | custom-call | flops 1509949440 | bytes 1572864 | tf_op jit(solution)/shard_map/pallas_call | solution.py:557
  27.6 0.7 %collective-permute-done.6.refs_10_ = f32[8,768]{1,0:T(8,128)S(1)} collective-permute-done((f32[8,768]{1,0:T(8,128)S(1)}, f32[8,768]{1,0:T(8,128)S(1)}, u32[]{:S(2)}, u32[]{:S(2)}) %collective-permute-start.6) | collective-permute-done | bytes 24608 | tf_op jit(solution)/shard_map/ppermute | solution.py:456
  28.3 0.6 %collective-permute-start.7 = (f32[4,768]{1,0:T(4,128)S(1)}, f32[4,768]{1,0:T(4,128)S(1)}, u32[]{:S(2)}, u32[]{:S(2)}) collective-permute-start(f32[4,768]{1,0:T(4,128)S(1)} %slice.18), channel_id=1, source_target_pairs={{0,2},{2,0},{4,6},{6,4},{8,10},{10,8},{12,14},{14,12},{1,3},{3,1},... | collective-permute-start | bytes 36872 | tf_op jit(solution)/shard_map/ppermute | solution.py:456
  28.9 0.0 collective-permute-done.4.refs_9_
  28.9 2.5 %shard_map.111 = (bf16[512,384]{1,0:T(8,128)(2,1)}, f32[6,512,128]{2,1,0:T(8,128)S(1)}) custom-call(bf16[3,512,512]{2,1,0:T(8,128)(2,1)S(1)} %get-tuple-element.105.refs_0_, bf16[384,512]{1,0:T(8,128)(2,1)S(1)} %get-tuple-element.78.qt_ref.refs_1_, bf16[384,512]{1,0:T(8,128)(2,1)S(1)} %get-tuple-element.93.gt_ref.refs_2_, ...), custom_call_target="tpu_custom_call" | custom-call | flops 1509949440 | bytes 1572864 | tf_op jit(solution)/shard_map/pallas_call | solution.py:565
  31.5 0.6 %collective-permute-done.7 = f32[4,768]{1,0:T(4,128)S(1)} collective-permute-done((f32[4,768]{1,0:T(4,128)S(1)}, f32[4,768]{1,0:T(4,128)S(1)}, u32[]{:S(2)}, u32[]{:S(2)}) %collective-permute-start.7) | collective-permute-done | bytes 12320 | tf_op jit(solution)/shard_map/ppermute | solution.py:456
  32.1 1.0 %shard_map.112 = (bf16[512,384]{1,0:T(8,128)(2,1)}, bf16[512,384]{1,0:T(8,128)(2,1)}) custom-call(s32[8,384]{1,0:T(8,128)S(1)} %get-tuple-element.109.refs_8_.lanes_ref, f32[6,512,128]{2,1,0:T(8,128)S(1)} %get-tuple-element.126.sum_ref, f32[4,768]{1,0:T(4,128)S(1)} %slice_add_fusion.1.far_ref), custom_call_target="tpu_custom_call" | custom-call | bytes 2359296 | tf_op jit(solution)/shard_map/pallas_call | solution.py:597
  (8 shorter events, 0.1 us)
Async XLA Ops:
  2.2 4.9 %collective-permute-start.1 = (bf16[4,768]{1,0:T(4,128)(2,1)S(1)}, bf16[4,768]{1,0:T(4,128)(2,1)S(1)}, u32[]{:S(2)}, u32[]{:S(2)}) collective-permute-start(bf16[4,768]{1,0:T(4,128)(2,1)S(1)} %get-tuple-element.69.after_ref), channel_id=1, source_target_pairs={{0,2},{2,0},{4,6},{6,4},{8,10},{10,8},{12,14},{14,12},{1,3},{3,1},... | collective-permute-start | bytes 18440 | tf_op jit(solution)/shard_map/ppermute | solution.py:456
  5.2 10.2 %collective-permute-start = (bf16[64,768]{1,0:T(8,128)(2,1)S(1)}, bf16[64,768]{1,0:T(8,128)(2,1)S(1)}, u32[]{:S(2)}, u32[]{:S(2)}) collective-permute-start(bf16[64,768]{1,0:T(8,128)(2,1)S(1)} %get-tuple-element.67), channel_id=1, source_target_pairs={{0,2},{2,0},{4,6},{6,4},{8,10},{10,8},{12,14},{14,12},{1,3},{3,1},... | collective-permute-start | bytes 294920 | tf_op jit(solution)/shard_map/ppermute | solution.py:456
  7.1 3.8 %collective-permute-start.2 = (bf16[8,768]{1,0:T(8,128)(2,1)S(1)}, bf16[8,768]{1,0:T(8,128)(2,1)S(1)}, u32[]{:S(2)}, u32[]{:S(2)}) collective-permute-start(bf16[8,768]{1,0:T(8,128)(2,1)S(1)} %pad_maximum_fusion.2), channel_id=1, source_target_pairs={{0,4},{2,6},{4,0},{6,2},{8,12},{10,14},{12,8},{14,10},{1,5},{3,7},... | collective-permute-start | bytes 36872 | tf_op jit(solution)/shard_map/ppermute | solution.py:456
  10.9 5.5 %collective-permute-start.3 = (bf16[16,768]{1,0:T(8,128)(2,1)S(1)}, bf16[16,768]{1,0:T(8,128)(2,1)S(1)}, u32[]{:S(2)}, u32[]{:S(2)}) collective-permute-start(bf16[16,768]{1,0:T(8,128)(2,1)S(1)} %pad_maximum_fusion.1), channel_id=1, source_target_pairs={{0,8},{2,10},{4,12},{6,14},{8,0},{10,2},{12,4},{14,6},{1,9},{3,11}... | collective-permute-start | bytes 73736 | tf_op jit(solution)/shard_map/ppermute | solution.py:456
  17.6 6.8 %collective-permute-start.5 = (f32[16,768]{1,0:T(8,128)S(1)}, f32[16,768]{1,0:T(8,128)S(1)}, u32[]{:S(2)}, u32[]{:S(2)}) collective-permute-start(f32[16,768]{1,0:T(8,128)S(1)} %get-tuple-element.103.after_ref.refs_8_), channel_id=1, source_target_pairs={{0,8},{2,10},{4,12},{6,14},{8,0},{10,2},{12,4},{14,6},{1,9},{3,11}... | collective-permute-start | bytes 147464 | tf_op jit(solution)/shard_map/ppermute | solution.py:456
  21.9 7.1 %collective-permute-start.4 = (bf16[64,768]{1,0:T(8,128)(2,1)S(1)}, bf16[64,768]{1,0:T(8,128)(2,1)S(1)}, u32[]{:S(2)}, u32[]{:S(2)}) collective-permute-start(bf16[64,768]{1,0:T(8,128)(2,1)S(1)} %get-tuple-element.110), channel_id=1, source_target_pairs={{0,2},{2,0},{4,6},{6,4},{8,10},{10,8},{12,14},{14,12},{1,3},{3,1},... | collective-permute-start | bytes 294920 | tf_op jit(solution)/shard_map/ppermute | solution.py:456
  24.4 3.9 %collective-permute-start.6 = (f32[8,768]{1,0:T(8,128)S(1)}, f32[8,768]{1,0:T(8,128)S(1)}, u32[]{:S(2)}, u32[]{:S(2)}) collective-permute-start(f32[8,768]{1,0:T(8,128)S(1)} %slice.16), channel_id=1, source_target_pairs={{0,4},{2,6},{4,0},{6,2},{8,12},{10,14},{12,8},{14,10},{1,5},{3,7},... | collective-permute-start | bytes 73736 | tf_op jit(solution)/shard_map/ppermute | solution.py:456
  28.3 3.8 %collective-permute-start.7 = (f32[4,768]{1,0:T(4,128)S(1)}, f32[4,768]{1,0:T(4,128)S(1)}, u32[]{:S(2)}, u32[]{:S(2)}) collective-permute-start(f32[4,768]{1,0:T(4,128)S(1)} %slice.18), channel_id=1, source_target_pairs={{0,2},{2,0},{4,6},{6,4},{8,10},{10,8},{12,14},{14,12},{1,3},{3,1},... | collective-permute-start | bytes 36872 | tf_op jit(solution)/shard_map/ppermute | solution.py:456

commit v4 on v3

--- a/solution.py
+++ b/solution.py
@@ -14,6 +14,7 @@
 LANES = 128
 STACK = 256
 ONES = 16
+OUT_AT = 2
 DEAD = -1e30
 SCALE = HEAD_WIDTH**-0.5
 EXP2_SCALE = SCALE * math.log2(math.e)
@@ -54,12 +55,8 @@
 
 
 def head_groups(heads):
-    size = -(-heads // 3)
-    groups = []
-    for first in range(0, heads, size):
-        last = min(first + size, heads)
-        groups.append((first, last, window(first)[0], window(last - 1)[1]))
-    return groups
+    edge = max(1, heads // 4)
+    return [(0, edge), (edge, heads - edge), (heads - edge, heads)]
 
 
 def lane_shifts(shift_ref, base, heads, width):
@@ -77,8 +74,8 @@
 
 def select_kernel(
     heads, center_any, wide_any, q_any, k_any, v_any, g_any,
-    near_ref, far_ref, q_ref, k_ref, v_ref, g_ref, table_ref, lanes_ref,
-    center_ref, wide_ref, spread_ref, sems,
+    far_ref, q_ref, k_ref, v_ref, g_ref, table_ref, lanes_ref,
+    center_ref, wide_ref, sems,
 ):
     rows, width = k_ref.shape
     pairs = (
@@ -98,7 +95,6 @@
     for h in range(heads):
         table_ref[h : h + 1, :] = jnp.full((1, rows), center_ref[base + h], jnp.int32)
         table_ref[heads + h : heads + h + 1, :] = jnp.full((1, rows), wide_ref[base + h], jnp.int32)
-    near_rows = rows // CENTER_DILATION
     far_rows = rows // WIDE_DILATION
     row = lax.broadcasted_iota(jnp.int32, (far_rows, WIDE_DILATION, LANES), 1)
     for at, ref, copy in ((0, k_ref, copies[2]), (width, v_ref, copies[3])):
@@ -107,19 +103,8 @@
             lanes = slice(low, low + LANES)
             packed = slice(at + low, at + low + LANES)
             spread = ref[:, lanes].astype(F32)
-            spread_ref[at // width * (width // LANES) + low // LANES] = spread
             chosen = jnp.where(row == wide[:, lanes], spread.reshape(row.shape), 0.0)
             far_ref[:, packed] = jnp.sum(chosen, axis=1).astype(BF16)
-    for at in (0, width):
-        for low in range(0, width, LANES):
-            lanes = slice(low, low + LANES)
-            packed = slice(at + low, at + low + LANES)
-            block = at // width * (width // LANES) + low // LANES
-            picked = jnp.zeros((near_rows, LANES), F32)
-            for step in range(CENTER_DILATION):
-                rows_at = spread_ref[block, pl.ds(step, near_rows, stride=CENTER_DILATION), :]
-                picked = jnp.where(center[:, lanes] == step, rows_at, picked)
-            near_ref[:, packed] = picked.astype(BF16)
     copies[4].wait()
     copies[5].wait()
 
@@ -127,7 +112,7 @@
 def forward_heads(
     group, heads, valid_ref, table_ref, k_ref, qt_ref, vt_ref, p_ref, ot_ref, max_ref, sum_ref
 ):
-    first, last, _, _ = group
+    first, last = group
     rows = k_ref.shape[0]
     device = lax.axis_index(("seq", "sub"))
     row = lax.broadcasted_iota(jnp.int32, (rows, LANES), 0)
@@ -157,10 +142,28 @@
         ot_ref[head_rows(at), :] = summed[:HEAD_WIDTH]
 
 
+def select_near(center_ref, source_ref, near_ref, at0, spread_ref):
+    rows, width = source_ref.shape
+    near_rows = rows // CENTER_DILATION
+    for low in range(0, width, LANES):
+        lanes = slice(low, low + LANES)
+        spread_ref[low // LANES] = source_ref[:, lanes].astype(F32)
+    for low in range(0, width, LANES):
+        lanes = slice(low, low + LANES)
+        picked = jnp.zeros((near_rows, LANES), F32)
+        for step in range(CENTER_DILATION):
+            strided = pl.ds(step, near_rows, stride=CENTER_DILATION)
+            picked = jnp.where(center_ref[0:1, lanes] == step, spread_ref[low // LANES, strided, :], picked)
+        near_ref[:, at0 + low : at0 + low + LANES] = picked.astype(BF16)
+
+
 def first_forward_kernel(
-    group, heads, valid_ref, table_ref, k_ref, q_ref, v_ref, g_ref, after_ref,
-    qt_ref, gt_ref, kt_ref, vt_ref, *outs,
+    group, heads, valid_ref, table_ref, k_ref, q_ref, v_ref, g_ref, lanes_ref, after_ref,
+    near_ref, qt_ref, gt_ref, kt_ref, vt_ref, *refs,
 ):
+    *outs, spread_ref = refs
+    select_near(lanes_ref, k_ref, near_ref, 0, spread_ref.at[0])
+    select_near(lanes_ref, v_ref, near_ref, v_ref.shape[1], spread_ref.at[1])
     qt_ref[...] = q_ref[...].T
     vt_ref[...] = v_ref[...].T
     forward_heads(group, heads, valid_ref, table_ref, k_ref, qt_ref, vt_ref, *outs)
@@ -224,7 +227,7 @@
     row = lax.broadcasted_iota(jnp.int32, (count, LANES), 0)
     room = valid_ref[0] - ((device ^ 1) * rows + row * CENTER_DILATION)
     where = {}
-    for part, (first, last, _, _) in enumerate(groups):
+    for part, (first, last) in enumerate(groups):
         for h in range(first, last):
             where[h] = part, h - first
     for stack in stacks(heads, count):
@@ -307,8 +310,8 @@
 
 
 def near_backward_kernel(
-    heads, near_ref, far_ref, qt_ref, gt_ref, p_ref, ds_ref, factor_ref, delta_ref, ot_ref, after_ref,
-    out_ref, dq_ref, send_ref, sum_ref,
+    heads, near_ref, far_ref, qt_ref, gt_ref, p_ref, ds_ref, factor_ref, delta_ref, after_ref,
+    dq_ref, send_ref, sum_ref,
 ):
     width, rows = qt_ref.shape
     count = near_ref.shape[0]
@@ -344,13 +347,12 @@
         first, last, _, _ = stack
         dscore = ds_ref[first * count : last * count, :]
         add_dq(stack, nn(stacked(far_ref[:, :width], stack).T, dscore))
-    out_ref[...] = ot_ref[...].T
 
 
 def backward_heads(
     group, p_ref, qt_ref, gt_ref, kt_ref, v_ref, dq2_ref, factor_ref, delta_ref, dqt_ref, dk_ref, dv_ref
 ):
-    first, last, _, _ = group
+    first, last = group
     rows = v_ref.shape[0]
     parts = [slice(at, at + rows // 2) for at in (0, rows // 2)]
     work = [(h, part) for h in range(first, last) for part in parts]
@@ -380,6 +382,12 @@
     backward_heads(group, *refs[:8], *refs[9:])
 
 
+def turning_backward_kernel(group, *refs):
+    ot_ref, out_ref = refs[9:11]
+    backward_heads(group, *refs[:8], *refs[11:])
+    out_ref[...] = ot_ref[...].T
+
+
 def last_backward_kernel(groups, index, *refs):
     others = len(groups) - 1
     lanes_ref, back_ref, after_ref = refs[8:11]
@@ -394,11 +402,11 @@
 
     rows, width = dq_ref.shape
     near_rows = rows // CENTER_DILATION
-    for (first, last, _, _), ref in zip(groups, all_groups(0, dqt_ref)):
+    for (first, last), ref in zip(groups, all_groups(0, dqt_ref)):
         turned_ref[first * HEAD_WIDTH : last * HEAD_WIDTH, :] = ref[...]
     dq_ref[...] = turned_ref[...].T
     for at, parts, by in ((0, all_groups(1, dk_ref), SCALE), (width, all_groups(2, dv_ref), 1.0)):
-        for (first, last, _, _), ref in zip(groups, parts):
+        for (first, last), ref in zip(groups, parts):
             wide_ref[first * HEAD_WIDTH : last * HEAD_WIDTH, :] = ref[...] * by
         for low in range(0, width, LANES):
             block = (at + low) // LANES
@@ -455,16 +463,15 @@
     def swap(value, apart):
         return lax.ppermute(value, axes, [(at, at ^ apart) for at in range(devices)])
 
-    near, far, q, k, v, g, table, lanes = call(
+    far, q, k, v, g, table, lanes = call(
         functools.partial(select_kernel, heads),
-        [((near_rows, 2 * width), BF16), ((far_own, 2 * width), BF16)]
+        [((far_own, 2 * width), BF16)]
         + [((rows, width), BF16)] * 4
         + [((2 * heads, rows), jnp.int32), ((8, width), jnp.int32)],
         [HBM] * 6,
         [
             pltpu.SMEM(center_shift.shape, jnp.int32),
             pltpu.SMEM(wide_shift.shape, jnp.int32),
-            pltpu.VMEM((blocks, rows, LANES), F32),
             pltpu.SemaphoreType.DMA((6,)),
         ],
         moved=16 * rows * width,
@@ -485,17 +492,18 @@
     fronts = {}
 
     def front(index, after):
-        first, last, _, _ = groups[index]
+        first, last = groups[index]
         size, tall = last - first, (last - first) * HEAD_WIDTH
         outs = [((size, rows, rows), BF16), ((tall, rows), F32), ((size, rows), F32), ((size, rows), F32)]
         if not turned:
             *flipped, p, o, top, total = call(
                 functools.partial(first_forward_kernel, groups[index], heads),
-                [((width, rows), BF16)] * 4 + outs,
-                [SMEM] + [VMEM] * 5 + [ANY],
+                [((near_rows, 2 * width), BF16)] + [((width, rows), BF16)] * 4 + outs,
+                [SMEM] + [VMEM] * 6 + [ANY],
+                [pltpu.VMEM((2, blocks // 2, rows, LANES), F32)],
                 **cost(size, rows, 2),
-            )(valid, table, k, q, v, g, after)
-            turned.update(zip(("qt", "gt", "kt", "vt"), flipped))
+            )(valid, table, k, q, v, g, lanes, after)
+            turned.update(zip(("near", "qt", "gt", "kt", "vt"), flipped))
         else:
             p, o, top, total = call(
                 functools.partial(forward_kernel, groups[index], heads),
@@ -511,15 +519,17 @@
         return arrived
 
     last = len(groups) - 1
-    order = [last, *range(last)]
+    front_order, back_order = [last, *range(last)], [*range(last, -1, -1)]
     after = far
     for at, step in enumerate(steps):
+        if at == 1:
+            near_out, far = lax.optimization_barrier((turned["near"], far))
         arrived = swap(far, step)
-        if at == 0:
-            near_came = swap(near, 1)
-        if at < len(order):
-            front(order[at], after)
-        if at == len(order) - 1:
+        if at == 1:
+            near_came = swap(near_out, 1)
+        if at < len(groups):
+            front(front_order[at], after)
+        if at == len(groups) - 1:
             p, o, top, total = zip(*(fronts[index] for index in range(len(groups))))
             fronts["near"] = call(
                 functools.partial(near_forward_kernel, heads, groups),
@@ -528,8 +538,8 @@
                 **cost(heads, near_rows, 2),
             )(valid, table, near_came, turned["qt"], *o, *top, *total, after)
             arrived = tie(arrived, fronts, "near")
-        elif at < len(order):
-            arrived = tie(arrived, fronts, order[at])
+        elif at < len(groups):
+            arrived = tie(arrived, fronts, front_order[at])
         after = arrived
         far = jnp.concatenate([far, arrived], axis=0)
     near_p, o, old, near_top, near_sum = fronts["near"]
@@ -549,10 +559,18 @@
     backs = {}
 
     def back(index, after):
-        first, end, _, _ = groups[index]
+        first, end = groups[index]
         size, tall = end - first, (end - first) * HEAD_WIDTH
         partial = [((tall, rows), BF16), ((tall, rows), F32), ((tall, rows), F32)]
-        given = (p[index], qt, gt, kt, v, backs["near"][1], local_factor, delta)
+        given = (p[index], qt, gt, kt, v, backs["near"][0], local_factor, delta)
+        if len(backs) == OUT_AT:
+            backs["out"], *backs[index] = call(
+                functools.partial(turning_backward_kernel, groups[index]),
+                [((rows, width), BF16), *partial],
+                [VMEM] * 8 + [ANY, VMEM],
+                **cost(size, rows, 4),
+            )(*given, after, ot)
+            return
         if len(backs) < len(groups):
             backs[index] = call(
                 functools.partial(backward_kernel, groups[index]),
@@ -580,27 +598,27 @@
         if at == 0:
             backs["near"] = call(
                 functools.partial(near_backward_kernel, heads),
-                [((rows, width), BF16), ((width, rows), F32), ((near_rows, 2 * width), BF16)],
-                [VMEM] * 9 + [ANY],
+                [((width, rows), F32), ((near_rows, 2 * width), BF16)],
+                [VMEM] * 8 + [ANY],
                 [pltpu.VMEM((near_rows, 2 * width), F32)],
                 **cost(heads, near_rows, 4),
-            )(near_came, far, qt, gt, near_p, ds, near_factor, delta, ot, after)
+            )(near_came, far, qt, gt, near_p, ds, near_factor, delta, after)
         if at == 1:
-            near_back = swap(backs["near"][2], 1)
-        if at < len(order):
-            back(order[at], after)
-            arrived = tie(arrived, backs, order[at])
+            near_back = swap(backs["near"][1], 1)
+        if at < len(groups):
+            back(back_order[at], after)
+            arrived = tie(arrived, backs, back_order[at])
         after = arrived
         terms = terms + arrived.astype(F32)
 
-    dq, sums = backs[order[-1]]
+    dq, sums = backs[back_order[-1]]
     key_gradient, value_gradient = call(
         combine_kernel,
         [((rows, width), BF16)] * 2,
         [VMEM] * 3,
         moved=12 * rows * width,
     )(lanes, sums, terms)
-    return backs["near"][0], dq, key_gradient, value_gradient
+    return backs["out"], dq, key_gradient, value_gradient
 
 
 def solution(mesh):

time: 33.2 us -> 32.6 us (0.982)
  waiting for transfers between devices: 1.61 us -> 0.58 us
  Pallas kernels: 15.4 us -> 15.8 us
    pallas_call x3 -> x4, Pallas kernels: 4.51 us -> 6.57 us  [the longest x1 2.56 us: back(): call(functools.partial(turning_backward_kernel, groups[index]), [((rows,...]
    pallas_call x2 -> x1, Pallas kernels: 2.46 us -> 1.05 us  [back(): call(functools.partial(backward_kernel, groups[index]), partial, [VMEM] *...]
    ppermute x8, waiting for transfers between devices: 1.61 us -> 0.58 us  [swap(): lax.ppermute(value, axes, [(at, at ^ apart) for at in range(devices)])]
    pallas_call x1, Pallas kernels: 2.55 us -> 2.18 us  [back(): call(functools.partial(last_backward_kernel, groups, index), [((rows, wid...]
  transfers between devices with their start and end apart: 8 -> 8, of which waited for: 3 -> 1; matrix products, arithmetic and copies ran while one was open for 0% -> 0% of each run, Pallas kernels for 35% -> 38%
where the time goes in v4:
time: 32.6 us; the launch traced here: 32.4 us
  Pallas kernels  15.8 us (48%)
  starting transfers between devices  14.6 us (45%)
  between operations  1.43 us (4%)
  waiting for transfers between devices  0.58 us (2%)
    ppermute x8, starting transfers between devices, swap(): lax.ppermute(value, axes, [(at, at ^ apart) for at in range(devices)])  14.6 us
    pallas_call x2, Pallas kernels, front(): call(functools.partial(forward_kernel, groups[index], heads), outs, [SMEM...  2.87 us
    pallas_call x1, Pallas kernels, back(): call(functools.partial(turning_backward_kernel, groups[index]), [((rows,...  2.56 us
    pallas_call x1, Pallas kernels, back(): call(functools.partial(last_backward_kernel, groups, index), [((rows, wid...  2.18 us
    pallas_call x1, Pallas kernels, front(): call(functools.partial(first_forward_kernel, groups[index], heads), [((ne...  1.51 us
    pallas_call x1, Pallas kernels, local(): call(functools.partial(select_kernel, heads), [((far_own, 2 * width), BF1...  1.41 us
    pallas_call x1, Pallas kernels, local(): call(functools.partial(wide_kernel, heads, far_own), [((width, rows), BF1...  1.21 us
    pallas_call x1, Pallas kernels, local(): call(functools.partial(near_backward_kernel, heads), [((width, rows), F32...  1.09 us
  transfers between devices with their start and end apart: 8, of which 1 were waited for; matrix products, arithmetic and copies ran while one was open for 0% of the time, Pallas kernels for 38%

profile of v4, /device:TPU:0, one launch (start us, length us, event | category | flops | bytes accessed | tf_op | source)
XLA Modules:
  0.0 32.4 jit_solution(16417392002839929546)
XLA Ops:
  0.6 1.4 %shard_map.102 = (bf16[4,768]{1,0:T(4,128)(2,1)S(1)}, bf16[512,384]{1,0:T(8,128)(2,1)S(1)}, bf16[512,384]{1,0:T(8,128)(2,1)S(1)}, bf16[512,384]{1,0:T(8,128)(2,1...) custom-call(s32[16]{0:T(128)} %center_any.1, s32[16]{0:T(128)} %wide_any.1, ...), custom_call_target="tpu_custom_call" | custom-call | bytes 3145728 | tf_op jit(solution)/shard_map/pallas_call | solution.py:466
  2.0 3.0 %collective-permute-start = (bf16[4,768]{1,0:T(4,128)(2,1)S(1)}, bf16[4,768]{1,0:T(4,128)(2,1)S(1)}, u32[]{:S(2)}, u32[]{:S(2)}) collective-permute-start(bf16[4,768]{1,0:T(4,128)(2,1)S(1)} %get-tuple-element.77.after_ref), channel_id=1, source_target_pairs={{0,2},{2,0},{4,6},{6,4},{8,10},{10,8},{12,14},{14,12},{1,3},{3,1},... | collective-permute-start | bytes 18440 | tf_op jit(solution)/shard_map/ppermute | solution.py:464
  5.7 1.5 %shard_map.103 = (bf16[64,768]{1,0:T(8,128)(2,1)S(1)}, bf16[384,512]{1,0:T(8,128)(2,1)S(1)}, bf16[384,512]{1,0:T(8,128)(2,1)S(1)}, bf16[384,512]{1,0:T(8,128)(2,...) custom-call(s32[1]{0:T(128)S(6)} %copy.13.valid_ref, ...), custom_call_target="tpu_custom_call" | custom-call | flops 503316480 | bytes 1048576 | tf_op jit(solution)/shard_map/pallas_call | solution.py:499
  7.2 0.0 collective-permute-done.after_ref
  7.2 1.6 %collective-permute-start.1 = (bf16[8,768]{1,0:T(8,128)(2,1)S(1)}, bf16[8,768]{1,0:T(8,128)(2,1)S(1)}, u32[]{:S(2)}, u32[]{:S(2)}) collective-permute-start(bf16[8,768]{1,0:T(8,128)(2,1)S(1)} %pad_maximum_fusion.1), channel_id=1, source_target_pairs={{0,4},{2,6},{4,0},{6,2},{8,12},{10,14},{12,8},{14,10},{1,5},{3,7},... | collective-permute-start | bytes 36872 | tf_op jit(solution)/shard_map/ppermute | solution.py:464
  8.9 1.4 %collective-permute-start.2 = (bf16[64,768]{1,0:T(8,128)(2,1)S(1)}, bf16[64,768]{1,0:T(8,128)(2,1)S(1)}, u32[]{:S(2)}, u32[]{:S(2)}) collective-permute-start(bf16[64,768]{1,0:T(8,128)(2,1)S(1)} %get-tuple-element.89), channel_id=1, source_target_pairs={{0,2},{2,0},{4,6},{6,4},{8,10},{10,8},{12,14},{14,12},{1,3},{3,1},... | collective-permute-start | bytes 294920 | tf_op jit(solution)/shard_map/ppermute | solution.py:464
  10.3 1.0 %shard_map.104 = (bf16[2,512,512]{2,1,0:T(8,128)(2,1)S(1)}, f32[96,512]{1,0:T(8,128)S(1)}, f32[2,512]{1,0:T(2,128)S(1)}, f32[2,512]{1,0:T(2,128)S(1)}) custom-call(s32[1]{0:T(128)S(6)} %copy.13.valid_ref, s32[16,512]{1,0:T(8,128)S(1)} %get-tuple-element.71.table_ref, bf16[512,384]{1,0:T(8,128)(2,1)S(1)} %get-tuple-element.72.k_ref, ...), custom_call_target="tpu_custom_call" | custom-call | flops 503316480 | bytes 1048576 | tf_op jit(solution)/shard_map/pallas_call | solution.py:508
  11.4 0.0 collective-permute-done.1.after_ref.refs_9_
  11.4 2.7 %collective-permute-start.3 = (bf16[16,768]{1,0:T(8,128)(2,1)S(1)}, bf16[16,768]{1,0:T(8,128)(2,1)S(1)}, u32[]{:S(2)}, u32[]{:S(2)}) collective-permute-start(bf16[16,768]{1,0:T(8,128)(2,1)S(1)} %pad_maximum_fusion), channel_id=1, source_target_pairs={{0,8},{2,10},{4,12},{6,14},{8,0},{10,2},{12,4},{14,6},{1,9},{3,11}... | collective-permute-start | bytes 73736 | tf_op jit(solution)/shard_map/ppermute | solution.py:464
  14.1 1.9 %shard_map.105 = (bf16[4,512,512]{2,1,0:T(8,128)(2,1)S(1)}, f32[192,512]{1,0:T(8,128)S(1)}, f32[4,512]{1,0:T(4,128)S(1)}, f32[4,512]{1,0:T(4,128)S(1)}) custom-call(s32[1]{0:T(128)S(6)} %copy.13.valid_ref, s32[16,512]{1,0:T(8,128)S(1)} %get-tuple-element.71.table_ref, bf16[512,384]{1,0:T(8,128)(2,1)S(1)} %get-tuple-element.72.k_ref, ...), custom_call_target="tpu_custom_call" | custom-call | flops 1006632960 | bytes 2097152 | tf_op jit(solution)/shard_map/pallas_call | solution.py:508
  15.9 0.0 collective-permute-done.2.near_ref
  15.9 0.9 %shard_map.106 = (bf16[512,512]{1,0:T(8,128)(2,1)S(1)}, f32[384,512]{1,0:T(8,128)S(1)}, f32[8,512]{1,0:T(8,128)S(1)}, f32[8,512]{1,0:T(8,128)S(1)}, f32[8,512]{1,0:T(8,128)S(1)}) custom-call(s32[1]{0:T(128)S(6)} %copy.13.valid_ref, s32[16,512]{1,0:T(8,128)S(1)} %get-tuple-element.71.table_ref, bf16[64,768]{1,0:T(8,128)(2,1)S(1)} %collective-permute-done.2.near_ref, ...), custom_call_target="tpu_custom_call" | custom-call | flops 251658240 | bytes 524288 | tf_op jit(solution)/shard_map/pallas_call | solution.py:534
  16.9 0.0 collective-permute-done.3
  16.9 1.2 %shard_map.107 = (bf16[384,512]{1,0:T(8,128)(2,1)S(1)}, f32[8,512]{1,0:T(8,128)S(1)}, f32[8,512]{1,0:T(8,128)S(1)}, f32[8,512]{1,0:T(8,128)S(1)}, bf16[256,512]{...) custom-call(s32[1]{0:T(128)S(6)} %copy.13.valid_ref, s32[16,512]{1,0:T(8,128)S(1)} %get-tuple-element.71.table_ref, ...), custom_call_target="tpu_custom_call" | custom-call | flops 314572800 | bytes 262144 | tf_op jit(solution)/shard_map/pallas_call | solution.py:548
  18.1 1.9 %collective-permute-start.4 = (f32[16,768]{1,0:T(8,128)S(1)}, f32[16,768]{1,0:T(8,128)S(1)}, u32[]{:S(2)}, u32[]{:S(2)}) collective-permute-start(f32[16,768]{1,0:T(8,128)S(1)} %get-tuple-element.109.after_ref.refs_8_), channel_id=1, source_target_pairs={{0,8},{2,10},{4,12},{6,14},{8,0},{10,2},{12,4},{14,6},{1,9},{3,11}... | collective-permute-start | bytes 147464 | tf_op jit(solution)/shard_map/ppermute | solution.py:464
  20.1 1.1 %shard_map.108 = (f32[384,512]{1,0:T(8,128)S(1)}, bf16[64,768]{1,0:T(8,128)(2,1)S(1)}) custom-call(bf16[64,768]{1,0:T(8,128)(2,1)S(1)} %collective-permute-done.2.near_ref, bf16[32,768]{1,0:T(8,128)(2,1)S(1)} %constant_dynamic-update-slice_fusion.far_ref, bf16[384,512]{1,0:T(8,128)(2,1)S(1)} %get-tuple-element.78.qt_ref.refs_1_, ...), custom_call_target="tpu_custom_call" | custom-call | flops 503316480 | bytes 524288 | tf_op jit(solution)/shard_map/pallas_call | solution.py:599
  21.2 1.1 %collective-permute-start.5 = (bf16[64,768]{1,0:T(8,128)(2,1)S(1)}, bf16[64,768]{1,0:T(8,128)(2,1)S(1)}, u32[]{:S(2)}, u32[]{:S(2)}) collective-permute-start(bf16[64,768]{1,0:T(8,128)(2,1)S(1)} %get-tuple-element.118), channel_id=1, source_target_pairs={{0,2},{2,0},{4,6},{6,4},{8,10},{10,8},{12,14},{14,12},{1,3},{3,1},... | collective-permute-start | bytes 294920 | tf_op jit(solution)/shard_map/ppermute | solution.py:464
  22.2 1.0 %shard_map.109 = (bf16[96,512]{1,0:T(8,128)(2,1)S(1)}, f32[96,512]{1,0:T(8,128)S(1)}, f32[96,512]{1,0:T(8,128)S(1)}) custom-call(bf16[2,512,512]{2,1,0:T(8,128)(2,1)S(1)} %get-tuple-element.112.refs_0_, bf16[384,512]{1,0:T(8,128)(2,1)S(1)} %get-tuple-element.78.qt_ref.refs_1_, bf16[384,512]{1,0:T(8,128)(2,1)S(1)} %get-tuple-element.87.gt_ref.refs_2_, ...), custom_call_target="tpu_custom_call" | custom-call | flops 1006632960 | bytes 1048576 | tf_op jit(solution)/shard_map/pallas_call | solution.py:575
  23.3 0.0 collective-permute-done.4.refs_8_
  23.3 1.8 %collective-permute-start.6 = (f32[8,768]{1,0:T(8,128)S(1)}, f32[8,768]{1,0:T(8,128)S(1)}, u32[]{:S(2)}, u32[]{:S(2)}) collective-permute-start(f32[8,768]{1,0:T(8,128)S(1)} %slice.16), channel_id=1, source_target_pairs={{0,4},{2,6},{4,0},{6,2},{8,12},{10,14},{12,8},{14,10},{1,5},{3,7},... | collective-permute-start | bytes 73736 | tf_op jit(solution)/shard_map/ppermute | solution.py:464
  25.1 2.6 %shard_map.110 = (bf16[512,384]{1,0:T(8,128)(2,1)}, bf16[192,512]{1,0:T(8,128)(2,1)S(1)}, f32[192,512]{1,0:T(8,128)S(1)}, f32[192,512]{1,0:T(8,128)S(1)}) custom-call(bf16[4,512,512]{2,1,0:T(8,128)(2,1)S(1)} %get-tuple-element.86.refs_0_, bf16[384,512]{1,0:T(8,128)(2,1)S(1)} %get-tuple-element.78.qt_ref.refs_1_, ...), custom_call_target="tpu_custom_call" | custom-call | flops 2013265920 | bytes 2097152 | tf_op jit(solution)/shard_map/pallas_call | solution.py:567
  27.7 0.0 collective-permute-done.6.refs_10_
  27.7 1.0 %collective-permute-start.7 = (f32[4,768]{1,0:T(4,128)S(1)}, f32[4,768]{1,0:T(4,128)S(1)}, u32[]{:S(2)}, u32[]{:S(2)}) collective-permute-start(f32[4,768]{1,0:T(4,128)S(1)} %slice.18), channel_id=1, source_target_pairs={{0,2},{2,0},{4,6},{6,4},{8,10},{10,8},{12,14},{14,12},{1,3},{3,1},... | collective-permute-start | bytes 36872 | tf_op jit(solution)/shard_map/ppermute | solution.py:464
  28.7 0.0 collective-permute-done.5.refs_9_
  28.7 2.2 %shard_map.111 = (bf16[512,384]{1,0:T(8,128)(2,1)}, f32[6,512,128]{2,1,0:T(8,128)S(1)}) custom-call(bf16[2,512,512]{2,1,0:T(8,128)(2,1)S(1)} %get-tuple-element.117.refs_0_, bf16[384,512]{1,0:T(8,128)(2,1)S(1)} %get-tuple-element.78.qt_ref.refs_1_, bf16[384,512]{1,0:T(8,128)(2,1)S(1)} %get-tuple-element.87.gt_ref.refs_2_, ...), custom_call_target="tpu_custom_call" | custom-call | flops 1006632960 | bytes 1048576 | tf_op jit(solution)/shard_map/pallas_call | solution.py:583
  30.9 0.6 %collective-permute-done.7 = f32[4,768]{1,0:T(4,128)S(1)} collective-permute-done((f32[4,768]{1,0:T(4,128)S(1)}, f32[4,768]{1,0:T(4,128)S(1)}, u32[]{:S(2)}, u32[]{:S(2)}) %collective-permute-start.7) | collective-permute-done | bytes 12320 | tf_op jit(solution)/shard_map/ppermute | solution.py:464
  31.5 1.0 %shard_map.112 = (bf16[512,384]{1,0:T(8,128)(2,1)}, bf16[512,384]{1,0:T(8,128)(2,1)}) custom-call(s32[8,384]{1,0:T(8,128)S(1)} %get-tuple-element.76.lanes_ref.refs_8_, f32[6,512,128]{2,1,0:T(8,128)S(1)} %get-tuple-element.130.sum_ref, f32[4,768]{1,0:T(4,128)S(1)} %slice_add_fusion.1.far_ref), custom_call_target="tpu_custom_call" | custom-call | bytes 2359296 | tf_op jit(solution)/shard_map/pallas_call | solution.py:615
  (10 shorter events, 0.1 us)
Async XLA Ops:
  2.0 5.2 %collective-permute-start = (bf16[4,768]{1,0:T(4,128)(2,1)S(1)}, bf16[4,768]{1,0:T(4,128)(2,1)S(1)}, u32[]{:S(2)}, u32[]{:S(2)}) collective-permute-start(bf16[4,768]{1,0:T(4,128)(2,1)S(1)} %get-tuple-element.77.after_ref), channel_id=1, source_target_pairs={{0,2},{2,0},{4,6},{6,4},{8,10},{10,8},{12,14},{14,12},{1,3},{3,1},... | collective-permute-start | bytes 18440 | tf_op jit(solution)/shard_map/ppermute | solution.py:464
  7.2 4.1 %collective-permute-start.1 = (bf16[8,768]{1,0:T(8,128)(2,1)S(1)}, bf16[8,768]{1,0:T(8,128)(2,1)S(1)}, u32[]{:S(2)}, u32[]{:S(2)}) collective-permute-start(bf16[8,768]{1,0:T(8,128)(2,1)S(1)} %pad_maximum_fusion.1), channel_id=1, source_target_pairs={{0,4},{2,6},{4,0},{6,2},{8,12},{10,14},{12,8},{14,10},{1,5},{3,7},... | collective-permute-start | bytes 36872 | tf_op jit(solution)/shard_map/ppermute | solution.py:464
  8.9 7.0 %collective-permute-start.2 = (bf16[64,768]{1,0:T(8,128)(2,1)S(1)}, bf16[64,768]{1,0:T(8,128)(2,1)S(1)}, u32[]{:S(2)}, u32[]{:S(2)}) collective-permute-start(bf16[64,768]{1,0:T(8,128)(2,1)S(1)} %get-tuple-element.89), channel_id=1, source_target_pairs={{0,2},{2,0},{4,6},{6,4},{8,10},{10,8},{12,14},{14,12},{1,3},{3,1},... | collective-permute-start | bytes 294920 | tf_op jit(solution)/shard_map/ppermute | solution.py:464
  11.4 5.5 %collective-permute-start.3 = (bf16[16,768]{1,0:T(8,128)(2,1)S(1)}, bf16[16,768]{1,0:T(8,128)(2,1)S(1)}, u32[]{:S(2)}, u32[]{:S(2)}) collective-permute-start(bf16[16,768]{1,0:T(8,128)(2,1)S(1)} %pad_maximum_fusion), channel_id=1, source_target_pairs={{0,8},{2,10},{4,12},{6,14},{8,0},{10,2},{12,4},{14,6},{1,9},{3,11}... | collective-permute-start | bytes 73736 | tf_op jit(solution)/shard_map/ppermute | solution.py:464
  18.1 5.2 %collective-permute-start.4 = (f32[16,768]{1,0:T(8,128)S(1)}, f32[16,768]{1,0:T(8,128)S(1)}, u32[]{:S(2)}, u32[]{:S(2)}) collective-permute-start(f32[16,768]{1,0:T(8,128)S(1)} %get-tuple-element.109.after_ref.refs_8_), channel_id=1, source_target_pairs={{0,8},{2,10},{4,12},{6,14},{8,0},{10,2},{12,4},{14,6},{1,9},{3,11}... | collective-permute-start | bytes 147464 | tf_op jit(solution)/shard_map/ppermute | solution.py:464
  21.2 7.6 %collective-permute-start.5 = (bf16[64,768]{1,0:T(8,128)(2,1)S(1)}, bf16[64,768]{1,0:T(8,128)(2,1)S(1)}, u32[]{:S(2)}, u32[]{:S(2)}) collective-permute-start(bf16[64,768]{1,0:T(8,128)(2,1)S(1)} %get-tuple-element.118), channel_id=1, source_target_pairs={{0,2},{2,0},{4,6},{6,4},{8,10},{10,8},{12,14},{14,12},{1,3},{3,1},... | collective-permute-start | bytes 294920 | tf_op jit(solution)/shard_map/ppermute | solution.py:464
  23.3 4.4 %collective-permute-start.6 = (f32[8,768]{1,0:T(8,128)S(1)}, f32[8,768]{1,0:T(8,128)S(1)}, u32[]{:S(2)}, u32[]{:S(2)}) collective-permute-start(f32[8,768]{1,0:T(8,128)S(1)} %slice.16), channel_id=1, source_target_pairs={{0,4},{2,6},{4,0},{6,2},{8,12},{10,14},{12,8},{14,10},{1,5},{3,7},... | collective-permute-start | bytes 73736 | tf_op jit(solution)/shard_map/ppermute | solution.py:464
  27.7 3.8 %collective-permute-start.7 = (f32[4,768]{1,0:T(4,128)S(1)}, f32[4,768]{1,0:T(4,128)S(1)}, u32[]{:S(2)}, u32[]{:S(2)}) collective-permute-start(f32[4,768]{1,0:T(4,128)S(1)} %slice.18), channel_id=1, source_target_pairs={{0,2},{2,0},{4,6},{6,4},{8,10},{10,8},{12,14},{14,12},{1,3},{3,1},... | collective-permute-start | bytes 36872 | tf_op jit(solution)/shard_map/ppermute | solution.py:464

commit v5 on v4

--- a/solution.py
+++ b/solution.py
@@ -390,9 +390,14 @@
 
 def last_backward_kernel(groups, index, *refs):
     others = len(groups) - 1
-    lanes_ref, back_ref, after_ref = refs[8:11]
-    terms = refs[11 : 11 + 3 * others]
-    dq_ref, sum_ref, dqt_ref, dk_ref, dv_ref, turned_ref, wide_ref = refs[11 + 3 * others :]
+    lanes_ref, back_ref, out_ref, after_ref = refs[8:12]
+    terms = refs[12 : 12 + 3 * others]
+    out_any, dq_any, sum_ref, dqt_ref, dk_ref, dv_ref, turned_ref, wide_ref, dq_ref, sems = refs[12 + 3 * others :]
+    copies = [
+        pltpu.make_async_copy(out_ref, out_any, sems.at[0]),
+        pltpu.make_async_copy(dq_ref, dq_any, sems.at[1]),
+    ]
+    copies[0].start()
     backward_heads(groups[index], *refs[:8], dqt_ref, dk_ref, dv_ref)
 
     def all_groups(at, mine):
@@ -405,6 +410,7 @@
     for (first, last), ref in zip(groups, all_groups(0, dqt_ref)):
         turned_ref[first * HEAD_WIDTH : last * HEAD_WIDTH, :] = ref[...]
     dq_ref[...] = turned_ref[...].T
+    copies[1].start()
     for at, parts, by in ((0, all_groups(1, dk_ref), SCALE), (width, all_groups(2, dv_ref), 1.0)):
         for (first, last), ref in zip(groups, parts):
             wide_ref[first * HEAD_WIDTH : last * HEAD_WIDTH, :] = ref[...] * by
@@ -416,6 +422,8 @@
             for step in range(CENTER_DILATION):
                 strided = pl.ds(step, near_rows, stride=CENTER_DILATION)
                 sum_ref[block, strided, :] += jnp.where(center == step, near, 0.0)
+    for copy in copies:
+        copy.wait()
 
 
 def combine_kernel(lanes_ref, sum_ref, far_ref, outk_ref, outv_ref):
@@ -437,12 +445,12 @@
 HBM = pl.BlockSpec(memory_space=pltpu.HBM)
 
 
-def call(body, outs, ins, scratch=(), *, flops=0, moved=0):
+def call(body, outs, ins, scratch=(), *, in_hbm=0, flops=0, moved=0):
     return pl.pallas_call(
         body,
         out_shape=[jax.ShapeDtypeStruct(s, d) for s, d in outs],
         in_specs=ins,
-        out_specs=[VMEM] * len(outs),
+        out_specs=[HBM] * in_hbm + [VMEM] * (len(outs) - in_hbm),
         scratch_shapes=list(scratch),
         compiler_params=pltpu.CompilerParams(vmem_limit_bytes=24 * 2**20),
         cost_estimate=pl.CostEstimate(flops=flops, bytes_accessed=moved, transcendentals=0),
@@ -580,14 +588,16 @@
             )(*given, after)
             return
         others = [backs[other] for other in range(len(groups)) if other != index]
-        backs[index] = call(
+        backs["out"], *backs[index] = call(
             functools.partial(last_backward_kernel, groups, index),
-            [((rows, width), BF16), ((blocks, rows, LANES), F32)],
-            [VMEM] * 10 + [ANY] + [VMEM] * (3 * len(others)),
+            [((rows, width), BF16)] * 2 + [((blocks, rows, LANES), F32)],
+            [VMEM] * 11 + [ANY] + [VMEM] * (3 * len(others)),
             [pltpu.VMEM(shape, dtype) for shape, dtype in partial]
-            + [pltpu.VMEM((width, rows), BF16), pltpu.VMEM((width, rows), F32)],
+            + [pltpu.VMEM((width, rows), BF16), pltpu.VMEM((width, rows), F32)]
+            + [pltpu.VMEM((rows, width), BF16), pltpu.SemaphoreType.DMA((2,))],
+            in_hbm=2,
             **cost(size, rows, 4),
-        )(*given, lanes, near_back, after, *[terms[i] for i in range(3) for terms in others])
+        )(*given, lanes, near_back, backs["out"], after, *[terms[i] for i in range(3) for terms in others])
 
     after = send
     for at, step in enumerate(reversed(steps)):

time: 32.6 us -> 32.1 us (0.985)
  Pallas kernels: 15.8 us -> 15.2 us
    pallas_call x1, Pallas kernels: 2.56 us -> 1.87 us  [back(): call(functools.partial(turning_backward_kernel, groups[index]), [((rows,...]
  transfers between devices with their start and end apart: 8 -> 8, of which waited for: 1 -> 2; matrix products, arithmetic and copies ran while one was open for 0% -> 0% of each run, Pallas kernels for 38% -> 36%
where the time goes in v5:
time: 32.1 us; the launch traced here: 32 us
  Pallas kernels  15.2 us (47%)
  starting transfers between devices  14.6 us (45%)
  between operations  1.43 us (4%)
  waiting for transfers between devices  0.67 us (2%)
    ppermute x8, starting transfers between devices, swap(): lax.ppermute(value, axes, [(at, at ^ apart) for at in range(devices)])  14.6 us
    pallas_call x2, Pallas kernels, front(): call(functools.partial(forward_kernel, groups[index], heads), outs, [SMEM...  2.87 us
    pallas_call x1, Pallas kernels, back(): call(functools.partial(last_backward_kernel, groups, index), [((rows, wid...  2.24 us
    pallas_call x1, Pallas kernels, back(): call(functools.partial(turning_backward_kernel, groups[index]), [((rows,...  1.87 us
    pallas_call x1, Pallas kernels, front(): call(functools.partial(first_forward_kernel, groups[index], heads), [((ne...  1.51 us
    pallas_call x1, Pallas kernels, local(): call(functools.partial(select_kernel, heads), [((far_own, 2 * width), BF1...  1.41 us
    pallas_call x1, Pallas kernels, local(): call(functools.partial(wide_kernel, heads, far_own), [((width, rows), BF1...  1.22 us
    pallas_call x1, Pallas kernels, local(): call(functools.partial(near_backward_kernel, heads), [((width, rows), F32...  1.09 us
  transfers between devices with their start and end apart: 8, of which 2 were waited for; matrix products, arithmetic and copies ran while one was open for 0% of the time, Pallas kernels for 36%

profile of v5, /device:TPU:0, one launch (start us, length us, event | category | flops | bytes accessed | tf_op | source)
XLA Modules:
  0.0 32.0 jit_solution(8633655604347615283)
XLA Ops:
  0.6 1.4 %shard_map.102 = (bf16[4,768]{1,0:T(4,128)(2,1)S(1)}, bf16[512,384]{1,0:T(8,128)(2,1)S(1)}, bf16[512,384]{1,0:T(8,128)(2,1)S(1)}, bf16[512,384]{1,0:T(8,128)(2,1...) custom-call(s32[16]{0:T(128)} %center_any.1, s32[16]{0:T(128)} %wide_any.1, ...), custom_call_target="tpu_custom_call" | custom-call | bytes 3145728 | tf_op jit(solution)/shard_map/pallas_call | solution.py:474
  2.0 3.0 %collective-permute-start = (bf16[4,768]{1,0:T(4,128)(2,1)S(1)}, bf16[4,768]{1,0:T(4,128)(2,1)S(1)}, u32[]{:S(2)}, u32[]{:S(2)}) collective-permute-start(bf16[4,768]{1,0:T(4,128)(2,1)S(1)} %get-tuple-element.78.after_ref), channel_id=1, source_target_pairs={{0,2},{2,0},{4,6},{6,4},{8,10},{10,8},{12,14},{14,12},{1,3},{3,1},... | collective-permute-start | bytes 18440 | tf_op jit(solution)/shard_map/ppermute | solution.py:472
  5.7 1.5 %shard_map.103 = (bf16[64,768]{1,0:T(8,128)(2,1)S(1)}, bf16[384,512]{1,0:T(8,128)(2,1)S(1)}, bf16[384,512]{1,0:T(8,128)(2,1)S(1)}, bf16[384,512]{1,0:T(8,128)(2,...) custom-call(s32[1]{0:T(128)S(6)} %copy.13.valid_ref, ...), custom_call_target="tpu_custom_call" | custom-call | flops 503316480 | bytes 1048576 | tf_op jit(solution)/shard_map/pallas_call | solution.py:507
  7.2 0.0 collective-permute-done.after_ref
  7.2 1.6 %collective-permute-start.2 = (bf16[8,768]{1,0:T(8,128)(2,1)S(1)}, bf16[8,768]{1,0:T(8,128)(2,1)S(1)}, u32[]{:S(2)}, u32[]{:S(2)}) collective-permute-start(bf16[8,768]{1,0:T(8,128)(2,1)S(1)} %pad_maximum_fusion.1), channel_id=1, source_target_pairs={{0,4},{2,6},{4,0},{6,2},{8,12},{10,14},{12,8},{14,10},{1,5},{3,7},... | collective-permute-start | bytes 36872 | tf_op jit(solution)/shard_map/ppermute | solution.py:472
  8.9 1.5 %collective-permute-start.1 = (bf16[64,768]{1,0:T(8,128)(2,1)S(1)}, bf16[64,768]{1,0:T(8,128)(2,1)S(1)}, u32[]{:S(2)}, u32[]{:S(2)}) collective-permute-start(bf16[64,768]{1,0:T(8,128)(2,1)S(1)} %get-tuple-element.87), channel_id=1, source_target_pairs={{0,2},{2,0},{4,6},{6,4},{8,10},{10,8},{12,14},{14,12},{1,3},{3,1},... | collective-permute-start | bytes 294920 | tf_op jit(solution)/shard_map/ppermute | solution.py:472
  10.3 1.0 %shard_map.104 = (bf16[2,512,512]{2,1,0:T(8,128)(2,1)S(1)}, f32[96,512]{1,0:T(8,128)S(1)}, f32[2,512]{1,0:T(2,128)S(1)}, f32[2,512]{1,0:T(2,128)S(1)}) custom-call(s32[1]{0:T(128)S(6)} %copy.13.valid_ref, s32[16,512]{1,0:T(8,128)S(1)} %get-tuple-element.72.table_ref, bf16[512,384]{1,0:T(8,128)(2,1)S(1)} %get-tuple-element.73.k_ref, ...), custom_call_target="tpu_custom_call" | custom-call | flops 503316480 | bytes 1048576 | tf_op jit(solution)/shard_map/pallas_call | solution.py:516
  11.4 0.0 collective-permute-done.2.after_ref.refs_9_
  11.4 2.7 %collective-permute-start.3 = (bf16[16,768]{1,0:T(8,128)(2,1)S(1)}, bf16[16,768]{1,0:T(8,128)(2,1)S(1)}, u32[]{:S(2)}, u32[]{:S(2)}) collective-permute-start(bf16[16,768]{1,0:T(8,128)(2,1)S(1)} %pad_maximum_fusion), channel_id=1, source_target_pairs={{0,8},{2,10},{4,12},{6,14},{8,0},{10,2},{12,4},{14,6},{1,9},{3,11}... | collective-permute-start | bytes 73736 | tf_op jit(solution)/shard_map/ppermute | solution.py:472
  14.0 1.9 %shard_map.105 = (bf16[4,512,512]{2,1,0:T(8,128)(2,1)S(1)}, f32[192,512]{1,0:T(8,128)S(1)}, f32[4,512]{1,0:T(4,128)S(1)}, f32[4,512]{1,0:T(4,128)S(1)}) custom-call(s32[1]{0:T(128)S(6)} %copy.13.valid_ref, s32[16,512]{1,0:T(8,128)S(1)} %get-tuple-element.72.table_ref, bf16[512,384]{1,0:T(8,128)(2,1)S(1)} %get-tuple-element.73.k_ref, ...), custom_call_target="tpu_custom_call" | custom-call | flops 1006632960 | bytes 2097152 | tf_op jit(solution)/shard_map/pallas_call | solution.py:516
  15.9 0.0 collective-permute-done.1.near_ref
  15.9 0.9 %shard_map.106 = (bf16[512,512]{1,0:T(8,128)(2,1)S(1)}, f32[384,512]{1,0:T(8,128)S(1)}, f32[8,512]{1,0:T(8,128)S(1)}, f32[8,512]{1,0:T(8,128)S(1)}, f32[8,512]{1,0:T(8,128)S(1)}) custom-call(s32[1]{0:T(128)S(6)} %copy.13.valid_ref, s32[16,512]{1,0:T(8,128)S(1)} %get-tuple-element.72.table_ref, bf16[64,768]{1,0:T(8,128)(2,1)S(1)} %collective-permute-done.1.near_ref, ...), custom_call_target="tpu_custom_call" | custom-call | flops 251658240 | bytes 524288 | tf_op jit(solution)/shard_map/pallas_call | solution.py:542
  16.9 0.0 collective-permute-done.3
  16.9 1.2 %shard_map.107 = (bf16[384,512]{1,0:T(8,128)(2,1)S(1)}, f32[8,512]{1,0:T(8,128)S(1)}, f32[8,512]{1,0:T(8,128)S(1)}, f32[8,512]{1,0:T(8,128)S(1)}, bf16[256,512]{...) custom-call(s32[1]{0:T(128)S(6)} %copy.13.valid_ref, s32[16,512]{1,0:T(8,128)S(1)} %get-tuple-element.72.table_ref, ...), custom_call_target="tpu_custom_call" | custom-call | flops 314572800 | bytes 262144 | tf_op jit(solution)/shard_map/pallas_call | solution.py:556
  18.1 1.9 %collective-permute-start.5 = (f32[16,768]{1,0:T(8,128)S(1)}, f32[16,768]{1,0:T(8,128)S(1)}, u32[]{:S(2)}, u32[]{:S(2)}) collective-permute-start(f32[16,768]{1,0:T(8,128)S(1)} %get-tuple-element.110.after_ref.refs_8_), channel_id=1, source_target_pairs={{0,8},{2,10},{4,12},{6,14},{8,0},{10,2},{12,4},{14,6},{1,9},{3,11}... | collective-permute-start | bytes 147464 | tf_op jit(solution)/shard_map/ppermute | solution.py:472
  20.1 1.1 %shard_map.108 = (f32[384,512]{1,0:T(8,128)S(1)}, bf16[64,768]{1,0:T(8,128)(2,1)S(1)}) custom-call(bf16[64,768]{1,0:T(8,128)(2,1)S(1)} %collective-permute-done.1.near_ref, bf16[32,768]{1,0:T(8,128)(2,1)S(1)} %constant_dynamic-update-slice_fusion.far_ref, bf16[384,512]{1,0:T(8,128)(2,1)S(1)} %get-tuple-element.79.qt_ref.refs_1_, ...), custom_call_target="tpu_custom_call" | custom-call | flops 503316480 | bytes 524288 | tf_op jit(solution)/shard_map/pallas_call | solution.py:609
  21.2 1.1 %collective-permute-start.4 = (bf16[64,768]{1,0:T(8,128)(2,1)S(1)}, bf16[64,768]{1,0:T(8,128)(2,1)S(1)}, u32[]{:S(2)}, u32[]{:S(2)}) collective-permute-start(bf16[64,768]{1,0:T(8,128)(2,1)S(1)} %get-tuple-element.113), channel_id=1, source_target_pairs={{0,2},{2,0},{4,6},{6,4},{8,10},{10,8},{12,14},{14,12},{1,3},{3,1},... | collective-permute-start | bytes 294920 | tf_op jit(solution)/shard_map/ppermute | solution.py:472
  22.2 1.0 %shard_map.109 = (bf16[96,512]{1,0:T(8,128)(2,1)S(1)}, f32[96,512]{1,0:T(8,128)S(1)}, f32[96,512]{1,0:T(8,128)S(1)}) custom-call(bf16[2,512,512]{2,1,0:T(8,128)(2,1)S(1)} %get-tuple-element.115.refs_0_, bf16[384,512]{1,0:T(8,128)(2,1)S(1)} %get-tuple-element.79.qt_ref.refs_1_, bf16[384,512]{1,0:T(8,128)(2,1)S(1)} %get-tuple-element.84.gt_ref.refs_2_, ...), custom_call_target="tpu_custom_call" | custom-call | flops 1006632960 | bytes 1048576 | tf_op jit(solution)/shard_map/pallas_call | solution.py:583
  23.3 0.0 collective-permute-done.5.refs_8_
  23.3 1.8 %collective-permute-start.6 = (f32[8,768]{1,0:T(8,128)S(1)}, f32[8,768]{1,0:T(8,128)S(1)}, u32[]{:S(2)}, u32[]{:S(2)}) collective-permute-start(f32[8,768]{1,0:T(8,128)S(1)} %slice.16), channel_id=1, source_target_pairs={{0,4},{2,6},{4,0},{6,2},{8,12},{10,14},{12,8},{14,10},{1,5},{3,7},... | collective-permute-start | bytes 73736 | tf_op jit(solution)/shard_map/ppermute | solution.py:472
  25.1 1.9 %shard_map.110 = (bf16[512,384]{1,0:T(8,128)(2,1)S(1)}, bf16[192,512]{1,0:T(8,128)(2,1)S(1)}, f32[192,512]{1,0:T(8,128)S(1)}, f32[192,512]{1,0:T(8,128)S(1)}) custom-call(bf16[4,512,512]{2,1,0:T(8,128)(2,1)S(1)} %get-tuple-element.114.refs_0_, bf16[384,512]{1,0:T(8,128)(2,1)S(1)} %get-tuple-element.79.qt_ref.refs_1_, ...), custom_call_target="tpu_custom_call" | custom-call | flops 2013265920 | bytes 2097152 | tf_op jit(solution)/shard_map/pallas_call | solution.py:575
  27.0 0.2 collective-permute-done.6.refs_11_
  27.2 1.1 %collective-permute-start.7 = (f32[4,768]{1,0:T(4,128)S(1)}, f32[4,768]{1,0:T(4,128)S(1)}, u32[]{:S(2)}, u32[]{:S(2)}) collective-permute-start(f32[4,768]{1,0:T(4,128)S(1)} %slice.18), channel_id=1, source_target_pairs={{0,2},{2,0},{4,6},{6,4},{8,10},{10,8},{12,14},{14,12},{1,3},{3,1},... | collective-permute-start | bytes 36872 | tf_op jit(solution)/shard_map/ppermute | solution.py:472
  28.3 0.0 collective-permute-done.4.refs_9_
  28.3 2.2 %shard_map.111 = (bf16[512,384]{1,0:T(8,128)(2,1)}, bf16[512,384]{1,0:T(8,128)(2,1)}, f32[6,512,128]{2,1,0:T(8,128)S(1)}) custom-call(bf16[2,512,512]{2,1,0:T(8,128)(2,1)S(1)} %get-tuple-element.83.refs_0_, bf16[384,512]{1,0:T(8,128)(2,1)S(1)} %get-tuple-element.79.qt_ref.refs_1_, bf16[384,512]{1,0:T(8,128)(2,1)S(1)} %get-tuple-element.84.gt_ref.refs_2_, ...), custom_call_target="tpu_custom_call" | custom-call | flops 1006632960 | bytes 1048576 | tf_op jit(solution)/shard_map/pallas_call | solution.py:591
  30.6 0.4 %collective-permute-done.7 = f32[4,768]{1,0:T(4,128)S(1)} collective-permute-done((f32[4,768]{1,0:T(4,128)S(1)}, f32[4,768]{1,0:T(4,128)S(1)}, u32[]{:S(2)}, u32[]{:S(2)}) %collective-permute-start.7) | collective-permute-done | bytes 12320 | tf_op jit(solution)/shard_map/ppermute | solution.py:472
  31.0 1.0 %shard_map.112 = (bf16[512,384]{1,0:T(8,128)(2,1)}, bf16[512,384]{1,0:T(8,128)(2,1)}) custom-call(s32[8,384]{1,0:T(8,128)S(1)} %get-tuple-element.77.lanes_ref.refs_8_, f32[6,512,128]{2,1,0:T(8,128)S(1)} %get-tuple-element.132.sum_ref, f32[4,768]{1,0:T(4,128)S(1)} %slice_add_fusion.1.far_ref), custom_call_target="tpu_custom_call" | custom-call | bytes 2359296 | tf_op jit(solution)/shard_map/pallas_call | solution.py:625
  (10 shorter events, 0.1 us)
Async XLA Ops:
  2.0 5.2 %collective-permute-start = (bf16[4,768]{1,0:T(4,128)(2,1)S(1)}, bf16[4,768]{1,0:T(4,128)(2,1)S(1)}, u32[]{:S(2)}, u32[]{:S(2)}) collective-permute-start(bf16[4,768]{1,0:T(4,128)(2,1)S(1)} %get-tuple-element.78.after_ref), channel_id=1, source_target_pairs={{0,2},{2,0},{4,6},{6,4},{8,10},{10,8},{12,14},{14,12},{1,3},{3,1},... | collective-permute-start | bytes 18440 | tf_op jit(solution)/shard_map/ppermute | solution.py:472
  7.2 4.1 %collective-permute-start.2 = (bf16[8,768]{1,0:T(8,128)(2,1)S(1)}, bf16[8,768]{1,0:T(8,128)(2,1)S(1)}, u32[]{:S(2)}, u32[]{:S(2)}) collective-permute-start(bf16[8,768]{1,0:T(8,128)(2,1)S(1)} %pad_maximum_fusion.1), channel_id=1, source_target_pairs={{0,4},{2,6},{4,0},{6,2},{8,12},{10,14},{12,8},{14,10},{1,5},{3,7},... | collective-permute-start | bytes 36872 | tf_op jit(solution)/shard_map/ppermute | solution.py:472
  8.9 7.0 %collective-permute-start.1 = (bf16[64,768]{1,0:T(8,128)(2,1)S(1)}, bf16[64,768]{1,0:T(8,128)(2,1)S(1)}, u32[]{:S(2)}, u32[]{:S(2)}) collective-permute-start(bf16[64,768]{1,0:T(8,128)(2,1)S(1)} %get-tuple-element.87), channel_id=1, source_target_pairs={{0,2},{2,0},{4,6},{6,4},{8,10},{10,8},{12,14},{14,12},{1,3},{3,1},... | collective-permute-start | bytes 294920 | tf_op jit(solution)/shard_map/ppermute | solution.py:472
  11.4 5.5 %collective-permute-start.3 = (bf16[16,768]{1,0:T(8,128)(2,1)S(1)}, bf16[16,768]{1,0:T(8,128)(2,1)S(1)}, u32[]{:S(2)}, u32[]{:S(2)}) collective-permute-start(bf16[16,768]{1,0:T(8,128)(2,1)S(1)} %pad_maximum_fusion), channel_id=1, source_target_pairs={{0,8},{2,10},{4,12},{6,14},{8,0},{10,2},{12,4},{14,6},{1,9},{3,11}... | collective-permute-start | bytes 73736 | tf_op jit(solution)/shard_map/ppermute | solution.py:472
  18.1 5.2 %collective-permute-start.5 = (f32[16,768]{1,0:T(8,128)S(1)}, f32[16,768]{1,0:T(8,128)S(1)}, u32[]{:S(2)}, u32[]{:S(2)}) collective-permute-start(f32[16,768]{1,0:T(8,128)S(1)} %get-tuple-element.110.after_ref.refs_8_), channel_id=1, source_target_pairs={{0,8},{2,10},{4,12},{6,14},{8,0},{10,2},{12,4},{14,6},{1,9},{3,11}... | collective-permute-start | bytes 147464 | tf_op jit(solution)/shard_map/ppermute | solution.py:472
  21.2 7.2 %collective-permute-start.4 = (bf16[64,768]{1,0:T(8,128)(2,1)S(1)}, bf16[64,768]{1,0:T(8,128)(2,1)S(1)}, u32[]{:S(2)}, u32[]{:S(2)}) collective-permute-start(bf16[64,768]{1,0:T(8,128)(2,1)S(1)} %get-tuple-element.113), channel_id=1, source_target_pairs={{0,2},{2,0},{4,6},{6,4},{8,10},{10,8},{12,14},{14,12},{1,3},{3,1},... | collective-permute-start | bytes 294920 | tf_op jit(solution)/shard_map/ppermute | solution.py:472
  23.3 3.9 %collective-permute-start.6 = (f32[8,768]{1,0:T(8,128)S(1)}, f32[8,768]{1,0:T(8,128)S(1)}, u32[]{:S(2)}, u32[]{:S(2)}) collective-permute-start(f32[8,768]{1,0:T(8,128)S(1)} %slice.16), channel_id=1, source_target_pairs={{0,4},{2,6},{4,0},{6,2},{8,12},{10,14},{12,8},{14,10},{1,5},{3,7},... | collective-permute-start | bytes 73736 | tf_op jit(solution)/shard_map/ppermute | solution.py:472
  27.2 3.8 %collective-permute-start.7 = (f32[4,768]{1,0:T(4,128)S(1)}, f32[4,768]{1,0:T(4,128)S(1)}, u32[]{:S(2)}, u32[]{:S(2)}) collective-permute-start(f32[4,768]{1,0:T(4,128)S(1)} %slice.18), channel_id=1, source_target_pairs={{0,2},{2,0},{4,6},{6,4},{8,10},{10,8},{12,14},{14,12},{1,3},{3,1},... | collective-permute-start | bytes 36872 | tf_op jit(solution)/shard_map/ppermute | solution.py:472

commit v6 on v5

--- a/solution.py
+++ b/solution.py
@@ -73,14 +73,14 @@
 
 
 def select_kernel(
-    heads, center_any, wide_any, q_any, k_any, v_any, g_any,
-    far_ref, q_ref, k_ref, v_ref, g_ref, table_ref, lanes_ref,
+    heads, center_any, wide_any, q_any, k_any, v_any,
+    far_ref, q_ref, k_ref, v_ref, table_ref, lanes_ref,
     center_ref, wide_ref, sems,
 ):
     rows, width = k_ref.shape
     pairs = (
         (center_any, center_ref), (wide_any, wide_ref),
-        (k_any, k_ref), (v_any, v_ref), (q_any, q_ref), (g_any, g_ref),
+        (k_any, k_ref), (v_any, v_ref), (q_any, q_ref),
     )
     copies = [pltpu.make_async_copy(a, b, sems.at[i]) for i, (a, b) in enumerate(pairs)]
     for copy in copies:
@@ -106,7 +106,6 @@
             chosen = jnp.where(row == wide[:, lanes], spread.reshape(row.shape), 0.0)
             far_ref[:, packed] = jnp.sum(chosen, axis=1).astype(BF16)
     copies[4].wait()
-    copies[5].wait()
 
 
 def forward_heads(
@@ -158,8 +157,8 @@
 
 
 def first_forward_kernel(
-    group, heads, valid_ref, table_ref, k_ref, q_ref, v_ref, g_ref, lanes_ref, after_ref,
-    near_ref, qt_ref, gt_ref, kt_ref, vt_ref, *refs,
+    group, heads, valid_ref, table_ref, k_ref, q_ref, v_ref, lanes_ref, after_ref,
+    near_ref, qt_ref, vt_ref, *refs,
 ):
     *outs, spread_ref = refs
     select_near(lanes_ref, k_ref, near_ref, 0, spread_ref.at[0])
@@ -167,8 +166,6 @@
     qt_ref[...] = q_ref[...].T
     vt_ref[...] = v_ref[...].T
     forward_heads(group, heads, valid_ref, table_ref, k_ref, qt_ref, vt_ref, *outs)
-    gt_ref[...] = g_ref[...].T
-    kt_ref[...] = k_ref[...].T
 
 
 def forward_kernel(group, heads, valid_ref, table_ref, k_ref, qt_ref, vt_ref, after_ref, *outs):
@@ -217,10 +214,12 @@
     return jnp.concatenate([value] * (rows // LANES), axis=1)
 
 
-def near_forward_kernel(heads, groups, valid_ref, table_ref, near_ref, qt_ref, *refs):
+def near_forward_kernel(heads, groups, valid_ref, table_ref, near_ref, qt_ref, k_ref, g_ref, *refs):
     parts = len(groups)
     o1_refs, max_refs, sum_refs = (refs[i * parts : (i + 1) * parts] for i in range(3))
-    after_ref, p_ref, o_ref, old_ref, top_ref, sum_ref = refs[3 * parts :]
+    after_ref, gt_ref, kt_ref, p_ref, o_ref, old_ref, top_ref, sum_ref = refs[3 * parts :]
+    gt_ref[...] = g_ref[...].T
+    kt_ref[...] = k_ref[...].T
     width, rows = qt_ref.shape
     count = near_ref.shape[0]
     device = lax.axis_index(("seq", "sub"))
@@ -292,6 +291,7 @@
             local_ref[one, :] = jnp.exp2((old_ref[one, :] - top) * EXP2_SCALE) * inverse
         weights = jnp.concatenate([prob.astype(BF16) for prob in probs], axis=0)
         added = nn(value_rows.T, weights)
+        unstack(sum_ref, width, stack, count, nt(weights, gt_ref[low:high, :]), 1.0, started)
         dscores = []
         for at, h in enumerate(range(first, last)):
             inside = added[h * HEAD_WIDTH - low : (h + 1) * HEAD_WIDTH - low]
@@ -304,7 +304,6 @@
         dscore = jnp.concatenate(dscores, axis=0)
         ds_ref[first * count : last * count, :] = dscore
         unstack(sum_ref, 0, stack, count, nt(dscore, qt_ref[low:high, :]), SCALE, started)
-        unstack(sum_ref, width, stack, count, nt(weights, gt_ref[low:high, :]), 1.0, started)
     keep_ref[...] = sum_ref[:half, :]
     send_ref[...] = sum_ref[half:, :].astype(send_ref.dtype)
 
@@ -471,22 +470,22 @@
     def swap(value, apart):
         return lax.ppermute(value, axes, [(at, at ^ apart) for at in range(devices)])
 
-    far, q, k, v, g, table, lanes = call(
+    far, q, k, v, table, lanes = call(
         functools.partial(select_kernel, heads),
         [((far_own, 2 * width), BF16)]
-        + [((rows, width), BF16)] * 4
+        + [((rows, width), BF16)] * 3
         + [((2 * heads, rows), jnp.int32), ((8, width), jnp.int32)],
-        [HBM] * 6,
+        [HBM] * 5,
         [
             pltpu.SMEM(center_shift.shape, jnp.int32),
             pltpu.SMEM(wide_shift.shape, jnp.int32),
-            pltpu.SemaphoreType.DMA((6,)),
+            pltpu.SemaphoreType.DMA((5,)),
         ],
         moved=16 * rows * width,
     )(
         *(
             pltpu.with_memory_space_constraint(value, pltpu.HBM)
-            for value in (center_shift, wide_shift, queries, keys, values, grad_out)
+            for value in (center_shift, wide_shift, queries, keys, values)
         )
     )
 
@@ -506,12 +505,12 @@
         if not turned:
             *flipped, p, o, top, total = call(
                 functools.partial(first_forward_kernel, groups[index], heads),
-                [((near_rows, 2 * width), BF16)] + [((width, rows), BF16)] * 4 + outs,
-                [SMEM] + [VMEM] * 6 + [ANY],
+                [((near_rows, 2 * width), BF16)] + [((width, rows), BF16)] * 2 + outs,
+                [SMEM] + [VMEM] * 5 + [ANY],
                 [pltpu.VMEM((2, blocks // 2, rows, LANES), F32)],
                 **cost(size, rows, 2),
-            )(valid, table, k, q, v, g, lanes, after)
-            turned.update(zip(("near", "qt", "gt", "kt", "vt"), flipped))
+            )(valid, table, k, q, v, lanes, after)
+            turned.update(zip(("near", "qt", "vt"), flipped))
         else:
             p, o, top, total = call(
                 functools.partial(forward_kernel, groups[index], heads),
@@ -541,17 +540,19 @@
             p, o, top, total = zip(*(fronts[index] for index in range(len(groups))))
             fronts["near"] = call(
                 functools.partial(near_forward_kernel, heads, groups),
-                [((heads * near_rows, rows), BF16), ((width, rows), F32)] + [((heads, rows), F32)] * 3,
-                [SMEM] + [VMEM] * (3 + 3 * len(groups)) + [ANY],
+                [((width, rows), BF16)] * 2
+                + [((heads * near_rows, rows), BF16), ((width, rows), F32)]
+                + [((heads, rows), F32)] * 3,
+                [SMEM] + [VMEM] * (5 + 3 * len(groups)) + [ANY],
                 **cost(heads, near_rows, 2),
-            )(valid, table, near_came, turned["qt"], *o, *top, *total, after)
+            )(valid, table, near_came, turned["qt"], k, grad_out, *o, *top, *total, after)
             arrived = tie(arrived, fronts, "near")
         elif at < len(groups):
             arrived = tie(arrived, fronts, front_order[at])
         after = arrived
         far = jnp.concatenate([far, arrived], axis=0)
-    near_p, o, old, near_top, near_sum = fronts["near"]
-    qt, gt, kt = (turned[name] for name in ("qt", "gt", "kt"))
+    gt, kt, near_p, o, old, near_top, near_sum = fronts["near"]
+    qt = turned["qt"]
 
     ot, local_factor, near_factor, delta, ds, terms, send = call(
         functools.partial(wide_kernel, heads, far_own),

time: 32.1 us -> 31.9 us (level)
  transfers between devices with their start and end apart: 8 -> 8, of which waited for: 2 -> 2; matrix products, arithmetic and copies ran while one was open for 0% -> 0% of each run, Pallas kernels for 36% -> 37%
where the time goes in v6:
time: 31.9 us; the launch traced here: 31.7 us
  Pallas kernels  15 us (47%)
  starting transfers between devices  14.6 us (46%)
  between operations  1.45 us (5%)
  waiting for transfers between devices  0.62 us (2%)
    ppermute x8, starting transfers between devices, swap(): lax.ppermute(value, axes, [(at, at ^ apart) for at in range(devices)])  14.6 us
    pallas_call x2, Pallas kernels, front(): call(functools.partial(forward_kernel, groups[index], heads), outs, [SMEM...  2.9 us
    pallas_call x1, Pallas kernels, back(): call(functools.partial(last_backward_kernel, groups, index), [((rows, wid...  2.25 us
    pallas_call x1, Pallas kernels, back(): call(functools.partial(turning_backward_kernel, groups[index]), [((rows,...  1.88 us
    pallas_call x1, Pallas kernels, front(): call(functools.partial(first_forward_kernel, groups[index], heads), [((ne...  1.47 us
    pallas_call x1, Pallas kernels, local(): call(functools.partial(select_kernel, heads), [((far_own, 2 * width), BF1...  1.28 us
    pallas_call x1, Pallas kernels, local(): call(functools.partial(near_backward_kernel, heads), [((width, rows), F32...  1.11 us
    pallas_call x1, Pallas kernels, local(): call(functools.partial(wide_kernel, heads, far_own), [((width, rows), BF1...  1.1 us
  transfers between devices with their start and end apart: 8, of which 2 were waited for; matrix products, arithmetic and copies ran while one was open for 0% of the time, Pallas kernels for 37%

profile of v6, /device:TPU:0, one launch (start us, length us, event | category | flops | bytes accessed | tf_op | source)
XLA Modules:
  0.0 31.7 jit_solution(8743049886480181049)
XLA Ops:
  0.6 1.3 %shard_map.102 = (bf16[4,768]{1,0:T(4,128)(2,1)S(1)}, bf16[512,384]{1,0:T(8,128)(2,1)S(1)}, bf16[512,384]{1,0:T(8,128)(2,1)S(1)}, bf16[512,384]{1,0:T(8,128)(2,1...) custom-call(s32[16]{0:T(128)} %center_any.1, s32[16]{0:T(128)} %wide_any.1, bf16[512,384]{1,0:T(8,128)(2,1)} %q_any.1, ...), custom_call_target="tpu_custom_call" | custom-call | bytes 3145728 | tf_op jit(solution)/shard_map/pallas_call | solution.py:473
  1.9 3.0 %collective-permute-start = (bf16[4,768]{1,0:T(4,128)(2,1)S(1)}, bf16[4,768]{1,0:T(4,128)(2,1)S(1)}, u32[]{:S(2)}, u32[]{:S(2)}) collective-permute-start(bf16[4,768]{1,0:T(4,128)(2,1)S(1)} %get-tuple-element.76.after_ref), channel_id=1, source_target_pairs={{0,2},{2,0},{4,6},{6,4},{8,10},{10,8},{12,14},{14,12},{1,3},{3,1},... | collective-permute-start | bytes 18440 | tf_op jit(solution)/shard_map/ppermute | solution.py:471
  5.6 1.5 %shard_map.103 = (bf16[64,768]{1,0:T(8,128)(2,1)S(1)}, bf16[384,512]{1,0:T(8,128)(2,1)S(1)}, bf16[384,512]{1,0:T(8,128)(2,1)S(1)}, bf16[2,512,512]{2,1,0:T(8,128...) custom-call(s32[1]{0:T(128)S(6)} %copy.13.valid_ref, ...), custom_call_target="tpu_custom_call" | custom-call | flops 503316480 | bytes 1048576 | tf_op jit(solution)/shard_map/pallas_call | solution.py:506
  7.0 0.0 collective-permute-done.after_ref
  7.1 1.6 %collective-permute-start.2 = (bf16[8,768]{1,0:T(8,128)(2,1)S(1)}, bf16[8,768]{1,0:T(8,128)(2,1)S(1)}, u32[]{:S(2)}, u32[]{:S(2)}) collective-permute-start(bf16[8,768]{1,0:T(8,128)(2,1)S(1)} %pad_maximum_fusion.1), channel_id=1, source_target_pairs={{0,4},{2,6},{4,0},{6,2},{8,12},{10,14},{12,8},{14,10},{1,5},{3,7},... | collective-permute-start | bytes 36872 | tf_op jit(solution)/shard_map/ppermute | solution.py:471
  8.7 1.5 %collective-permute-start.1 = (bf16[64,768]{1,0:T(8,128)(2,1)S(1)}, bf16[64,768]{1,0:T(8,128)(2,1)S(1)}, u32[]{:S(2)}, u32[]{:S(2)}) collective-permute-start(bf16[64,768]{1,0:T(8,128)(2,1)S(1)} %get-tuple-element.83), channel_id=1, source_target_pairs={{0,2},{2,0},{4,6},{6,4},{8,10},{10,8},{12,14},{14,12},{1,3},{3,1},... | collective-permute-start | bytes 294920 | tf_op jit(solution)/shard_map/ppermute | solution.py:471
  10.2 1.0 %shard_map.104 = (bf16[2,512,512]{2,1,0:T(8,128)(2,1)S(1)}, f32[96,512]{1,0:T(8,128)S(1)}, f32[2,512]{1,0:T(2,128)S(1)}, f32[2,512]{1,0:T(2,128)S(1)}) custom-call(s32[1]{0:T(128)S(6)} %copy.13.valid_ref, s32[16,512]{1,0:T(8,128)S(1)} %get-tuple-element.71.table_ref, bf16[512,384]{1,0:T(8,128)(2,1)S(1)} %get-tuple-element.72.k_ref, ...), custom_call_target="tpu_custom_call" | custom-call | flops 503316480 | bytes 1048576 | tf_op jit(solution)/shard_map/pallas_call | solution.py:515
  11.2 0.0 copy-start
  11.3 0.0 collective-permute-done.2.after_ref.refs_9_
  11.3 2.7 %collective-permute-start.3 = (bf16[16,768]{1,0:T(8,128)(2,1)S(1)}, bf16[16,768]{1,0:T(8,128)(2,1)S(1)}, u32[]{:S(2)}, u32[]{:S(2)}) collective-permute-start(bf16[16,768]{1,0:T(8,128)(2,1)S(1)} %pad_maximum_fusion), channel_id=1, source_target_pairs={{0,8},{2,10},{4,12},{6,14},{8,0},{10,2},{12,4},{14,6},{1,9},{3,11}... | collective-permute-start | bytes 73736 | tf_op jit(solution)/shard_map/ppermute | solution.py:471
  13.9 1.9 %shard_map.105 = (bf16[4,512,512]{2,1,0:T(8,128)(2,1)S(1)}, f32[192,512]{1,0:T(8,128)S(1)}, f32[4,512]{1,0:T(4,128)S(1)}, f32[4,512]{1,0:T(4,128)S(1)}) custom-call(s32[1]{0:T(128)S(6)} %copy.13.valid_ref, s32[16,512]{1,0:T(8,128)S(1)} %get-tuple-element.71.table_ref, bf16[512,384]{1,0:T(8,128)(2,1)S(1)} %get-tuple-element.72.k_ref, ...), custom_call_target="tpu_custom_call" | custom-call | flops 1006632960 | bytes 2097152 | tf_op jit(solution)/shard_map/pallas_call | solution.py:515
  15.8 0.0 collective-permute-done.1.near_ref
  15.8 0.0 copy-done
  15.9 1.0 %shard_map.106 = (bf16[384,512]{1,0:T(8,128)(2,1)S(1)}, bf16[384,512]{1,0:T(8,128)(2,1)S(1)}, bf16[512,512]{1,0:T(8,128)(2,1)S(1)}, f32[384,512]{1,0:T(8,128)S(1...) custom-call(s32[1]{0:T(128)S(6)} %copy.13.valid_ref, ...), custom_call_target="tpu_custom_call" | custom-call | flops 251658240 | bytes 524288 | tf_op jit(solution)/shard_map/pallas_call | solution.py:541
  16.8 0.0 collective-permute-done.3
  16.8 1.1 %shard_map.107 = (bf16[384,512]{1,0:T(8,128)(2,1)S(1)}, f32[8,512]{1,0:T(8,128)S(1)}, f32[8,512]{1,0:T(8,128)S(1)}, f32[8,512]{1,0:T(8,128)S(1)}, bf16[256,512]{...) custom-call(s32[1]{0:T(128)S(6)} %copy.13.valid_ref, s32[16,512]{1,0:T(8,128)S(1)} %get-tuple-element.71.table_ref, ...), custom_call_target="tpu_custom_call" | custom-call | flops 314572800 | bytes 262144 | tf_op jit(solution)/shard_map/pallas_call | solution.py:557
  17.9 1.9 %collective-permute-start.5 = (f32[16,768]{1,0:T(8,128)S(1)}, f32[16,768]{1,0:T(8,128)S(1)}, u32[]{:S(2)}, u32[]{:S(2)}) collective-permute-start(f32[16,768]{1,0:T(8,128)S(1)} %get-tuple-element.108.after_ref.refs_8_), channel_id=1, source_target_pairs={{0,8},{2,10},{4,12},{6,14},{8,0},{10,2},{12,4},{14,6},{1,9},{3,11}... | collective-permute-start | bytes 147464 | tf_op jit(solution)/shard_map/ppermute | solution.py:471
  19.9 1.1 %shard_map.108 = (f32[384,512]{1,0:T(8,128)S(1)}, bf16[64,768]{1,0:T(8,128)(2,1)S(1)}) custom-call(bf16[64,768]{1,0:T(8,128)(2,1)S(1)} %collective-permute-done.1.near_ref, bf16[32,768]{1,0:T(8,128)(2,1)S(1)} %constant_dynamic-update-slice_fusion.far_ref, bf16[384,512]{1,0:T(8,128)(2,1)S(1)} %get-tuple-element.77.qt_ref.refs_1_, ...), custom_call_target="tpu_custom_call" | custom-call | flops 503316480 | bytes 524288 | tf_op jit(solution)/shard_map/pallas_call | solution.py:610
  21.0 1.0 %collective-permute-start.4 = (bf16[64,768]{1,0:T(8,128)(2,1)S(1)}, bf16[64,768]{1,0:T(8,128)(2,1)S(1)}, u32[]{:S(2)}, u32[]{:S(2)}) collective-permute-start(bf16[64,768]{1,0:T(8,128)(2,1)S(1)} %get-tuple-element.111), channel_id=1, source_target_pairs={{0,2},{2,0},{4,6},{6,4},{8,10},{10,8},{12,14},{14,12},{1,3},{3,1},... | collective-permute-start | bytes 294920 | tf_op jit(solution)/shard_map/ppermute | solution.py:471
  22.0 1.0 %shard_map.109 = (bf16[96,512]{1,0:T(8,128)(2,1)S(1)}, f32[96,512]{1,0:T(8,128)S(1)}, f32[96,512]{1,0:T(8,128)S(1)}) custom-call(bf16[2,512,512]{2,1,0:T(8,128)(2,1)S(1)} %get-tuple-element.113.refs_0_, bf16[384,512]{1,0:T(8,128)(2,1)S(1)} %get-tuple-element.77.qt_ref.refs_1_, bf16[384,512]{1,0:T(8,128)(2,1)S(1)} %get-tuple-element.96.gt_ref.refs_2_, ...), custom_call_target="tpu_custom_call" | custom-call | flops 1006632960 | bytes 1048576 | tf_op jit(solution)/shard_map/pallas_call | solution.py:584
  23.1 0.0 collective-permute-done.5.refs_8_
  23.1 1.8 %collective-permute-start.6 = (f32[8,768]{1,0:T(8,128)S(1)}, f32[8,768]{1,0:T(8,128)S(1)}, u32[]{:S(2)}, u32[]{:S(2)}) collective-permute-start(f32[8,768]{1,0:T(8,128)S(1)} %slice.16), channel_id=1, source_target_pairs={{0,4},{2,6},{4,0},{6,2},{8,12},{10,14},{12,8},{14,10},{1,5},{3,7},... | collective-permute-start | bytes 73736 | tf_op jit(solution)/shard_map/ppermute | solution.py:471
  24.9 1.9 %shard_map.110 = (bf16[512,384]{1,0:T(8,128)(2,1)S(1)}, bf16[192,512]{1,0:T(8,128)(2,1)S(1)}, f32[192,512]{1,0:T(8,128)S(1)}, f32[192,512]{1,0:T(8,128)S(1)}) custom-call(bf16[4,512,512]{2,1,0:T(8,128)(2,1)S(1)} %get-tuple-element.112.refs_0_, bf16[384,512]{1,0:T(8,128)(2,1)S(1)} %get-tuple-element.77.qt_ref.refs_1_, ...), custom_call_target="tpu_custom_call" | custom-call | flops 2013265920 | bytes 2097152 | tf_op jit(solution)/shard_map/pallas_call | solution.py:576
  26.8 0.2 collective-permute-done.6.refs_11_
  27.0 1.1 %collective-permute-start.7 = (f32[4,768]{1,0:T(4,128)S(1)}, f32[4,768]{1,0:T(4,128)S(1)}, u32[]{:S(2)}, u32[]{:S(2)}) collective-permute-start(f32[4,768]{1,0:T(4,128)S(1)} %slice.18), channel_id=1, source_target_pairs={{0,2},{2,0},{4,6},{6,4},{8,10},{10,8},{12,14},{14,12},{1,3},{3,1},... | collective-permute-start | bytes 36872 | tf_op jit(solution)/shard_map/ppermute | solution.py:471
  28.1 0.0 collective-permute-done.4.refs_9_
  28.1 2.2 %shard_map.111 = (bf16[512,384]{1,0:T(8,128)(2,1)}, bf16[512,384]{1,0:T(8,128)(2,1)}, f32[6,512,128]{2,1,0:T(8,128)S(1)}) custom-call(bf16[2,512,512]{2,1,0:T(8,128)(2,1)S(1)} %get-tuple-element.81.refs_0_, bf16[384,512]{1,0:T(8,128)(2,1)S(1)} %get-tuple-element.77.qt_ref.refs_1_, bf16[384,512]{1,0:T(8,128)(2,1)S(1)} %get-tuple-element.96.gt_ref.refs_2_, ...), custom_call_target="tpu_custom_call" | custom-call | flops 1006632960 | bytes 1048576 | tf_op jit(solution)/shard_map/pallas_call | solution.py:592
  30.4 0.4 %collective-permute-done.7 = f32[4,768]{1,0:T(4,128)S(1)} collective-permute-done((f32[4,768]{1,0:T(4,128)S(1)}, f32[4,768]{1,0:T(4,128)S(1)}, u32[]{:S(2)}, u32[]{:S(2)}) %collective-permute-start.7) | collective-permute-done | bytes 12320 | tf_op jit(solution)/shard_map/ppermute | solution.py:471
  30.8 1.0 %shard_map.112 = (bf16[512,384]{1,0:T(8,128)(2,1)}, bf16[512,384]{1,0:T(8,128)(2,1)}) custom-call(s32[8,384]{1,0:T(8,128)S(1)} %get-tuple-element.75.lanes_ref.refs_8_, f32[6,512,128]{2,1,0:T(8,128)S(1)} %get-tuple-element.130.sum_ref, f32[4,768]{1,0:T(4,128)S(1)} %slice_add_fusion.1.far_ref), custom_call_target="tpu_custom_call" | custom-call | bytes 2359296 | tf_op jit(solution)/shard_map/pallas_call | solution.py:626
  (10 shorter events, 0.1 us)
Async XLA Ops:
  1.9 5.1 %collective-permute-start = (bf16[4,768]{1,0:T(4,128)(2,1)S(1)}, bf16[4,768]{1,0:T(4,128)(2,1)S(1)}, u32[]{:S(2)}, u32[]{:S(2)}) collective-permute-start(bf16[4,768]{1,0:T(4,128)(2,1)S(1)} %get-tuple-element.76.after_ref), channel_id=1, source_target_pairs={{0,2},{2,0},{4,6},{6,4},{8,10},{10,8},{12,14},{14,12},{1,3},{3,1},... | collective-permute-start | bytes 18440 | tf_op jit(solution)/shard_map/ppermute | solution.py:471
  7.1 4.2 %collective-permute-start.2 = (bf16[8,768]{1,0:T(8,128)(2,1)S(1)}, bf16[8,768]{1,0:T(8,128)(2,1)S(1)}, u32[]{:S(2)}, u32[]{:S(2)}) collective-permute-start(bf16[8,768]{1,0:T(8,128)(2,1)S(1)} %pad_maximum_fusion.1), channel_id=1, source_target_pairs={{0,4},{2,6},{4,0},{6,2},{8,12},{10,14},{12,8},{14,10},{1,5},{3,7},... | collective-permute-start | bytes 36872 | tf_op jit(solution)/shard_map/ppermute | solution.py:471
  8.7 7.1 %collective-permute-start.1 = (bf16[64,768]{1,0:T(8,128)(2,1)S(1)}, bf16[64,768]{1,0:T(8,128)(2,1)S(1)}, u32[]{:S(2)}, u32[]{:S(2)}) collective-permute-start(bf16[64,768]{1,0:T(8,128)(2,1)S(1)} %get-tuple-element.83), channel_id=1, source_target_pairs={{0,2},{2,0},{4,6},{6,4},{8,10},{10,8},{12,14},{14,12},{1,3},{3,1},... | collective-permute-start | bytes 294920 | tf_op jit(solution)/shard_map/ppermute | solution.py:471
  11.2 4.6 %copy-start = (bf16[512,384]{1,0:T(8,128)(2,1)S(1)}, bf16[512,384]{1,0:T(8,128)(2,1)}, u32[]{:S(2)}) copy-start(bf16[512,384]{1,0:T(8,128)(2,1)} %g_ref.1) | copy-start | bytes 1179652
  11.3 5.5 %collective-permute-start.3 = (bf16[16,768]{1,0:T(8,128)(2,1)S(1)}, bf16[16,768]{1,0:T(8,128)(2,1)S(1)}, u32[]{:S(2)}, u32[]{:S(2)}) collective-permute-start(bf16[16,768]{1,0:T(8,128)(2,1)S(1)} %pad_maximum_fusion), channel_id=1, source_target_pairs={{0,8},{2,10},{4,12},{6,14},{8,0},{10,2},{12,4},{14,6},{1,9},{3,11}... | collective-permute-start | bytes 73736 | tf_op jit(solution)/shard_map/ppermute | solution.py:471
  17.9 5.1 %collective-permute-start.5 = (f32[16,768]{1,0:T(8,128)S(1)}, f32[16,768]{1,0:T(8,128)S(1)}, u32[]{:S(2)}, u32[]{:S(2)}) collective-permute-start(f32[16,768]{1,0:T(8,128)S(1)} %get-tuple-element.108.after_ref.refs_8_), channel_id=1, source_target_pairs={{0,8},{2,10},{4,12},{6,14},{8,0},{10,2},{12,4},{14,6},{1,9},{3,11}... | collective-permute-start | bytes 147464 | tf_op jit(solution)/shard_map/ppermute | solution.py:471
  21.0 7.2 %collective-permute-start.4 = (bf16[64,768]{1,0:T(8,128)(2,1)S(1)}, bf16[64,768]{1,0:T(8,128)(2,1)S(1)}, u32[]{:S(2)}, u32[]{:S(2)}) collective-permute-start(bf16[64,768]{1,0:T(8,128)(2,1)S(1)} %get-tuple-element.111), channel_id=1, source_target_pairs={{0,2},{2,0},{4,6},{6,4},{8,10},{10,8},{12,14},{14,12},{1,3},{3,1},... | collective-permute-start | bytes 294920 | tf_op jit(solution)/shard_map/ppermute | solution.py:471
  23.1 3.9 %collective-permute-start.6 = (f32[8,768]{1,0:T(8,128)S(1)}, f32[8,768]{1,0:T(8,128)S(1)}, u32[]{:S(2)}, u32[]{:S(2)}) collective-permute-start(f32[8,768]{1,0:T(8,128)S(1)} %slice.16), channel_id=1, source_target_pairs={{0,4},{2,6},{4,0},{6,2},{8,12},{10,14},{12,8},{14,10},{1,5},{3,7},... | collective-permute-start | bytes 73736 | tf_op jit(solution)/shard_map/ppermute | solution.py:471
  27.0 3.8 %collective-permute-start.7 = (f32[4,768]{1,0:T(4,128)S(1)}, f32[4,768]{1,0:T(4,128)S(1)}, u32[]{:S(2)}, u32[]{:S(2)}) collective-permute-start(f32[4,768]{1,0:T(4,128)S(1)} %slice.18), channel_id=1, source_target_pairs={{0,2},{2,0},{4,6},{6,4},{8,10},{10,8},{12,14},{14,12},{1,3},{3,1},... | collective-permute-start | bytes 36872 | tf_op jit(solution)/shard_map/ppermute | solution.py:471

commit v7 on v6

--- a/solution.py
+++ b/solution.py
@@ -329,17 +329,19 @@
     for stack in stacks(heads, count):
         first, last, low, high = stack
         grad_prob = nn(stacked(near_ref[:, width:], stack), gt_ref[low:high, :])
-        weights, dscores = [], []
+        probs = [
+            p_ref[h * count : (h + 1) * count, :].astype(F32) * factor_ref[h : h + 1, :]
+            for h in range(first, last)
+        ]
+        weight = jnp.concatenate([prob.astype(BF16) for prob in probs], axis=0)
+        unstack(sum_ref, width, stack, count, nt(weight, gt_ref[low:high, :]), 1.0, started)
+        dscores = []
         for at, h in enumerate(range(first, last)):
-            prob = p_ref[h * count : (h + 1) * count, :].astype(F32) * factor_ref[h : h + 1, :]
             here = grad_prob[at * count : (at + 1) * count]
-            weights.append(prob.astype(BF16))
-            dscores.append((prob * (here - delta_ref[h : h + 1, :])).astype(BF16))
+            dscores.append((probs[at] * (here - delta_ref[h : h + 1, :])).astype(BF16))
         dscore = jnp.concatenate(dscores, axis=0)
+        unstack(sum_ref, 0, stack, count, nt(dscore, qt_ref[low:high, :]), SCALE, started)
         add_dq(stack, nn(stacked(near_ref[:, :width], stack).T, dscore))
-        unstack(sum_ref, 0, stack, count, nt(dscore, qt_ref[low:high, :]), SCALE, started)
-        weight = jnp.concatenate(weights, axis=0)
-        unstack(sum_ref, width, stack, count, nt(weight, gt_ref[low:high, :]), 1.0, started)
     send_ref[...] = sum_ref[...].astype(send_ref.dtype)
     count = far_ref.shape[0]
     for stack in stacks(heads, count):
@@ -559,7 +561,7 @@
         [((width, rows), BF16)]
         + [((heads, rows), F32)] * 3
         + [((heads * far_rows, rows), BF16)]
-        + [((far_rows // 2, 2 * width), F32)] * 2,
+        + [((far_rows // 2, 2 * width), F32), ((far_rows // 2, 2 * width), BF16)],
         [SMEM] + [VMEM] * 8,
         [pltpu.VMEM((far_rows, 2 * width), F32)],
         **cost(heads, far_rows, 5),

time: 31.9 us -> 31.7 us (level)
  transfers between devices with their start and end apart: 8 -> 8, of which waited for: 2 -> 2; matrix products, arithmetic and copies ran while one was open for 0% -> 0% of each run, Pallas kernels for 37% -> 36%
where the time goes in v7:
time: 31.7 us; the launch traced here: 31.5 us
  Pallas kernels  14.7 us (46%)
  starting transfers between devices  14.6 us (46%)
  between operations  1.45 us (5%)
  waiting for transfers between devices  0.62 us (2%)
    ppermute x8, starting transfers between devices, swap(): lax.ppermute(value, axes, [(at, at ^ apart) for at in range(devices)])  14.6 us
    pallas_call x2, Pallas kernels, front(): call(functools.partial(forward_kernel, groups[index], heads), outs, [SMEM...  2.9 us
    pallas_call x1, Pallas kernels, back(): call(functools.partial(last_backward_kernel, groups, index), [((rows, wid...  2.25 us
    pallas_call x1, Pallas kernels, back(): call(functools.partial(turning_backward_kernel, groups[index]), [((rows,...  1.88 us
    pallas_call x1, Pallas kernels, front(): call(functools.partial(first_forward_kernel, groups[index], heads), [((ne...  1.47 us
    pallas_call x1, Pallas kernels, local(): call(functools.partial(select_kernel, heads), [((far_own, 2 * width), BF1...  1.28 us
    pallas_call x1, Pallas kernels, local(): call(functools.partial(wide_kernel, heads, far_own), [((width, rows), BF1...  1.1 us
    pallas_call x1, Pallas kernels, back(): call(functools.partial(backward_kernel, groups[index]), partial, [VMEM] *...  1.04 us
  transfers between devices with their start and end apart: 8, of which 2 were waited for; matrix products, arithmetic and copies ran while one was open for 0% of the time, Pallas kernels for 36%

profile of v7, /device:TPU:0, one launch (start us, length us, event | category | flops | bytes accessed | tf_op | source)
XLA Modules:
  0.0 31.5 jit_solution(6520059799120270937)
XLA Ops:
  0.6 1.3 %shard_map.102 = (bf16[4,768]{1,0:T(4,128)(2,1)S(1)}, bf16[512,384]{1,0:T(8,128)(2,1)S(1)}, bf16[512,384]{1,0:T(8,128)(2,1)S(1)}, bf16[512,384]{1,0:T(8,128)(2,1...) custom-call(s32[16]{0:T(128)} %center_any.1, s32[16]{0:T(128)} %wide_any.1, bf16[512,384]{1,0:T(8,128)(2,1)} %q_any.1, ...), custom_call_target="tpu_custom_call" | custom-call | bytes 3145728 | tf_op jit(solution)/shard_map/pallas_call | solution.py:475
  1.9 3.0 %collective-permute-start = (bf16[4,768]{1,0:T(4,128)(2,1)S(1)}, bf16[4,768]{1,0:T(4,128)(2,1)S(1)}, u32[]{:S(2)}, u32[]{:S(2)}) collective-permute-start(bf16[4,768]{1,0:T(4,128)(2,1)S(1)} %get-tuple-element.76.after_ref), channel_id=1, source_target_pairs={{0,2},{2,0},{4,6},{6,4},{8,10},{10,8},{12,14},{14,12},{1,3},{3,1},... | collective-permute-start | bytes 18440 | tf_op jit(solution)/shard_map/ppermute | solution.py:473
  5.6 1.5 %shard_map.103 = (bf16[64,768]{1,0:T(8,128)(2,1)S(1)}, bf16[384,512]{1,0:T(8,128)(2,1)S(1)}, bf16[384,512]{1,0:T(8,128)(2,1)S(1)}, bf16[2,512,512]{2,1,0:T(8,128...) custom-call(s32[1]{0:T(128)S(6)} %copy.13.valid_ref, ...), custom_call_target="tpu_custom_call" | custom-call | flops 503316480 | bytes 1048576 | tf_op jit(solution)/shard_map/pallas_call | solution.py:508
  7.0 0.0 collective-permute-done.after_ref
  7.1 1.6 %collective-permute-start.2 = (bf16[8,768]{1,0:T(8,128)(2,1)S(1)}, bf16[8,768]{1,0:T(8,128)(2,1)S(1)}, u32[]{:S(2)}, u32[]{:S(2)}) collective-permute-start(bf16[8,768]{1,0:T(8,128)(2,1)S(1)} %pad_maximum_fusion.1), channel_id=1, source_target_pairs={{0,4},{2,6},{4,0},{6,2},{8,12},{10,14},{12,8},{14,10},{1,5},{3,7},... | collective-permute-start | bytes 36872 | tf_op jit(solution)/shard_map/ppermute | solution.py:473
  8.7 1.5 %collective-permute-start.1 = (bf16[64,768]{1,0:T(8,128)(2,1)S(1)}, bf16[64,768]{1,0:T(8,128)(2,1)S(1)}, u32[]{:S(2)}, u32[]{:S(2)}) collective-permute-start(bf16[64,768]{1,0:T(8,128)(2,1)S(1)} %get-tuple-element.83), channel_id=1, source_target_pairs={{0,2},{2,0},{4,6},{6,4},{8,10},{10,8},{12,14},{14,12},{1,3},{3,1},... | collective-permute-start | bytes 294920 | tf_op jit(solution)/shard_map/ppermute | solution.py:473
  10.2 1.0 %shard_map.104 = (bf16[2,512,512]{2,1,0:T(8,128)(2,1)S(1)}, f32[96,512]{1,0:T(8,128)S(1)}, f32[2,512]{1,0:T(2,128)S(1)}, f32[2,512]{1,0:T(2,128)S(1)}) custom-call(s32[1]{0:T(128)S(6)} %copy.13.valid_ref, s32[16,512]{1,0:T(8,128)S(1)} %get-tuple-element.71.table_ref, bf16[512,384]{1,0:T(8,128)(2,1)S(1)} %get-tuple-element.72.k_ref, ...), custom_call_target="tpu_custom_call" | custom-call | flops 503316480 | bytes 1048576 | tf_op jit(solution)/shard_map/pallas_call | solution.py:517
  11.2 0.0 copy-start
  11.3 0.0 collective-permute-done.2.after_ref.refs_9_
  11.3 2.7 %collective-permute-start.3 = (bf16[16,768]{1,0:T(8,128)(2,1)S(1)}, bf16[16,768]{1,0:T(8,128)(2,1)S(1)}, u32[]{:S(2)}, u32[]{:S(2)}) collective-permute-start(bf16[16,768]{1,0:T(8,128)(2,1)S(1)} %pad_maximum_fusion), channel_id=1, source_target_pairs={{0,8},{2,10},{4,12},{6,14},{8,0},{10,2},{12,4},{14,6},{1,9},{3,11}... | collective-permute-start | bytes 73736 | tf_op jit(solution)/shard_map/ppermute | solution.py:473
  13.9 1.9 %shard_map.105 = (bf16[4,512,512]{2,1,0:T(8,128)(2,1)S(1)}, f32[192,512]{1,0:T(8,128)S(1)}, f32[4,512]{1,0:T(4,128)S(1)}, f32[4,512]{1,0:T(4,128)S(1)}) custom-call(s32[1]{0:T(128)S(6)} %copy.13.valid_ref, s32[16,512]{1,0:T(8,128)S(1)} %get-tuple-element.71.table_ref, bf16[512,384]{1,0:T(8,128)(2,1)S(1)} %get-tuple-element.72.k_ref, ...), custom_call_target="tpu_custom_call" | custom-call | flops 1006632960 | bytes 2097152 | tf_op jit(solution)/shard_map/pallas_call | solution.py:517
  15.8 0.0 collective-permute-done.1.near_ref
  15.8 0.0 copy-done
  15.9 1.0 %shard_map.106 = (bf16[384,512]{1,0:T(8,128)(2,1)S(1)}, bf16[384,512]{1,0:T(8,128)(2,1)S(1)}, bf16[512,512]{1,0:T(8,128)(2,1)S(1)}, f32[384,512]{1,0:T(8,128)S(1...) custom-call(s32[1]{0:T(128)S(6)} %copy.13.valid_ref, ...), custom_call_target="tpu_custom_call" | custom-call | flops 251658240 | bytes 524288 | tf_op jit(solution)/shard_map/pallas_call | solution.py:543
  16.8 0.0 collective-permute-done.3
  16.8 1.1 %shard_map.107 = (bf16[384,512]{1,0:T(8,128)(2,1)S(1)}, f32[8,512]{1,0:T(8,128)S(1)}, f32[8,512]{1,0:T(8,128)S(1)}, f32[8,512]{1,0:T(8,128)S(1)}, bf16[256,512]{...) custom-call(s32[1]{0:T(128)S(6)} %copy.13.valid_ref, ...), custom_call_target="tpu_custom_call" | custom-call | flops 314572800 | bytes 262144 | tf_op jit(solution)/shard_map/pallas_call | solution.py:559
  17.9 1.9 %collective-permute-start.5 = (bf16[16,768]{1,0:T(8,128)(2,1)S(1)}, bf16[16,768]{1,0:T(8,128)(2,1)S(1)}, u32[]{:S(2)}, u32[]{:S(2)}) collective-permute-start(bf16[16,768]{1,0:T(8,128)(2,1)S(1)} %get-tuple-element.108.after_ref.refs_8_), channel_id=1, source_target_pairs={{0,8},{2,10},{4,12},{6,14},{8,0},{10,2},{12,4},{14,6},{1,9},{3,11}... | collective-permute-start | bytes 73736 | tf_op jit(solution)/shard_map/ppermute | solution.py:473
  19.9 0.9 %shard_map.108 = (f32[384,512]{1,0:T(8,128)S(1)}, bf16[64,768]{1,0:T(8,128)(2,1)S(1)}) custom-call(bf16[64,768]{1,0:T(8,128)(2,1)S(1)} %collective-permute-done.1.near_ref, bf16[32,768]{1,0:T(8,128)(2,1)S(1)} %constant_dynamic-update-slice_fusion.far_ref, bf16[384,512]{1,0:T(8,128)(2,1)S(1)} %get-tuple-element.77.qt_ref.refs_1_, ...), custom_call_target="tpu_custom_call" | custom-call | flops 503316480 | bytes 524288 | tf_op jit(solution)/shard_map/pallas_call | solution.py:612
  20.8 1.0 %collective-permute-start.4 = (bf16[64,768]{1,0:T(8,128)(2,1)S(1)}, bf16[64,768]{1,0:T(8,128)(2,1)S(1)}, u32[]{:S(2)}, u32[]{:S(2)}) collective-permute-start(bf16[64,768]{1,0:T(8,128)(2,1)S(1)} %get-tuple-element.111), channel_id=1, source_target_pairs={{0,2},{2,0},{4,6},{6,4},{8,10},{10,8},{12,14},{14,12},{1,3},{3,1},... | collective-permute-start | bytes 294920 | tf_op jit(solution)/shard_map/ppermute | solution.py:473
  21.8 1.0 %shard_map.109 = (bf16[96,512]{1,0:T(8,128)(2,1)S(1)}, f32[96,512]{1,0:T(8,128)S(1)}, f32[96,512]{1,0:T(8,128)S(1)}) custom-call(bf16[2,512,512]{2,1,0:T(8,128)(2,1)S(1)} %get-tuple-element.113.refs_0_, bf16[384,512]{1,0:T(8,128)(2,1)S(1)} %get-tuple-element.77.qt_ref.refs_1_, bf16[384,512]{1,0:T(8,128)(2,1)S(1)} %get-tuple-element.96.gt_ref.refs_2_, ...), custom_call_target="tpu_custom_call" | custom-call | flops 1006632960 | bytes 1048576 | tf_op jit(solution)/shard_map/pallas_call | solution.py:586
  22.8 0.0 collective-permute-done.5.refs_8_
  22.9 1.8 %collective-permute-start.6 = (f32[8,768]{1,0:T(8,128)S(1)}, f32[8,768]{1,0:T(8,128)S(1)}, u32[]{:S(2)}, u32[]{:S(2)}) collective-permute-start(f32[8,768]{1,0:T(8,128)S(1)} %slice.16), channel_id=1, source_target_pairs={{0,4},{2,6},{4,0},{6,2},{8,12},{10,14},{12,8},{14,10},{1,5},{3,7},... | collective-permute-start | bytes 73736 | tf_op jit(solution)/shard_map/ppermute | solution.py:473
  24.7 1.9 %shard_map.110 = (bf16[512,384]{1,0:T(8,128)(2,1)S(1)}, bf16[192,512]{1,0:T(8,128)(2,1)S(1)}, f32[192,512]{1,0:T(8,128)S(1)}, f32[192,512]{1,0:T(8,128)S(1)}) custom-call(bf16[4,512,512]{2,1,0:T(8,128)(2,1)S(1)} %get-tuple-element.112.refs_0_, bf16[384,512]{1,0:T(8,128)(2,1)S(1)} %get-tuple-element.77.qt_ref.refs_1_, ...), custom_call_target="tpu_custom_call" | custom-call | flops 2013265920 | bytes 2097152 | tf_op jit(solution)/shard_map/pallas_call | solution.py:578
  26.6 0.2 collective-permute-done.6.refs_11_
  26.8 1.1 %collective-permute-start.7 = (f32[4,768]{1,0:T(4,128)S(1)}, f32[4,768]{1,0:T(4,128)S(1)}, u32[]{:S(2)}, u32[]{:S(2)}) collective-permute-start(f32[4,768]{1,0:T(4,128)S(1)} %slice.18), channel_id=1, source_target_pairs={{0,2},{2,0},{4,6},{6,4},{8,10},{10,8},{12,14},{14,12},{1,3},{3,1},... | collective-permute-start | bytes 36872 | tf_op jit(solution)/shard_map/ppermute | solution.py:473
  27.9 0.0 collective-permute-done.4.refs_9_
  27.9 2.3 %shard_map.111 = (bf16[512,384]{1,0:T(8,128)(2,1)}, bf16[512,384]{1,0:T(8,128)(2,1)}, f32[6,512,128]{2,1,0:T(8,128)S(1)}) custom-call(bf16[2,512,512]{2,1,0:T(8,128)(2,1)S(1)} %get-tuple-element.81.refs_0_, bf16[384,512]{1,0:T(8,128)(2,1)S(1)} %get-tuple-element.77.qt_ref.refs_1_, bf16[384,512]{1,0:T(8,128)(2,1)S(1)} %get-tuple-element.96.gt_ref.refs_2_, ...), custom_call_target="tpu_custom_call" | custom-call | flops 1006632960 | bytes 1048576 | tf_op jit(solution)/shard_map/pallas_call | solution.py:594
  30.2 0.4 %collective-permute-done.7 = f32[4,768]{1,0:T(4,128)S(1)} collective-permute-done((f32[4,768]{1,0:T(4,128)S(1)}, f32[4,768]{1,0:T(4,128)S(1)}, u32[]{:S(2)}, u32[]{:S(2)}) %collective-permute-start.7) | collective-permute-done | bytes 12320 | tf_op jit(solution)/shard_map/ppermute | solution.py:473
  30.6 1.0 %shard_map.112 = (bf16[512,384]{1,0:T(8,128)(2,1)}, bf16[512,384]{1,0:T(8,128)(2,1)}) custom-call(s32[8,384]{1,0:T(8,128)S(1)} %get-tuple-element.75.lanes_ref.refs_8_, f32[6,512,128]{2,1,0:T(8,128)S(1)} %get-tuple-element.130.sum_ref, f32[4,768]{1,0:T(4,128)S(1)} %slice_add_fusion.1.far_ref), custom_call_target="tpu_custom_call" | custom-call | bytes 2359296 | tf_op jit(solution)/shard_map/pallas_call | solution.py:628
  (10 shorter events, 0.1 us)
Async XLA Ops:
  1.9 5.1 %collective-permute-start = (bf16[4,768]{1,0:T(4,128)(2,1)S(1)}, bf16[4,768]{1,0:T(4,128)(2,1)S(1)}, u32[]{:S(2)}, u32[]{:S(2)}) collective-permute-start(bf16[4,768]{1,0:T(4,128)(2,1)S(1)} %get-tuple-element.76.after_ref), channel_id=1, source_target_pairs={{0,2},{2,0},{4,6},{6,4},{8,10},{10,8},{12,14},{14,12},{1,3},{3,1},... | collective-permute-start | bytes 18440 | tf_op jit(solution)/shard_map/ppermute | solution.py:473
  7.1 4.2 %collective-permute-start.2 = (bf16[8,768]{1,0:T(8,128)(2,1)S(1)}, bf16[8,768]{1,0:T(8,128)(2,1)S(1)}, u32[]{:S(2)}, u32[]{:S(2)}) collective-permute-start(bf16[8,768]{1,0:T(8,128)(2,1)S(1)} %pad_maximum_fusion.1), channel_id=1, source_target_pairs={{0,4},{2,6},{4,0},{6,2},{8,12},{10,14},{12,8},{14,10},{1,5},{3,7},... | collective-permute-start | bytes 36872 | tf_op jit(solution)/shard_map/ppermute | solution.py:473
  8.7 7.1 %collective-permute-start.1 = (bf16[64,768]{1,0:T(8,128)(2,1)S(1)}, bf16[64,768]{1,0:T(8,128)(2,1)S(1)}, u32[]{:S(2)}, u32[]{:S(2)}) collective-permute-start(bf16[64,768]{1,0:T(8,128)(2,1)S(1)} %get-tuple-element.83), channel_id=1, source_target_pairs={{0,2},{2,0},{4,6},{6,4},{8,10},{10,8},{12,14},{14,12},{1,3},{3,1},... | collective-permute-start | bytes 294920 | tf_op jit(solution)/shard_map/ppermute | solution.py:473
  11.2 4.6 %copy-start = (bf16[512,384]{1,0:T(8,128)(2,1)S(1)}, bf16[512,384]{1,0:T(8,128)(2,1)}, u32[]{:S(2)}) copy-start(bf16[512,384]{1,0:T(8,128)(2,1)} %g_ref.1) | copy-start | bytes 1179652
  11.3 5.5 %collective-permute-start.3 = (bf16[16,768]{1,0:T(8,128)(2,1)S(1)}, bf16[16,768]{1,0:T(8,128)(2,1)S(1)}, u32[]{:S(2)}, u32[]{:S(2)}) collective-permute-start(bf16[16,768]{1,0:T(8,128)(2,1)S(1)} %pad_maximum_fusion), channel_id=1, source_target_pairs={{0,8},{2,10},{4,12},{6,14},{8,0},{10,2},{12,4},{14,6},{1,9},{3,11}... | collective-permute-start | bytes 73736 | tf_op jit(solution)/shard_map/ppermute | solution.py:473
  17.9 4.9 %collective-permute-start.5 = (bf16[16,768]{1,0:T(8,128)(2,1)S(1)}, bf16[16,768]{1,0:T(8,128)(2,1)S(1)}, u32[]{:S(2)}, u32[]{:S(2)}) collective-permute-start(bf16[16,768]{1,0:T(8,128)(2,1)S(1)} %get-tuple-element.108.after_ref.refs_8_), channel_id=1, source_target_pairs={{0,8},{2,10},{4,12},{6,14},{8,0},{10,2},{12,4},{14,6},{1,9},{3,11}... | collective-permute-start | bytes 73736 | tf_op jit(solution)/shard_map/ppermute | solution.py:473
  20.8 7.2 %collective-permute-start.4 = (bf16[64,768]{1,0:T(8,128)(2,1)S(1)}, bf16[64,768]{1,0:T(8,128)(2,1)S(1)}, u32[]{:S(2)}, u32[]{:S(2)}) collective-permute-start(bf16[64,768]{1,0:T(8,128)(2,1)S(1)} %get-tuple-element.111), channel_id=1, source_target_pairs={{0,2},{2,0},{4,6},{6,4},{8,10},{10,8},{12,14},{14,12},{1,3},{3,1},... | collective-permute-start | bytes 294920 | tf_op jit(solution)/shard_map/ppermute | solution.py:473
  22.9 3.9 %collective-permute-start.6 = (f32[8,768]{1,0:T(8,128)S(1)}, f32[8,768]{1,0:T(8,128)S(1)}, u32[]{:S(2)}, u32[]{:S(2)}) collective-permute-start(f32[8,768]{1,0:T(8,128)S(1)} %slice.16), channel_id=1, source_target_pairs={{0,4},{2,6},{4,0},{6,2},{8,12},{10,14},{12,8},{14,10},{1,5},{3,7},... | collective-permute-start | bytes 73736 | tf_op jit(solution)/shard_map/ppermute | solution.py:473
  26.8 3.8 %collective-permute-start.7 = (f32[4,768]{1,0:T(4,128)S(1)}, f32[4,768]{1,0:T(4,128)S(1)}, u32[]{:S(2)}, u32[]{:S(2)}) collective-permute-start(f32[4,768]{1,0:T(4,128)S(1)} %slice.18), channel_id=1, source_target_pairs={{0,2},{2,0},{4,6},{6,4},{8,10},{10,8},{12,14},{14,12},{1,3},{3,1},... | collective-permute-start | bytes 36872 | tf_op jit(solution)/shard_map/ppermute | solution.py:473
